TPU v7x, 32 devices: a whole 2x2x4 slice. The times are simulated.
32 devices in a mesh: grp: 2 (over core), seq: 16 (over z, y, x).
Axes of the slice: x: 2, y: 2, z: 4, core: 2. Of those that a mesh axis runs over, the one named last changes fastest.
Arguments:
- tokens: bfloat16 [4096, 1152], P(('grp', 'seq')), may hold values from -6 to 6
- routes: int32 [4096], P(('grp', 'seq')), may hold values from 0 to 1
- lengths: int32 [2, 2], P('grp'), may hold values from 512 to 1536, as said below
- grad_out: float32 [4096, 1152], P(('grp', 'seq')), may hold values from -6 to 6
- norm_gains: float32 [2, 1152], replicated, may hold values from 0.1 to 1.9
- router: bfloat16 [1152, 2], replicated, may hold values from -0.1875 to 0.1875
- in_weight: bfloat16 [2, 2304, 1152], P(None, ('grp', 'seq')), may hold values from -0.1875 to 0.1875
- conv_weight: bfloat16 [2304, 4], P(('grp', 'seq')), may hold values from -3 to 3
- x_weight: bfloat16 [2304, 104], P(('grp', 'seq')), may hold values from -0.125 to 0.125
- dt_weight: bfloat16 [2304, 72], P(('grp', 'seq')), may hold values from -0.75 to 0.75
- dt_bias: bfloat16 [2304], P(('grp', 'seq')), may hold values from -6 to -4
- a_log: bfloat16 [2304, 16], P(('grp', 'seq')), may hold values from -6 to 2
- skip_gain: bfloat16 [2304], P(('grp', 'seq')), may hold values from 0.5 to 1.5
- out_weight: bfloat16 [2304, 1152], P(('grp', 'seq')), may hold values from -0.375 to 0.375
- expert_in: bfloat16 [2, 3072, 1152], P(None, ('grp', 'seq')), may hold values from -0.1875 to 0.1875
- expert_out: bfloat16 [2, 3072, 1152], P(None, ('grp', 'seq')), may hold values from -0.21875 to 0.21875
Outputs:
- mixed_out: bfloat16 [4096, 1152], P(('grp', 'seq'))
- grad_tokens: float32 [4096, 1152], P(('grp', 'seq'))
- grad_gains: float32 [2, 1152], replicated
- grad_router: float32 [1152, 2], replicated
- grad_in_weight: float32 [2, 2304, 1152], P(None, ('grp', 'seq'))
- grad_conv_weight: float32 [2304, 4], P(('grp', 'seq'))
- grad_x_weight: float32 [2304, 104], P(('grp', 'seq'))
- grad_dt_weight: float32 [2304, 72], P(('grp', 'seq'))
- grad_dt_bias: float32 [2304], P(('grp', 'seq'))
- grad_a_log: float32 [2304, 16], P(('grp', 'seq'))
- grad_skip: float32 [2304], P(('grp', 'seq'))
- grad_out_weight: float32 [2304, 1152], P(('grp', 'seq'))
- grad_expert_in: float32 [2, 3072, 1152], P(None, ('grp', 'seq'))
- grad_expert_out: float32 [2, 3072, 1152], P(None, ('grp', 'seq'))
Inputs may be any that keep to these rules, and one draw needn't show every extreme that they name: lengths[g, 0] + lengths[g, 1] = 2048 for every group.
All inputs are finite; a program needn't handle non-finite values.
Results may differ from a plain program's by a relative error of at most 0.012.
The roundings to bfloat16 on the way count: a program that leaves them out, or rounds other values in their place, can miss the bound.
Values may be sent and summed in bfloat16 or wider, within the bound.
A program may use at most 448 MiB of HBM per device.

v0:
```python
import jax
import jax.numpy as jnp
from jax import lax
from jax.sharding import PartitionSpec as P

eps_norm = 1e-05
unroll_rows = 16
highest = lax.Precision.HIGHEST


def from_behind(value, axis, steps):
    count = lax.axis_size(axis)
    initial, last = (max(0, -steps), min(count, count - steps))
    return lax.ppermute(value, axis, [(source, source + steps) for source in range(initial, last)])


def entering(part, axis, combine, identity, reverse):
    count = lax.axis_size(axis)
    place = lax.axis_index(axis)
    ahead = count - 1 - place if reverse else place
    gathered = jax.tree.map(lambda a: lax.all_gather(a, axis), part)
    state = jax.tree.map(lambda a, e: jnp.zeros_like(a) + jnp.asarray(e, a.dtype), part, identity)

    def one(turn, state):
        source = count - 1 - turn if reverse else turn
        return combine(
            state, jax.tree.map(lambda a: lax.dynamic_index_in_dim(a, source, 0, False), gathered)
        )

    return lax.fori_loop(0, ahead, one, state)


def norm_rows(values, gain_row):
    return values * lax.rsqrt(jnp.mean(values * values, -1, keepdims=True) + eps_norm) * gain_row


def combine_pairs(earlier, later_pair):
    return (earlier[0] * later_pair[0], later_pair[0] * earlier[1] + later_pair[1])


def matmul(first_op, second_op):
    return jnp.dot(first_op, second_op, preferred_element_type=jnp.float32)


def matmul_nt(first_op, second_op):
    return lax.dot_general(
        first_op, second_op, (((1,), (1,)), ((), ())), preferred_element_type=jnp.float32
    )


def matmul_tn(first_op, second_op):
    return lax.dot_general(
        first_op, second_op, (((0,), (0,)), ((), ())), preferred_element_type=jnp.float32
    )


def shards(
    tokens,
    routes,
    lengths,
    grad_out,
    norm_gains,
    router,
    in_weight,
    conv_weight,
    x_weight,
    dt_weight,
    dt_bias,
    a_log,
    skip_gain,
    out_weight,
    expert_in,
    expert_out,
):
    in_full, conv_full, x_full, dt_full, bias_full, alog_full, skip_full, out_full = (
        lax.all_gather(in_weight, ("grp", "seq"), axis=1, tiled=True),
        lax.all_gather(conv_weight, ("grp", "seq"), axis=0, tiled=True),
        lax.all_gather(x_weight, ("grp", "seq"), axis=0, tiled=True),
        lax.all_gather(dt_weight, ("grp", "seq"), axis=0, tiled=True),
        lax.all_gather(dt_bias, ("grp", "seq"), axis=0, tiled=True),
        lax.all_gather(a_log, ("grp", "seq"), axis=0, tiled=True),
        lax.all_gather(skip_gain, ("grp", "seq"), axis=0, tiled=True),
        lax.all_gather(out_weight, ("grp", "seq"), axis=0, tiled=True),
    )
    experts_in, experts_out = (
        lax.all_gather(expert_in, ("grp", "seq"), axis=1, tiled=True),
        lax.all_gather(expert_out, ("grp", "seq"), axis=1, tiled=True),
    )
    inner_width = conv_full.shape[0]
    tap_count = conv_full.shape[1]
    dt_rank = dt_full.shape[1]
    states = alog_full.shape[1]
    expert_count = experts_in.shape[0]
    hidden_width = experts_in.shape[1]
    model_width = tokens.shape[1]
    row_count = tokens.shape[0]
    blocks = row_count // unroll_rows
    place = lax.axis_index("seq") * row_count + jnp.arange(row_count, dtype=jnp.int32)
    first_len = lengths[0, 0]
    offset = jnp.where(place < first_len, place, place - first_len)
    keep_rows = (offset != 0).astype(jnp.float32)

    def shape_blocks(values):
        return values.reshape((blocks, unroll_rows) + values.shape[1:])

    inputs = tokens.astype(jnp.float32)
    normed = norm_rows(inputs, norm_gains[0]).astype(jnp.bfloat16)
    conv_input = matmul_nt(normed, in_full[0]).astype(jnp.bfloat16)
    z_gate = matmul_nt(normed, in_full[1])
    before = from_behind(conv_input[row_count - (tap_count - 1) :], "seq", 1)
    window = jnp.concatenate([before, conv_input], 0).astype(jnp.float32)
    conv_taps = conv_full.astype(jnp.float32)
    valid_rows = [
        (offset >= tap_count - 1 - k).astype(jnp.float32)[:, None] for k in range(tap_count)
    ]
    conv_sum = sum(
        (conv_taps[:, k] * window[k : k + row_count] * valid_rows[k] for k in range(tap_count))
    )
    mixed_in = jax.nn.silu(conv_sum).astype(jnp.bfloat16)
    mixed_val = mixed_in.astype(jnp.float32)
    coef_rows = matmul(mixed_in, x_full)
    dt_low = coef_rows[:, :dt_rank].astype(jnp.bfloat16)
    in_coef = coef_rows[:, dt_rank : dt_rank + states]
    out_coef = coef_rows[:, dt_rank + states :]
    dt_pre = matmul_nt(dt_low, dt_full)
    bias_vals = bias_full.astype(jnp.float32)
    step_size = jax.nn.softplus(dt_pre + bias_vals)
    decay_rate = -jnp.exp(alog_full.astype(jnp.float32)).T
    skip_vals = skip_full.astype(jnp.float32)

    def forward_block(carry_in, pieces):
        state_now, total_step, alive_flag = carry_in
        delta_b, in_b, out_b, mixed_b, keep_b = pieces
        start_state = state_now
        y_rows, total_rows, alive_rows = ([], [], [])
        for t in range(unroll_rows):
            factor = jnp.exp(delta_b[t][None, :] * decay_rate) * keep_b[t]
            state_now = factor * state_now + in_b[t][:, None] * (delta_b[t] * mixed_b[t])[None, :]
            total_step = total_step + delta_b[t]
            alive_flag = alive_flag * keep_b[t]
            y_rows.append(jnp.sum(out_b[t][:, None] * state_now, 0))
            total_rows.append(total_step)
            alive_rows.append(alive_flag)
        return (
            (state_now, total_step, alive_flag),
            (jnp.stack(y_rows), jnp.stack(total_rows), jnp.stack(alive_rows), start_state),
        )

    start_carry = (
        jnp.zeros((states, inner_width), jnp.float32),
        jnp.zeros((inner_width,), jnp.float32),
        jnp.ones((), jnp.float32),
    )
    ends, stacked = lax.scan(
        forward_block,
        start_carry,
        tuple((shape_blocks(a) for a in (step_size, in_coef, out_coef, mixed_val, keep_rows))),
    )
    end_state, end_total, end_alive = ends
    y_local, total_blocks, alive_blocks, local_starts = stacked
    end_decay = jnp.exp(end_total[None, :] * decay_rate) * end_alive
    carried = entering(
        (end_decay, end_state),
        "seq",
        combine_pairs,
        (jnp.ones_like(end_decay), jnp.zeros_like(end_state)),
        False,
    )[1]

    def correct_block(pieces):
        total_b, alive_b, out_b = pieces
        growth = jnp.exp(total_b[:, None, :] * decay_rate[None]) * alive_b[:, None, None]
        return jnp.einsum("tnc,tn->tc", growth * carried[None], out_b, precision=highest)

    y_add = lax.map(correct_block, (total_blocks, alive_blocks, shape_blocks(out_coef))).reshape(
        row_count, inner_width
    )
    y_value = y_local.reshape(row_count, inner_width) + y_add + skip_vals * mixed_val
    prev_total = jnp.concatenate(
        [jnp.zeros((1, inner_width), jnp.float32), total_blocks[:-1, -1]], 0
    )
    prev_alive = jnp.concatenate([jnp.ones((1,), jnp.float32), alive_blocks[:-1, -1]], 0)
    true_starts = (
        local_starts
        + jnp.exp(prev_total[:, None, :] * decay_rate[None])
        * prev_alive[:, None, None]
        * carried[None]
    )
    gate_z = jax.nn.silu(z_gate)
    gated = (y_value * gate_z).astype(jnp.bfloat16)
    branch = matmul(gated, out_full)
    resid = inputs + branch
    second = norm_rows(resid, norm_gains[1]).astype(jnp.bfloat16)
    logits = matmul(second, router)
    soft_probs = jax.nn.softmax(logits, -1)
    chosen = (routes[:, None] == jnp.arange(expert_count, dtype=jnp.int32)[None, :]).astype(
        jnp.float32
    )
    gate_prob = jnp.sum(soft_probs * chosen, -1)
    combined = resid
    pre_acts, activated, expert_ys = ([], [], [])
    for e in range(expert_count):
        pre_act = matmul_nt(second, experts_in[e])
        act_low = jax.nn.gelu(pre_act, approximate=False).astype(jnp.bfloat16)
        expert_y = matmul(act_low, experts_out[e])
        pre_acts.append(pre_act)
        activated.append(act_low)
        expert_ys.append(expert_y)
        combined = combined + chosen[:, e : e + 1] * gate_prob[:, None] * expert_y
    mixed_out = combined.astype(jnp.bfloat16)
    d_gate = jnp.zeros((row_count,), jnp.float32)
    d_second = jnp.zeros(second.shape, jnp.float32)
    routed_list, d_pre_list = ([], [])
    for e in range(expert_count):
        routed_grad = (chosen[:, e : e + 1] * gate_prob[:, None] * grad_out).astype(jnp.bfloat16)
        d_act = matmul_nt(routed_grad, experts_out[e])
        _, gelu_pull = jax.vjp(lambda v: jax.nn.gelu(v, approximate=False), pre_acts[e])
        d_pre = gelu_pull(d_act)[0].astype(jnp.bfloat16)
        routed_list.append(routed_grad)
        d_pre_list.append(d_pre)
        d_second = d_second + matmul(d_pre, experts_in[e])
        d_gate = d_gate + chosen[:, e] * jnp.sum(expert_ys[e] * grad_out, -1)
    _, soft_pull = jax.vjp(lambda v: jax.nn.softmax(v, -1), logits)
    d_logits = soft_pull(chosen * d_gate[:, None])[0].astype(jnp.bfloat16)
    grad_router = matmul_tn(second, d_logits)
    d_second = d_second + matmul_nt(d_logits, router)
    _, norm_pull_two = jax.vjp(norm_rows, resid, norm_gains[1])
    d_resid_norm, d_gain_two = norm_pull_two(d_second)
    d_resid = grad_out + d_resid_norm
    g_branch = d_resid.astype(jnp.bfloat16)
    d_gated = matmul_nt(g_branch, out_full)
    d_y = d_gated * gate_z
    _, silu_pull = jax.vjp(jax.nn.silu, z_gate)
    d_z = silu_pull(d_gated * y_value)[0]
    grad_skip = jnp.sum(d_y * mixed_val, 0)

    def end_block(pieces):
        total_b, alive_b, out_b, dy_b = pieces
        growth = jnp.exp(total_b[:, None, :] * decay_rate[None]) * alive_b[:, None, None]
        return jnp.einsum("tnc,tn,tc->nc", growth, out_b, dy_b, precision=highest)

    end_back = jnp.sum(
        lax.map(end_block, (total_blocks, alive_blocks, shape_blocks(out_coef), shape_blocks(d_y))),
        0,
    )
    incoming = entering(
        (end_decay, end_back),
        "seq",
        combine_pairs,
        (jnp.ones_like(end_decay), jnp.zeros_like(end_back)),
        True,
    )[1]

    def backward_block(carry_in, pieces):
        later_grad, rate_sum = carry_in
        delta_b, in_b, out_b, mixed_b, keep_b, dy_b, start_state = pieces
        state_now = start_state
        state_list = [start_state]
        factors = []
        for t in range(unroll_rows):
            factor = jnp.exp(delta_b[t][None, :] * decay_rate) * keep_b[t]
            state_now = factor * state_now + in_b[t][:, None] * (delta_b[t] * mixed_b[t])[None, :]
            factors.append(factor)
            state_list.append(state_now)
        delta_rows, mixed_rows, in_rows, out_rows = ([], [], [], [])
        for t in reversed(range(unroll_rows)):
            d_state = out_b[t][:, None] * dy_b[t][None, :] + later_grad
            scaled = d_state * state_list[t] * factors[t]
            rate_sum = rate_sum + scaled * delta_b[t][None, :]
            in_sum = jnp.sum(d_state * in_b[t][:, None], 0)
            delta_rows.append(jnp.sum(scaled * decay_rate, 0) + in_sum * mixed_b[t])
            mixed_rows.append(in_sum * delta_b[t])
            in_rows.append(jnp.sum(d_state * (delta_b[t] * mixed_b[t])[None, :], 1))
            out_rows.append(jnp.sum(state_list[t + 1] * dy_b[t][None, :], 1))
            later_grad = factors[t] * d_state
        return (
            (later_grad, rate_sum),
            tuple((jnp.stack(r[::-1]) for r in (delta_rows, mixed_rows, in_rows, out_rows))),
        )

    back_pieces = tuple(
        (shape_blocks(a) for a in (step_size, in_coef, out_coef, mixed_val, keep_rows, d_y))
    ) + (true_starts,)
    back_carry, back_rows = lax.scan(
        backward_block,
        (incoming, jnp.zeros((states, inner_width), jnp.float32)),
        back_pieces,
        reverse=True,
    )
    rate_sum = back_carry[1]
    d_step = back_rows[0].reshape(row_count, inner_width)
    d_mixed = skip_vals * d_y + back_rows[1].reshape(row_count, inner_width)
    d_in_coef = back_rows[2].reshape(row_count, states)
    d_out_coef = back_rows[3].reshape(row_count, states)
    grad_alog = (rate_sum * decay_rate).T
    _, softplus_pull = jax.vjp(jax.nn.softplus, dt_pre + bias_vals)
    d_dt = softplus_pull(d_step)[0]
    grad_bias = jnp.sum(d_dt, 0)
    g_dt = d_dt.astype(jnp.bfloat16)
    grad_dt_w = matmul_tn(g_dt, dt_low)
    d_dt_low = matmul(g_dt, dt_full)
    g_coef = jnp.concatenate([d_dt_low, d_in_coef, d_out_coef], 1).astype(jnp.bfloat16)
    grad_x_w = matmul_tn(mixed_in, g_coef)
    d_mixed = d_mixed + matmul_nt(g_coef, x_full)
    _, conv_pull = jax.vjp(jax.nn.silu, conv_sum)
    d_conv = conv_pull(d_mixed)[0]
    grad_conv = jnp.stack(
        [jnp.sum(d_conv * valid_rows[k] * window[k : k + row_count], 0) for k in range(tap_count)],
        1,
    )
    d_window = sum(
        (
            jnp.pad(conv_taps[:, k] * d_conv * valid_rows[k], ((k, tap_count - 1 - k), (0, 0)))
            for k in range(tap_count)
        )
    )
    from_next = from_behind(d_window[: tap_count - 1], "seq", -1)
    d_input = d_window[tap_count - 1 :] + jnp.pad(
        from_next, ((row_count - (tap_count - 1), 0), (0, 0))
    )
    g_in = d_input.astype(jnp.bfloat16)
    g_z = d_z.astype(jnp.bfloat16)
    d_normed = matmul(g_in, in_full[0]) + matmul(g_z, in_full[1])
    _, norm_pull_one = jax.vjp(norm_rows, inputs, norm_gains[0])
    d_inputs, d_gain_one = norm_pull_one(d_normed)
    grad_tokens = d_resid + d_inputs
    grad_gains, grad_router_sum = lax.psum(
        (jnp.stack([d_gain_one, d_gain_two]), grad_router), ("grp", "seq")
    )
    mixer_rest = jnp.concatenate(
        [grad_conv, grad_x_w, grad_dt_w, grad_bias[:, None], grad_alog, grad_skip[:, None]], 1
    )
    all_count = lax.axis_size(("grp", "seq"))
    part_gated = lax.slice_in_dim(
        gated, 0, inner_width // all_count * lax.axis_size(("grp", "seq")), axis=1
    )
    part_rest = lax.slice_in_dim(
        mixer_rest, 0, inner_width // all_count * lax.axis_size(("grp", "seq")), axis=0
    )
    mixer_local = lax.psum_scatter(
        jnp.concatenate(
            [
                matmul_tn(g_in, normed),
                matmul_tn(g_z, normed),
                matmul_tn(part_gated, g_branch),
                part_rest,
            ],
            1,
        ),
        ("grp", "seq"),
        scatter_dimension=0,
        tiled=True,
    )
    firsts = [
        matmul_tn(
            lax.slice_in_dim(
                d_pre_list[e], 0, hidden_width // all_count * lax.axis_size(("grp", "seq")), axis=1
            ),
            second,
        )
        for e in range(expert_count)
    ]
    seconds = [
        matmul_tn(
            lax.slice_in_dim(
                activated[e], 0, hidden_width // all_count * lax.axis_size(("grp", "seq")), axis=1
            ),
            routed_list[e],
        )
        for e in range(expert_count)
    ]
    expert_local = lax.psum_scatter(
        jnp.concatenate(firsts + seconds, 1), ("grp", "seq"), scatter_dimension=0, tiled=True
    )
    grad_in_w = jnp.stack(
        [mixer_local[:, :model_width], mixer_local[:, model_width : 2 * model_width]]
    )
    grad_out_w = mixer_local[:, 2 * model_width : 3 * model_width]
    column = 3 * model_width
    grad_conv_l = mixer_local[:, column : column + tap_count]
    column = column + tap_count
    grad_x_l = mixer_local[:, column : column + dt_rank + 2 * states]
    column = column + dt_rank + 2 * states
    grad_dt_l = mixer_local[:, column : column + dt_rank]
    column = column + dt_rank
    grad_bias_l = mixer_local[:, column]
    column = column + 1
    grad_alog_l = mixer_local[:, column : column + states]
    column = column + states
    grad_skip_l = mixer_local[:, column]
    expert_rows = expert_local.shape[0]
    expert_parts = expert_local.reshape(expert_rows, 2, expert_count, model_width).transpose(
        1, 2, 0, 3
    )
    return (
        mixed_out,
        grad_tokens,
        grad_gains,
        grad_router_sum,
        grad_in_w,
        grad_conv_l,
        grad_x_l,
        grad_dt_l,
        grad_bias_l,
        grad_alog_l,
        grad_skip_l,
        grad_out_w,
        expert_parts[0],
        expert_parts[1],
    )


def solution(mesh):
    in_specs = (
        P(("grp", "seq"), None),
        P(("grp", "seq")),
        P("grp", None),
        P(("grp", "seq"), None),
        P(),
        P(),
        P(None, ("grp", "seq"), None),
        P(("grp", "seq"), None),
        P(("grp", "seq"), None),
        P(("grp", "seq"), None),
        P(("grp", "seq")),
        P(("grp", "seq"), None),
        P(("grp", "seq")),
        P(("grp", "seq"), None),
        P(None, ("grp", "seq"), None),
        P(None, ("grp", "seq"), None),
    )
    out_specs = (
        P(("grp", "seq"), None),
        P(("grp", "seq"), None),
        P(),
        P(),
        P(None, ("grp", "seq"), None),
        P(("grp", "seq"), None),
        P(("grp", "seq"), None),
        P(("grp", "seq"), None),
        P(("grp", "seq")),
        P(("grp", "seq"), None),
        P(("grp", "seq")),
        P(("grp", "seq"), None),
        P(None, ("grp", "seq"), None),
        P(None, ("grp", "seq"), None),
    )
    return jax.shard_map(shards, mesh=mesh, in_specs=in_specs, out_specs=out_specs, check_vma=False)
```

profile of v0, /device:TPU:0, one launch (start us, length us, event | category | flops | bytes accessed | tf_op | source)
XLA Modules:
  0.0 3087.1 jit_solution(985513732007581799)
XLA Ops:
  8.0 70.8 %all-gather.3 = bf16[32,72,4]{1,2,0:T(4,128)(2,1)S(1)} all-gather(bf16[1,72,4]{1,2,0:T(4,128)(2,1)} %bitcast.799), channel_id=1, replica_groups=mesh['grp'=2,'seq'=16] {'grp','seq'}, dimensions={0}, use_global_device_ids=true | all-gather | bytes 19008 | tf_op jit(solution)/shard_map/all_gather | solution.py:77
  78.9 64.6 %all-gather.4 = bf16[32,72,16]{1,2,0:T(8,128)(2,1)S(1)} all-gather(bf16[1,72,16]{1,2,0:T(8,128)(2,1)} %bitcast.796), channel_id=1, replica_groups=mesh['grp'=2,'seq'=16] {'grp','seq'}, dimensions={0}, use_global_device_ids=true | all-gather | bytes 76032 | tf_op jit(solution)/shard_map/all_gather | solution.py:81
  147.4 73.8 %all_gather.53 = bf16[2304,72]{1,0:T(8,128)(2,1)} all-gather(bf16[72,72]{1,0:T(8,128)(2,1)} %param.37), channel_id=1, replica_groups=mesh['grp'=2,'seq'=16] {'grp','seq'}, dimensions={0}, use_global_device_ids=true | all-gather | bytes 342144 | tf_op jit(solution)/shard_map/all_gather | solution.py:79
  221.8 66.7 %all_gather.52 = bf16[2304,104]{1,0:T(8,128)(2,1)S(1)} all-gather(bf16[72,104]{1,0:T(8,128)(2,1)S(1)} %copy-done.63), channel_id=1, replica_groups=mesh['grp'=2,'seq'=16] {'grp','seq'}, dimensions={0}, use_global_device_ids=true | all-gather | bytes 494208 | tf_op jit(solution)/shard_map/all_gather | solution.py:78
  298.0 37.1 %all-reduce.10 = (bf16[2304]{0:T(1024)(128)(2,1)}, bf16[2304]{0:T(1024)(128)(2,1)S(1)}) all-reduce(bf16[2304]{0:T(1024)(128)(2,1)S(1)} %dynamic-update-slice.1, bf16[2304]{0:T(1024)(128)(2,1)S(1)} %dynamic-update-slice), channel_id=1, replica_groups=mesh['grp'=2,'seq'=16] {'grp','seq'}, use_global_device_ids=true, to_apply=%add.7 | all-reduce | flops 4608 | bytes 18432
  348.5 467.1 %while.98 = (s32[]{:T(128)}, f32[16,2304]{1,0:T(8,128)S(1)}, f32[2304]{0:T(1024)}, f32[]{:T(128)}, f32[8,16,2304]{2,1,0:T(8,128)}, /*index=5*/f32[8,16,2304]{2,1...) while((s32[]{:T(128)}, f32[16,2304]{1,0:T(8,128)S(1)}, ...), condition=%wide.region_18.19_spmd.clone, body=%wide.region_1.18_spmd.clone.sunk | while | flops 5753122 | bytes 7605298 | solution.py:154
  819.7 59.8 %all-gather.23.cloned.1.call-done = f32[256,2304]{1,0:T(8,128)} async-done(((f32[16,2304]{1,0:T(8,128)}), f32[256,2304]{1,0:T(8,128)}) %all-gather.23.cloned.1.call-update) | async-done | bytes 2359312 | tf_op jit(solution)/shard_map/all_gather | solution.py:21
  879.5 64.5 %all-gather.21.cloned.1.call-done = f32[256,2304]{1,0:T(8,128)} async-done(((f32[16,2304]{1,0:T(8,128)}), f32[256,2304]{1,0:T(8,128)}) %all-gather.21.cloned.1.call-update) | async-done | bytes 2359312 | tf_op jit(solution)/shard_map/all_gather | solution.py:21
  944.1 33.8 %while.95 = (s32[]{:T(128)}, f32[8,16,2304]{2,1,0:T(8,128)S(1)}, f32[8,16,2304]{2,1,0:T(8,128)}, f32[16,2304]{1,0:T(8,128)S(1)}, f32[8,16]{1,0:T(8,128)}, /*inde...) while((s32[]{:T(128)}, f32[8,16,2304]{2,1,0:T(8,128)S(1)}, f32[8,16,2304]{2,1,0:T(8,128)}, ...), condition=%wide.region_22.23_spmd, body=%wide.region_21.22_spmd.sunk | while | flops 8847362 | bytes 1183021 | solution.py:175
  987.1 24.1 all-gather.15.cloned.1.call-done
  1015.3 100.7 %all-gather.17.cloned.1.call-done = bf16[2,3072,1152]{2,1,0:T(8,128)(2,1)} async-done(((bf16[2,96,1152]{2,1,0:T(8,128)(2,1)}), bf16[2,3072,1152]{2,1,0:T(8,128)(2,1)}) %all-gather.17.cloned.1.call-update) | async-done | bytes 14155792 | tf_op jit(solution)/shard_map/all_gather | solution.py:86
  1129.3 91.1 %all-gather.19.cloned.1.call-done = bf16[2,3072,1152]{2,1,0:T(8,128)(2,1)} async-done(((bf16[2,96,1152]{2,1,0:T(8,128)(2,1)}), bf16[2,3072,1152]{2,1,0:T(8,128)(2,1)}) %all-gather.19.cloned.1.call-update) | async-done | bytes 14155792 | tf_op jit(solution)/shard_map/all_gather | solution.py:87
  1254.9 24.5 while.96
  1295.9 44.9 %all-gather.25.cloned.1.call-done = f32[256,2304]{1,0:T(8,128)} async-done(((f32[16,2304]{1,0:T(8,128)}), f32[256,2304]{1,0:T(8,128)}) %all-gather.25.cloned.1.call-update) | async-done | bytes 2359312 | tf_op jit(solution)/shard_map/all_gather | solution.py:21
  1340.8 16.2 while.97
  1360.5 622.5 %while.99 = (s32[]{:T(128)}, f32[16,2304]{1,0:T(8,128)S(1)}, f32[16,2304]{1,0:T(8,128)}, f32[8,16,2304]{2,1,0:T(8,128)}, f32[8,16,2304]{2,1,0:T(8,128)}, /*index...) while((s32[]{:T(128)}, f32[16,2304]{1,0:T(8,128)S(1)}, ...), condition=%wide.region_101.102_spmd.clone, body=%wide.region_36.101_spmd.clone.sunk | while | flops 21048852 | bytes 15533391 | solution.py:284
  1370.6 11.6 multiply_reduce_fusion.114
  1837.7 11.6 multiply_reduce_fusion.114
  2004.8 87.4 %concatenate.23 = f32[2304,3654]{0,1:T(8,128)} concatenate(f32[2304,1152]{0,1:T(8,128)} %fusion.242, f32[2304,1152]{0,1:T(8,128)} %fusion.271, f32[2304,1152]{0,1:T(8,128)} %fusion.238, f32[2304,1]{0,1:T(1,128)S(1)} %stack.536, f32[2304,1]{0,1:T(1,128)S(1)} %stack.537, f32[2304,1]{0,1:T(1,128)S(1)} %stack.538, f32[2304,1]{0,1:T(1,128)S(1)} %stack.539, ...), dimensions={1} | concatenate | bytes 67350528 | tf_op jit(solution)/shard_map/concatenate | solution.py:341
  2118.9 46.5 %pad_maximum_fusion = f32[3072,4608]{0,1:T(8,128)} fusion(f32[3072,1152]{0,1:T(8,128)} %fusion.270, f32[3072,1152]{0,1:T(8,128)} %fusion.269, f32[3072,1152]{0,1:T(8,128)S(1)} %fusion.287, f32[3072,1152]{0,1:T(8,128)} %fusion.286), kind=kLoop, calls=%fused_computation.549 | loop fusion | flops 42467328 | bytes 113246208 | tf_op jit(solution)/shard_map/concatenate | solution.py:373
  2165.5 55.9 %copy.101 = f32[3072,4608]{1,0:T(8,128)} copy(f32[3072,4608]{0,1:T(8,128)} %pad_maximum_fusion) | data formatting | bytes 113246208
  2230.0 38.7 %all-reduce.9 = (f32[2,1152]{1,0:T(2,128)}, f32[1152,2]{0,1:T(2,128)}) all-reduce(f32[2,1152]{1,0:T(2,128)S(1)} %pad_maximum_fusion.5, f32[1152,2]{0,1:T(2,128)S(1)} %fusion.266), channel_id=1, replica_groups=mesh['grp'=2,'seq'=16] {'grp','seq'}, use_global_device_ids=true, to_apply=%region_105.106 | all-reduce | flops 4608 | bytes 36864 | tf_op jit(solution)/shard_map/psum | solution.py:327
  2269.7 325.7 %all-reduce.13.cloned.1.call-done = f32[2304,3654]{0,1:T(8,128)} async-done(((f32[2304,3654]{0,1:T(8,128)}), f32[2304,3654]{0,1:T(8,128)}) %all-reduce.13.cloned.1.call-update) | async-done | bytes 33675280
  2607.6 466.2 %reduce-scatter.5.cloned.1.call-done = f32[96,4608]{1,0:T(8,128)} async-done(((f32[3072,4608]{1,0:T(8,128)}), f32[96,4608]{1,0:T(8,128)}) %reduce-scatter.5.cloned.1.call-update) | async-done | bytes 1769488
  (1554 shorter events, 1245.9 us)
Async XLA Ops:
  7.2 1007.9 %copy-start = (bf16[1152,2]{0,1:T(2,128)(2,1)S(1)}, bf16[1152,2]{0,1:T(2,128)(2,1)}, u32[]{:S(2)}) copy-start(bf16[1152,2]{0,1:T(2,128)(2,1)} %param.33) | copy-start | bytes 13828
  7.2 281.3 %copy-start.7 = (bf16[128,1152]{1,0:T(8,128)(2,1)S(1)}, bf16[128,1152]{1,0:T(8,128)(2,1)}, u32[]{:S(2)}) copy-start(bf16[128,1152]{1,0:T(8,128)(2,1)} %param.28) | copy-start | bytes 884740
  7.2 214.6 %copy-start.63 = (bf16[72,104]{1,0:T(8,128)(2,1)S(1)}, bf16[72,104]{1,0:T(8,128)(2,1)}, u32[]{:S(2)}) copy-start(bf16[72,104]{1,0:T(8,128)(2,1)} %param.36) | copy-start | bytes 44932
  7.2 281.3 %all-gather.13.cloned.1.call-start = ((), (), s32[]{:S(2)}) async-start(), calls=%async_computation.1 | async-start | bytes 10948608 | tf_op jit(solution)/shard_map/all_gather | solution.py:76
  8.0 871.5 %all-gather.23.cloned.1.call-start = ((), (), s32[]{:S(2)}) async-start(), calls=%async_computation.6 | async-start | bytes 2506752 | tf_op jit(solution)/shard_map/all_gather | solution.py:21
  146.2 189.9 %copy-start.51 = (f32[2304]{0:T(1024)}, f32[2304]{0:T(1024)S(1)}, u32[]{:S(2)}) copy-start(f32[2304]{0:T(1024)S(1)} %get-tuple-element.1096) | copy-start | bytes 27652
  146.2 189.9 %copy-start.53 = (f32[2304]{0:T(1024)}, f32[2304]{0:T(1024)S(1)}, u32[]{:S(2)}) copy-start(f32[2304]{0:T(1024)S(1)} %get-tuple-element.1097) | copy-start | bytes 27652
  146.2 189.9 %copy-start.55 = (f32[2304]{0:T(1024)}, f32[2304]{0:T(1024)S(1)}, u32[]{:S(2)}) copy-start(f32[2304]{0:T(1024)S(1)} %get-tuple-element.1098) | copy-start | bytes 27652
  146.3 189.9 %copy-start.57 = (f32[2304]{0:T(1024)}, f32[2304]{0:T(1024)S(1)}, u32[]{:S(2)}) copy-start(f32[2304]{0:T(1024)S(1)} %get-tuple-element.1099) | copy-start | bytes 27652
  147.4 145.5 %copy-start.88 = (f32[128]{0:T(128)}, f32[128]{0:T(128)S(1)}, u32[]{:S(2)}) copy-start(f32[128]{0:T(128)S(1)} %fusion.232) | copy-start | bytes 1540
  292.9 43.1 %collective-permute-start = (bf16[3,2304]{1,0:T(4,128)(2,1)S(1)}, bf16[3,2304]{1,0:T(4,128)(2,1)S(1)}, u32[]{:S(2)}, u32[]{:S(2)}) collective-permute-start(bf16[3,2304]{1,0:T(4,128)(2,1)S(1)} %slice.1807), channel_id=1, source_target_pairs={{0,1},{1,2},{2,3},{3,4},{4,5},{5,6},{6,7},{7,8},{8,9},{9,10},{10,1... | collective-permute-start | bytes 41480 | tf_op jit(solution)/shard_map/ppermute | solution.py:14
  815.7 128.3 %copy-start.3 = (f32[8,16,2304]{2,1,0:T(8,128)}, f32[8,16,2304]{2,1,0:T(8,128)S(1)}, u32[]{:S(2)}) copy-start(f32[8,16,2304]{2,1,0:T(8,128)S(1)} %get-tuple-element.2751) | copy-start | bytes 3538948
  816.3 127.6 %all-gather.21.cloned.1.call-start = ((), (), s32[]{:S(2)}) async-start(), calls=%async_computation.5 | async-start | bytes 2506752 | tf_op jit(solution)/shard_map/all_gather | solution.py:21
  817.8 193.3 %all-gather.15.cloned.1.call-start = ((), (), s32[]{:S(2)}) async-start(), calls=%async_computation.2 | async-start | bytes 5474304 | tf_op jit(solution)/shard_map/all_gather | solution.py:83
  818.4 297.7 %all-gather.17.cloned.1.call-start = ((), (), s32[]{:S(2)}) async-start(), calls=%async_computation.3 | async-start | bytes 14598144 | tf_op jit(solution)/shard_map/all_gather | solution.py:86
  819.0 401.4 %all-gather.19.cloned.1.call-start = ((), (), s32[]{:S(2)}) async-start(), calls=%async_computation.4 | async-start | bytes 14598144 | tf_op jit(solution)/shard_map/all_gather | solution.py:87
  819.6 521.2 %all-gather.25.cloned.1.call-start = ((), (), s32[]{:S(2)}) async-start(), calls=%async_computation.7 | async-start | bytes 2506752 | tf_op jit(solution)/shard_map/all_gather | solution.py:21
  819.6 431.5 %copy-start.50 = (f32[2304]{0:T(1024)}, f32[2304]{0:T(1024)S(1)}, u32[]{:S(2)}) copy-start(f32[2304]{0:T(1024)S(1)} %convert_element_type.133) | copy-start | bytes 27652
  1015.2 233.9 %copy-start.61 = (f32[128,2]{0,1:T(2,128)}, f32[128,2]{0,1:T(2,128)S(1)}, u32[]{:S(2)}) copy-start(f32[128,2]{0,1:T(2,128)S(1)} %get-tuple-element.1441) | copy-start | bytes 3076
  1015.3 233.8 %copy-start.64 = (f32[128]{0:T(128)}, f32[128]{0:T(128)S(1)}, u32[]{:S(2)}) copy-start(f32[128]{0:T(128)S(1)} %get-tuple-element.1440) | copy-start | bytes 1540
  1015.3 233.8 %copy-start.69 = (f32[128]{0:T(128)}, f32[128]{0:T(128)S(1)}, u32[]{:S(2)}) copy-start(f32[128]{0:T(128)S(1)} %fusion.265) | copy-start | bytes 1540
  1280.2 1315.2 %all-reduce.13.cloned.1.call-start = ((), (), s32[]{:S(2)}) async-start(), calls=%async_computation.9 | async-start | bytes 67387392
  1993.3 5.9 collective-permute-start.1
  2092.3 981.5 %reduce-scatter.5.cloned.1.call-start = ((), (), s32[]{:S(2)}) async-start(), calls=%async_computation.8 | async-start | bytes 58392576
  (196 other events, 2620.8 us)
Sparse Core Ops, SparseCore 0:
  11.0 91.2 all-gather.12
  816.5 62.9 all-gather.22
  882.8 61.0 all-gather.20
  946.7 64.4 all-gather.14
  1013.9 102.0 all-gather.16
  1118.9 101.4 all-gather.18
  1280.3 60.4 all-gather.24
  2092.4 502.9 all-reduce.12
  2601.9 471.8 reduce-scatter.4
where the time goes:
time: 3120 us; the launch traced here: 3090 us
  waiting for transfers between devices  1180 us (38%)
  other arithmetic  798 us (26%)
  local copies, waits for them, and re-layouts  518 us (17%)
  blocking collectives  352 us (11%)
  matrix products  131 us (4%)
  loops' own time  84.1 us (3%)
    unnamed x11, waiting for transfers between devices  794 us
    reduce_sum x56, other arithmetic, backward_block(): delta_rows.append(jnp.sum(scaled * decay_rate, 0) + in_sum * mixed_b[t])  187 us
    all_gather x3, waiting for transfers between devices, entering(): gathered = jax.tree.map(lambda a: lax.all_gather(a, axis), part)  169 us
    reduce_sum x40, other arithmetic, forward_block(): y_rows.append(jnp.sum(out_b[t][:, None] * state_now, 0))  147 us
    all_gather x1, waiting for transfers between devices, shards(): lax.all_gather(expert_in, ('grp', 'seq'), axis=1, tiled=True)  101 us
    reduce_sum x8, other arithmetic, backward_block(): out_rows.append(jnp.sum(state_list[t + 1] * dy_b[t][None, :], 1))  92.5 us
    all_gather x1, waiting for transfers between devices, shards(): lax.all_gather(expert_out, ('grp', 'seq'), axis=1, tiled=True)  91.1 us
    add x8, other arithmetic, backward_block(): rate_sum = rate_sum + scaled * delta_b[t][None, :]  88.6 us
  transfers between devices with their start and end apart: 11, of which 9 were waited for; matrix products, arithmetic and copies ran while one was open for 7% of the time, Pallas kernels for 0%

commit v1 on v0

v1 whole, which is shorter than its diff:
```python
import functools
import math

import jax
import jax.numpy as jnp
from jax import lax
from jax.experimental import pallas as pl
from jax.experimental.pallas import tpu as pltpu
from jax.sharding import PartitionSpec as P

eps_norm = 1e-05
split = 4
lanes = 128
subs = 8
log2e = 1.4426950408889634


def spread(coef_ref, first, spread_ref, steps, states):
    def one(s, _):
        rows = coef_ref[pl.ds(s, subs, stride=steps), :]
        for n in range(states):
            spread_ref[s, n] = jnp.broadcast_to(rows[:, first + n : first + n + 1], (subs, lanes))
        return 0

    lax.fori_loop(0, steps, one, 0, unroll=8)


def chain_rows(grow, state, reverse):
    row = lax.broadcasted_iota(jnp.int32, (subs, lanes), 0)
    shift = 1
    while shift < subs:
        turn = subs - shift if reverse else shift
        has = row < subs - shift if reverse else row >= shift
        near_grow = jnp.where(has, pltpu.roll(grow, turn, 0), 1.0)
        near_state = jnp.where(has, pltpu.roll(state, turn, 0), 0.0)
        state = state + grow * near_state
        grow = grow * near_grow
        shift *= 2
    return grow, state


def ends_kernel(
    first, reverse, states, steps, peers,
    delta_ref, reset_ref, drive_ref, coef_ref, rate_ref,
    grow_ref, state_ref, enter_ref,
    spread_ref, send_ref, arrive_ref, send_sem, arrive_sem,
):
    tile = pl.program_id(0)
    tiles = pl.num_programs(0)
    place = lax.axis_index("seq")
    high, low, core = place // split, place % split, lax.axis_index("grp")

    def other(k):
        return (core, lax.rem(high + (peers + 1 - k if reverse else k), peers + 1) * split + low)

    def copy_to(k, j):
        return pltpu.make_async_remote_copy(
            src_ref=send_ref.at[j],
            dst_ref=arrive_ref.at[k - 1, j],
            send_sem=send_sem.at[k - 1, j],
            recv_sem=arrive_sem.at[k - 1, j],
            device_id=other(k),
            device_id_type=pl.DeviceIdType.MESH,
        )

    @pl.when(tile == 0)
    def _():
        if peers:
            barrier = pltpu.get_barrier_semaphore()
            for k in range(1, peers + 1):
                pl.semaphore_signal(
                    barrier, inc=1, device_id=other(k), device_id_type=pl.DeviceIdType.MESH
                )
        spread(coef_ref, first, spread_ref, steps, states)

    rates = [jnp.broadcast_to(rate_ref[n : n + 1, :], (subs, lanes)) for n in range(states)]

    def one(turn, carry):
        s = steps - 1 - turn if reverse else turn
        total, held = carry
        step = delta_ref[pl.ds(s, subs, stride=steps), :] + reset_ref[pl.ds(s, subs, stride=steps), :]
        drive = drive_ref[pl.ds(s, subs, stride=steps), :]
        after = []
        for n in range(states):
            factor = jnp.exp2(step * rates[n])
            if reverse:
                after.append(factor * (held[n] + spread_ref[s, n] * drive))
            else:
                after.append(factor * held[n] + spread_ref[s, n] * drive)
        return total + step, tuple(after)

    zero = jnp.zeros((subs, lanes), jnp.float32)
    total, held = lax.fori_loop(0, steps, one, (zero, (zero,) * states), unroll=2)
    last = 0 if reverse else subs - 1
    for n in range(states):
        grow, state = chain_rows(jnp.exp2(total * rates[n]), held[n], reverse)
        grow_ref[n] = grow
        state_ref[n] = state
        if peers:
            send_ref[tile, n : n + 1] = grow[last : last + 1]
            send_ref[tile, states + n : states + n + 1] = state[last : last + 1]
    if not peers:
        enter_ref[...] = jnp.zeros_like(enter_ref)
        return

    @pl.when(tile == 0)
    def _():
        pl.semaphore_wait(pltpu.get_barrier_semaphore(), peers)

    for k in range(1, peers + 1):
        copy_to(k, tile).start()

    @pl.when(tile == tiles - 1)
    def _():
        for j in range(enter_ref.shape[1] // lanes):
            total = jnp.zeros((states, lanes), jnp.float32)
            for k in range(peers, 0, -1):
                copy_to(k, j).wait()
                piece = arrive_ref[k - 1, j]
                has = high + k <= peers if reverse else high >= k
                total = jnp.where(has, piece[states:] + piece[:states] * total, 0.0)
            enter_ref[:, j * lanes : (j + 1) * lanes] = total


def scan_ends(delta, reset, drive, coef, rate, first, reverse, peers):
    row_count, width = delta.shape
    states = rate.shape[0]
    steps = row_count // subs
    tiles = width // lanes
    column = pl.BlockSpec((row_count, lanes), lambda j: (0, j))
    whole = pl.BlockSpec((row_count, lanes), lambda j: (0, 0))
    ends = pl.BlockSpec((states, subs, lanes), lambda j: (0, 0, j))
    params = dict(vmem_limit_bytes=48 << 20)
    if peers:
        params.update(collective_id=2 if reverse else 1, has_side_effects=True)
    slots = max(peers, 1)
    return pl.pallas_call(
        functools.partial(ends_kernel, first, reverse, states, steps, peers),
        grid=(tiles,),
        in_specs=[column, whole, column, whole, pl.BlockSpec((states, lanes), lambda j: (0, j))],
        out_specs=[ends, ends, pl.BlockSpec((states, width), lambda j: (0, 0))],
        out_shape=[jax.ShapeDtypeStruct((states, subs, width), jnp.float32)] * 2
        + [jax.ShapeDtypeStruct((states, width), jnp.float32)],
        scratch_shapes=[
            pltpu.VMEM((steps, states, subs, lanes), jnp.float32),
            pltpu.VMEM((tiles, 2 * states, lanes), jnp.float32),
            pltpu.VMEM((slots, tiles, 2 * states, lanes), jnp.float32),
            pltpu.SemaphoreType.DMA((slots, tiles)),
            pltpu.SemaphoreType.DMA((slots, tiles)),
        ],
        compiler_params=pltpu.CompilerParams(**params),
        cost_estimate=pl.CostEstimate(flops=1000, bytes_accessed=1000, transcendentals=0),
    )(delta, reset, drive, coef, rate)


def forward_kernel(first_in, first_out, states, steps, delta_ref, reset_ref, drive_ref, coef_ref, rate_ref, grow_ref, state_ref, enter_ref, y_ref, start_ref, hist_ref, in_ref, out_ref):
    @pl.when(pl.program_id(0) == 0)
    def _():
        spread(coef_ref, first_in, in_ref, steps, states)
        spread(coef_ref, first_out, out_ref, steps, states)

    rates = [jnp.broadcast_to(rate_ref[n : n + 1, :], (subs, lanes)) for n in range(states)]
    row = lax.broadcasted_iota(jnp.int32, (subs, lanes), 0)
    held = []
    for n in range(states):
        near_grow = jnp.where(row >= 1, pltpu.roll(grow_ref[n], 1, 0), 1.0)
        near_state = jnp.where(row >= 1, pltpu.roll(state_ref[n], 1, 0), 0.0)
        start = near_state + near_grow * jnp.broadcast_to(enter_ref[n : n + 1, :], (subs, lanes))
        start_ref[n] = start
        held.append(start)

    def one(s, held):
        step = delta_ref[pl.ds(s, subs, stride=steps), :] + reset_ref[pl.ds(s, subs, stride=steps), :]
        drive = drive_ref[pl.ds(s, subs, stride=steps), :]
        after = []
        y = jnp.zeros((subs, lanes), jnp.float32)
        for n in range(states):
            now = jnp.exp2(step * rates[n]) * held[n] + in_ref[s, n] * drive
            hist_ref[0, s, n] = now
            y = y + out_ref[s, n] * now
            after.append(now)
        y_ref[pl.ds(s, subs, stride=steps), :] = y
        return tuple(after)

    lax.fori_loop(0, steps, one, tuple(held), unroll=2)


def scan_forward(delta, reset, drive, coef, rate, grow, state, enter, first_in, first_out):
    row_count, width = delta.shape
    states = rate.shape[0]
    steps = row_count // subs
    tiles = width // lanes
    column = pl.BlockSpec((row_count, lanes), lambda j: (0, j))
    whole = pl.BlockSpec((row_count, lanes), lambda j: (0, 0))
    ends = pl.BlockSpec((states, subs, lanes), lambda j: (0, 0, j))
    per_state = pl.BlockSpec((states, lanes), lambda j: (0, j))
    return pl.pallas_call(
        functools.partial(forward_kernel, first_in, first_out, states, steps),
        grid=(tiles,),
        in_specs=[column, whole, column, whole, per_state, ends, ends, per_state],
        out_specs=[column, ends, pl.BlockSpec((1, steps, states, subs, lanes), lambda j: (j, 0, 0, 0, 0))],
        out_shape=[
            jax.ShapeDtypeStruct((row_count, width), jnp.float32),
            jax.ShapeDtypeStruct((states, subs, width), jnp.float32),
            jax.ShapeDtypeStruct((tiles, steps, states, subs, lanes), jnp.float32),
        ],
        scratch_shapes=[pltpu.VMEM((steps, states, subs, lanes), jnp.float32)] * 2,
        compiler_params=pltpu.CompilerParams(vmem_limit_bytes=48 << 20),
        cost_estimate=pl.CostEstimate(flops=1000, bytes_accessed=1000, transcendentals=0),
    )(delta, reset, drive, coef, rate, grow, state, enter)


def backward_kernel(first_in, first_out, states, steps, delta_ref, reset_ref, drive_ref, dy_ref, coef_ref, rate_ref, start_ref, hist_ref, grow_ref, state_ref, enter_ref, q_ref, r_ref, rsum_ref, din_ref, dout_ref, in_ref, out_ref, ain_ref, aout_ref):
    tile = pl.program_id(0)

    @pl.when(tile == 0)
    def _():
        spread(coef_ref, first_in, in_ref, steps, states)
        spread(coef_ref, first_out, out_ref, steps, states)
        ain_ref[...] = jnp.zeros_like(ain_ref)
        aout_ref[...] = jnp.zeros_like(aout_ref)

    row = lax.broadcasted_iota(jnp.int32, (subs, lanes), 0)
    rates = [jnp.broadcast_to(rate_ref[n : n + 1, :], (subs, lanes)) for n in range(states)]
    later = []
    for n in range(states):
        near_grow = jnp.where(row < subs - 1, pltpu.roll(grow_ref[n], subs - 1, 0), 1.0)
        near_state = jnp.where(row < subs - 1, pltpu.roll(state_ref[n], subs - 1, 0), 0.0)
        later.append(near_state + near_grow * jnp.broadcast_to(enter_ref[n : n + 1, :], (subs, lanes)))

    def at(s, load_before, carry):
        later, sums = carry
        delta = delta_ref[pl.ds(s, subs, stride=steps), :]
        step = delta + reset_ref[pl.ds(s, subs, stride=steps), :]
        drive = drive_ref[pl.ds(s, subs, stride=steps), :]
        dy = dy_ref[pl.ds(s, subs, stride=steps), :]
        q = jnp.zeros((subs, lanes), jnp.float32)
        r = jnp.zeros((subs, lanes), jnp.float32)
        after, sums_after = [], []
        for n in range(states):
            d_state = out_ref[s, n] * dy + later[n]
            back = jnp.exp2(step * rates[n]) * d_state
            scaled = back * load_before(n)
            sums_after.append(sums[n] + scaled * delta)
            q = q + scaled * rates[n]
            r = r + d_state * in_ref[s, n]
            ain_ref[s, n] += d_state * drive
            aout_ref[s, n] += hist_ref[0, s, n] * dy
            after.append(back)
        q_ref[pl.ds(s, subs, stride=steps), :] = q * (1.0 / log2e)
        r_ref[pl.ds(s, subs, stride=steps), :] = r
        return tuple(after), tuple(sums_after)

    zero = jnp.zeros((subs, lanes), jnp.float32)

    def one(turn, carry):
        s = steps - 1 - turn
        return at(s, lambda n: hist_ref[0, s - 1, n], carry)

    carry = lax.fori_loop(0, steps - 1, one, (tuple(later), (zero,) * states))
    _, sums = at(0, lambda n: start_ref[n], carry)
    for n in range(states):
        rsum_ref[n : n + 1, :] = jnp.sum(sums[n] * rates[n], 0, keepdims=True) * (1.0 / log2e)

    @pl.when(tile == pl.num_programs(0) - 1)
    def _():
        ones = jnp.ones((subs, lanes), jnp.bfloat16)

        def fold(ref, s):
            values = ref[s].reshape(states * subs, lanes)
            high = values.astype(jnp.bfloat16)
            low = (values - high.astype(jnp.float32)).astype(jnp.bfloat16)
            dims = (((1,), (1,)), ((), ()))
            return lax.dot_general(ones, high, dims, preferred_element_type=jnp.float32) + lax.dot_general(ones, low, dims, preferred_element_type=jnp.float32)

        def both(s, _):
            din_ref[pl.ds(s, 1), :] = fold(ain_ref, s)[:1]
            dout_ref[pl.ds(s, 1), :] = fold(aout_ref, s)[:1]
            return 0

        lax.fori_loop(0, steps, both, 0)


def scan_backward(delta, reset, drive, dy, coef, rate, start, hist, grow, state, enter, first_in, first_out):
    row_count, width = delta.shape
    states = rate.shape[0]
    steps = row_count // subs
    tiles = width // lanes
    column = pl.BlockSpec((row_count, lanes), lambda j: (0, j))
    whole = pl.BlockSpec((row_count, lanes), lambda j: (0, 0))
    ends = pl.BlockSpec((states, subs, lanes), lambda j: (0, 0, j))
    per_state = pl.BlockSpec((states, lanes), lambda j: (0, j))
    folded = pl.BlockSpec((steps, states * subs), lambda j: (0, 0))
    q, r, rsum, din, dout = pl.pallas_call(
        functools.partial(backward_kernel, first_in, first_out, states, steps),
        grid=(tiles,),
        in_specs=[column, whole, column, column, whole, per_state, ends, pl.BlockSpec((1, steps, states, subs, lanes), lambda j: (j, 0, 0, 0, 0)), ends, ends, per_state],
        out_specs=[column, column, per_state, folded, folded],
        out_shape=[
            jax.ShapeDtypeStruct((row_count, width), jnp.float32),
            jax.ShapeDtypeStruct((row_count, width), jnp.float32),
            jax.ShapeDtypeStruct((states, width), jnp.float32),
            jax.ShapeDtypeStruct((steps, states * subs), jnp.float32),
            jax.ShapeDtypeStruct((steps, states * subs), jnp.float32),
        ],
        scratch_shapes=[pltpu.VMEM((steps, states, subs, lanes), jnp.float32)] * 4,
        compiler_params=pltpu.CompilerParams(vmem_limit_bytes=56 << 20),
        cost_estimate=pl.CostEstimate(flops=1000, bytes_accessed=1000, transcendentals=0),
    )(delta, reset, drive, dy, coef, rate, start, hist, grow, state, enter)

    def unfold(folded_rows):
        return folded_rows.reshape(steps, states, subs).transpose(2, 0, 1).reshape(row_count, states)

    return q, r, rsum, unfold(din), unfold(dout)


def experts_kernel(
    expert_count, second_ref, routed_ref, route_ref, *refs
):
    weights_in, weights_out = refs[:expert_count], refs[expert_count : 2 * expert_count]
    sums_ref, grads_ref, y_ref, d_ref = refs[2 * expert_count :]
    step = pl.program_id(0)
    blocks, hidden, model_width = weights_in[0].shape
    rows = blocks * hidden

    @pl.when(step == 0)
    def _():
        y_ref[...] = jnp.zeros_like(y_ref)
        d_ref[...] = jnp.zeros_like(d_ref)

    up = jnp.concatenate([w[...].reshape(rows, model_width) for w in weights_in], 0)
    down = jnp.concatenate([w[...].reshape(rows, model_width) for w in weights_out], 0)
    second, routed = second_ref[...], routed_ref[...]
    pre = matmul_nt(second, up)
    column = lax.broadcasted_iota(jnp.int32, (1, expert_count * rows), 1)
    owner = jnp.zeros_like(column)
    for e in range(1, expert_count):
        owner = owner + (column >= e * rows).astype(jnp.int32)
    picked = route_ref[:, :1] == owner.astype(jnp.float32)
    half = 0.5 + 0.5 * lax.erf(pre * (0.5**0.5))
    bell = jnp.exp(-0.5 * pre * pre) * (1.0 / (2.0 * math.pi) ** 0.5)
    act = low_bits(jnp.where(picked, pre * half, 0.0))
    d_pre = low_bits(jnp.where(picked, matmul_nt(routed, down) * (half + pre * bell), 0.0))
    y_ref[...] += matmul(act, down)
    d_ref[...] += matmul(d_pre, up)
    grad_up = low_bits(matmul_tn(d_pre, second))
    grad_down = low_bits(matmul_tn(act, routed))
    for e in range(expert_count):
        for b in range(blocks):
            at = e * rows + b * hidden
            grads_ref[b, e * hidden : (e + 1) * hidden] = grad_up[at : at + hidden]
            to = (expert_count + e) * hidden
            grads_ref[b, to : to + hidden] = grad_down[at : at + hidden]

    @pl.when(step == pl.num_programs(0) - 1)
    def _():
        sums_ref[:, :model_width] = low_bits(y_ref[...])
        sums_ref[:, model_width:] = low_bits(d_ref[...])


def run_experts(second, routed, route_lanes, parts, hidden):
    row_count, model_width = second.shape
    expert_count = len(parts) // 2
    block_count = parts[0][0].shape[0]
    blocks = 2
    fixed = pl.BlockSpec((row_count, model_width), lambda i: (0, 0))

    def spec(first):
        return pl.BlockSpec((blocks, hidden, model_width), lambda i: (i, first // hidden, 0))

    return pl.pallas_call(
        functools.partial(experts_kernel, expert_count),
        grid=(block_count // blocks,),
        in_specs=[fixed, fixed, pl.BlockSpec((row_count, lanes), lambda i: (0, 0))]
        + [spec(first) for _, first in parts],
        out_specs=[
            pl.BlockSpec((row_count, 2 * model_width), lambda i: (0, 0)),
            pl.BlockSpec((blocks, 2 * expert_count * hidden, model_width), lambda i: (i, 0, 0)),
        ],
        out_shape=[
            jax.ShapeDtypeStruct((row_count, 2 * model_width), jnp.bfloat16),
            jax.ShapeDtypeStruct(
                (block_count, 2 * expert_count * hidden, model_width), jnp.bfloat16
            ),
        ],
        scratch_shapes=[pltpu.VMEM((row_count, model_width), jnp.float32)] * 2,
        compiler_params=pltpu.CompilerParams(vmem_limit_bytes=56 << 20),
        cost_estimate=pl.CostEstimate(flops=1000, bytes_accessed=1000, transcendentals=0),
    )(second, routed, route_lanes, *[w for w, _ in parts])


def norm_rows(values, gain_row):
    return values * lax.rsqrt(jnp.mean(values * values, -1, keepdims=True) + eps_norm) * gain_row


def matmul(first_op, second_op):
    return jnp.dot(first_op, second_op, preferred_element_type=jnp.float32)


def matmul_nt(first_op, second_op):
    return lax.dot_general(
        first_op, second_op, (((1,), (1,)), ((), ())), preferred_element_type=jnp.float32
    )


def matmul_tn(first_op, second_op):
    return lax.dot_general(
        first_op, second_op, (((0,), (0,)), ((), ())), preferred_element_type=jnp.float32
    )


def low_bits(value):
    return value.astype(jnp.bfloat16)


def swap_low(value, k):
    count = lax.axis_size("seq")
    return lax.ppermute(value, "seq", [(s, s ^ k) for s in range(count)])


def turn_high(value, k):
    count = lax.axis_size("seq")
    return lax.ppermute(value, "seq", [(s, (s + split * k) % count) for s in range(count)])


def from_high(value, k):
    count = lax.axis_size("seq")
    pairs = [(s, s + split * k) for s in range(count) if 0 <= s + split * k < count]
    return lax.ppermute(value, "seq", pairs)


def swap_core(value):
    return lax.ppermute(value, "grp", [(0, 1), (1, 0)])


def high_groups():
    count = lax.axis_size("seq")
    return [[h * split + l for h in range(count // split)] for l in range(split)]


def gather_low(value):
    low = lax.axis_index("seq") % split
    first_bit, second_bit = low % 2 == 1, low // 2 == 1
    own, one, two, three = [value] + [swap_low(value, k) for k in range(1, split)]
    a, b = jnp.where(first_bit, one, own), jnp.where(first_bit, own, one)
    c, d = jnp.where(first_bit, three, two), jnp.where(first_bit, two, three)
    pieces = [
        jnp.where(second_bit, c, a),
        jnp.where(second_bit, d, b),
        jnp.where(second_bit, a, c),
        jnp.where(second_bit, b, d),
    ]
    return jnp.concatenate(pieces, 0)


def scatter_low(partial):
    low = lax.axis_index("seq") % split
    rows = partial.shape[0] // split

    def block(at):
        return lax.dynamic_slice_in_dim(partial, at * rows, rows, 0)

    arrived = [swap_low(low_bits(block(low ^ k)), k) for k in range(1, split)]
    return sum(a.astype(jnp.float32) for a in [block(low)] + arrived)


def sum_low(partial):
    low_partial = low_bits(partial)
    arrived = [swap_low(low_partial, k) for k in range(1, split)]
    return partial + sum(a.astype(jnp.float32) for a in arrived)


def gather_high(value):
    high_count = lax.axis_size("seq") // split
    if high_count > 4:
        return lax.all_gather(value, "seq", axis_index_groups=high_groups())
    high = lax.axis_index("seq") // split
    turned = [turn_high(value, k) for k in range(1, high_count)]
    line = turned[::-1] + [value] + turned[::-1]
    return lax.dynamic_slice_in_dim(jnp.stack(line), high_count - 1 - high, high_count, 0)


def gather_core(own):
    full = jnp.stack([own, swap_core(own)])
    return full.reshape((-1,) + own.shape[1:])


def after(value, *others):
    return lax.optimization_barrier((value,) + others)[0]


def pad_rows(value, rows):
    return jnp.pad(value, ((0, rows - value.shape[0]), (0, 0)))


def fold_core(partial, rows):
    high_count = lax.axis_size("seq") // split
    blocks = partial.reshape(2, high_count, rows, partial.shape[-1])
    arrived = swap_core(low_bits(blocks[1]))
    return low_bits(blocks[0].astype(jnp.float32) + arrived.astype(jnp.float32))


def fold_high(mine):
    high_count = lax.axis_size("seq") // split
    if high_count > 4:
        return lax.psum_scatter(
            mine.astype(jnp.float32), "seq", scatter_dimension=0, axis_index_groups=high_groups()
        )
    high = lax.axis_index("seq") // split

    def block(at):
        return lax.dynamic_index_in_dim(mine, at % high_count, 0, False)

    arrived = [turn_high(block(high + k), k) for k in range(1, high_count)]
    return sum(a.astype(jnp.float32) for a in [block(high)] + arrived)


def sum_all(partial):
    high_count = lax.axis_size("seq") // split
    total = partial + swap_core(partial)
    step = 1
    while step < high_count * split:
        total = total + swap_low(total, step)
        step *= 2
    return total


def entering_state(grow, state, reverse):
    high_count = lax.axis_size("seq") // split
    packed = jnp.concatenate([grow, state], 0)
    states = grow.shape[0]
    if high_count > 4:
        high = lax.axis_index("seq") // split
        every = lax.all_gather(packed, "seq", axis_index_groups=high_groups())

        def one(turn, total):
            source = high_count - 1 - turn if reverse else turn
            piece = lax.dynamic_index_in_dim(every, source, 0, False)
            return piece[states:] + piece[:states] * total

        ahead = high_count - 1 - high if reverse else high
        return lax.fori_loop(0, ahead, one, jnp.zeros_like(state))
    total = jnp.zeros_like(state)
    near = [from_high(packed, -k if reverse else k) for k in range(1, high_count)]
    for piece in near[::-1]:
        total = piece[states:] + piece[:states] * total
    return total


def shards(
    tokens,
    routes,
    lengths,
    grad_out,
    norm_gains,
    router,
    in_weight,
    conv_weight,
    x_weight,
    dt_weight,
    dt_bias,
    a_log,
    skip_gain,
    out_weight,
    expert_in,
    expert_out,
):
    channels, tap_count = conv_weight.shape
    dt_rank = dt_weight.shape[1]
    states = a_log.shape[1]
    expert_count, hidden, model_width = expert_in.shape
    own_rows = tokens.shape[0]
    row_count = own_rows * split
    high_count = lax.axis_size("seq") // split
    low = lax.axis_index("seq") % split
    high = lax.axis_index("seq") // split
    coef_count = dt_rank + 2 * states
    channel_rows = -(-channels // 16) * 16
    width = 2 * high_count * channel_rows
    hidden_rows = expert_count * hidden
    small_width = -(-(coef_count + dt_rank + tap_count + 2 + states) // lanes) * lanes

    small = jnp.concatenate(
        [x_weight, dt_weight, conv_weight, dt_bias[:, None], a_log, skip_gain[:, None]], 1
    )
    small = jnp.pad(small, ((0, 0), (0, small_width - small.shape[1])))
    inputs = tokens.astype(jnp.float32)
    edge = 16
    halo = from_high(tokens[own_rows - edge :], 1).astype(jnp.float32)
    normed_own = low_bits(norm_rows(jnp.concatenate([inputs, halo], 0), norm_gains[0]))
    payload = pad_rows(jnp.concatenate([in_weight[0], small], 1), channel_rows)
    first_full = gather_core(gather_high(payload)).reshape(width, -1)
    normed = gather_low(normed_own).reshape(split, own_rows + edge, model_width)
    normed_edge = normed[split - 1, own_rows:]
    normed = normed[:, :own_rows].reshape(row_count, model_width)
    first_in, small_full = first_full[:, :model_width], first_full[:, model_width:]
    x_full = small_full[:, :coef_count]
    at = coef_count
    dt_full = small_full[:, at : at + dt_rank]
    at = at + dt_rank
    conv_taps = small_full[:, at : at + tap_count].astype(jnp.float32)
    at = at + tap_count
    bias_vals = small_full[:, at].astype(jnp.float32)
    at = at + 1
    decay_rate = -jnp.exp(small_full[:, at : at + states].astype(jnp.float32)).T
    at = at + states
    skip_vals = small_full[:, at].astype(jnp.float32)
    rate = decay_rate * log2e

    early_part = jnp.concatenate(
        [
            pad_rows(in_weight[1], channel_rows),
            pad_rows(out_weight, channel_rows),
            expert_in[0],
        ],
        0,
    )
    early_part = gather_high(after(early_part, first_full))
    routed_part = jnp.concatenate(
        [grad_out, routes[:, None].astype(jnp.float32) * jnp.ones((1, lanes), jnp.float32)], 1
    )
    routed_part = gather_low(after(low_bits(routed_part), normed))
    grad_rows = routed_part[:, :model_width]
    routes_all = routed_part[:, model_width : model_width + 1].astype(jnp.int32)
    late_part = jnp.concatenate(
        [expert_in[1:].reshape(-1, model_width), expert_out.reshape(-1, model_width)], 0
    )

    place = high * row_count + jnp.arange(row_count, dtype=jnp.int32)
    first_len = lengths[0, 0]
    offset = jnp.where(place < first_len, place, place - first_len)
    reset = jnp.where(offset[:, None] == 0, 1e30, 0.0) * jnp.ones((1, lanes), jnp.float32)
    valid_rows = [
        (offset >= tap_count - 1 - k).astype(jnp.float32)[:, None] for k in range(tap_count)
    ]

    all_input = low_bits(matmul_nt(jnp.concatenate([normed_edge, normed], 0), first_in))
    conv_input = all_input[edge:]
    window = all_input[edge - (tap_count - 1) :].astype(jnp.float32)
    conv_sum = sum(
        conv_taps[:, k] * window[k : k + row_count] * valid_rows[k] for k in range(tap_count)
    )
    mixed_in = low_bits(jax.nn.silu(conv_sum))
    mixed_val = mixed_in.astype(jnp.float32)
    coef_pad = jnp.pad(x_full, ((0, 0), (0, lanes - coef_count)))
    coef_rows = sum_low(matmul(mixed_in, coef_pad))
    dt_low = low_bits(coef_rows[:, :dt_rank])
    dt_pre = matmul_nt(dt_low, dt_full) + bias_vals
    step_size = jax.nn.softplus(dt_pre)
    drive = step_size * mixed_val
    first_b, first_c = dt_rank, dt_rank + states
    peers = high_count - 1 if high_count <= 4 else 0
    grow, state, enter = scan_ends(
        step_size, reset, drive, coef_rows, rate, first_b, False, peers
    )
    slice_grow = grow[:, subs - 1]
    if not peers:
        enter = entering_state(slice_grow, state[:, subs - 1], False)
    enter, early_part, late_part = lax.optimization_barrier((enter, early_part, late_part))
    early_full = gather_core(early_part)
    late_part = gather_high(late_part)
    y_scan, start, hist = scan_forward(
        step_size, reset, drive, coef_rows, rate, grow, state, enter, first_b, first_c
    )
    y_scan, early_full = lax.optimization_barrier((y_scan, early_full))
    second_in = early_full[:, :channel_rows].reshape(width, model_width)
    out_full = early_full[:, channel_rows : 2 * channel_rows].reshape(width, model_width)
    z_gate = matmul_nt(normed, second_in)
    y_value = y_scan + skip_vals * mixed_val
    gate_z = jax.nn.silu(z_gate)
    gated = low_bits(y_value * gate_z)
    resid = inputs + scatter_low(matmul(gated, out_full))

    resid, late_part = lax.optimization_barrier((resid, late_part))
    late_full = gather_core(late_part)
    second_own = low_bits(norm_rows(resid, norm_gains[1]))
    second = gather_low(second_own)

    def gate_of(rows, row_routes):
        logits = matmul(rows, router)
        chosen = row_routes == jnp.arange(expert_count, dtype=jnp.int32)[None, :]
        chosen = chosen.astype(jnp.float32)
        probs = jax.nn.softmax(logits, -1)
        return logits, chosen, jnp.sum(probs * chosen, -1, keepdims=True)

    gate_rows = gate_of(second, routes_all)[2]
    routed = low_bits(gate_rows * grad_rows.astype(jnp.float32))
    parts = [(early_full[:, 2 * channel_rows :], 0)]
    parts += [(late_full, e * hidden) for e in range(2 * expert_count - 1)]
    step_rows = hidden
    if hidden % 16:
        step_rows = 2 * high_count * hidden // 4
        parts = [
            (w[:, a : a + hidden].reshape(4, step_rows, model_width), 0) for w, a in parts
        ]
    sums, hidden_grads = run_experts(
        second, routed, routed_part[:, model_width:].astype(jnp.float32), parts, step_rows
    )
    if hidden % 16:
        pieces = hidden_grads.reshape(4, 2 * expert_count, -1, hidden, model_width)
        hidden_grads = pieces.swapaxes(1, 2).reshape(-1, 2 * hidden_rows, model_width)
    hidden_mine = fold_core(hidden_grads, 2 * hidden_rows)
    sums = scatter_low(sums)
    expert_y, d_second = sums[:, :model_width], sums[:, model_width:]
    d_second, hidden_mine = lax.optimization_barrier((d_second, hidden_mine))
    cut = hidden_rows * 2 // 3
    hidden_early = fold_high(hidden_mine[:, :cut])
    hidden_mine = hidden_mine[:, cut:]
    logits, chosen, gate_own = gate_of(second_own, routes[:, None])
    mixed_out = low_bits(resid + gate_own * expert_y)
    d_gate = jnp.sum(expert_y * grad_out, -1, keepdims=True)
    _, soft_pull = jax.vjp(lambda v: jax.nn.softmax(v, -1), logits)
    d_logits = low_bits(soft_pull(chosen * d_gate)[0])
    grad_router = matmul_tn(d_logits, second_own)
    d_second = d_second + matmul_nt(d_logits, router)
    _, norm_pull_two = jax.vjp(norm_rows, resid, norm_gains[1])
    d_resid_norm, d_gain_two = norm_pull_two(d_second)
    d_resid = grad_out + d_resid_norm

    g_branch = gather_low(low_bits(d_resid))
    d_gated = matmul_nt(g_branch, out_full)
    d_y = d_gated * gate_z
    _, silu_pull = jax.vjp(jax.nn.silu, z_gate)
    d_z = silu_pull(d_gated * y_value)[0]
    gate_grads = jnp.concatenate(
        [matmul_tn(low_bits(d_z), normed), matmul_tn(gated, g_branch)], 1
    )
    gate_mine = fold_core(gate_grads, channel_rows)
    back_grow, back_state, back_enter = scan_ends(
        step_size, reset, d_y, coef_rows, rate, first_c, True, peers
    )
    if not peers:
        back_enter = entering_state(slice_grow, back_state[:, 0], True)
    back_enter, hidden_mine = lax.optimization_barrier((back_enter, hidden_mine))
    hidden_late = fold_high(hidden_mine)
    scaled_sum, in_sum, rate_sum, d_in_coef, d_out_coef = scan_backward(
        step_size,
        reset,
        drive,
        d_y,
        coef_rows,
        rate,
        start,
        hist,
        back_grow,
        back_state,
        back_enter,
        first_b,
        first_c,
    )
    d_step = scaled_sum + in_sum * mixed_val
    d_mixed = skip_vals * d_y + in_sum * step_size
    grad_skip = jnp.sum(d_y * mixed_val, 0)
    d_dt = d_step * jax.nn.sigmoid(dt_pre)
    grad_bias = jnp.sum(d_dt, 0)
    g_dt = low_bits(d_dt)
    grad_dt = matmul_tn(g_dt, dt_low)
    part_coef = jnp.concatenate([matmul(g_dt, dt_full), d_in_coef, d_out_coef], 1)
    part_coef = jnp.pad(part_coef, ((0, 0), (0, lanes - coef_count)))
    g_coef = low_bits(sum_low(part_coef)[:, :coef_count])
    grad_x = matmul_tn(mixed_in, g_coef)
    d_mixed = d_mixed + matmul_nt(g_coef, x_full)
    _, conv_pull = jax.vjp(jax.nn.silu, conv_sum)
    d_conv = conv_pull(d_mixed)[0]
    grad_conv = jnp.stack(
        [jnp.sum(d_conv * valid_rows[k] * window[k : k + row_count], 0) for k in range(tap_count)],
        1,
    )
    d_window = sum(
        jnp.pad(conv_taps[:, k] * d_conv * valid_rows[k], ((k, tap_count - 1 - k), (0, 0)))
        for k in range(tap_count)
    )
    from_next = from_high(d_window[: tap_count - 1], -1)
    d_input = d_window[tap_count - 1 :] + jnp.pad(
        from_next, ((row_count - (tap_count - 1), 0), (0, 0))
    )
    g_in = low_bits(d_input)
    g_in, hidden_late, gate_mine = lax.optimization_barrier((g_in, hidden_late, gate_mine))
    hidden_own = jnp.concatenate([hidden_early, hidden_late], 0)
    gate_own_grads = fold_high(gate_mine)
    g_z = low_bits(d_z)
    d_normed = scatter_low(matmul(g_in, first_in) + matmul(g_z, second_in))
    _, norm_pull_one = jax.vjp(norm_rows, inputs, norm_gains[0])
    d_inputs, d_gain_one = norm_pull_one(d_normed)
    grad_tokens = d_resid + d_inputs

    rest = jnp.concatenate(
        [grad_x, grad_dt, grad_conv, grad_bias[:, None], rate_sum.T, grad_skip[:, None]], 1
    )
    rest = jnp.pad(rest, ((0, 0), (0, small_width - rest.shape[1])))
    first_own = fold_high(
        fold_core(jnp.concatenate([matmul_tn(g_in, normed), rest], 1), channel_rows)
    )[:channels]
    rest_own = first_own[:, model_width:]
    gate_own_grads = gate_own_grads[:channels]
    sums = sum_all(jnp.concatenate([jnp.stack([d_gain_one, d_gain_two]), grad_router], 0))
    ends = [0]
    for count in (coef_count, dt_rank, tap_count, 1, states, 1):
        ends.append(ends[-1] + count)
    grad_x, grad_dt, grad_conv, grad_bias, grad_alog, grad_skip = (
        rest_own[:, a:b] for a, b in zip(ends[:-1], ends[1:], strict=True)
    )
    return (
        mixed_out,
        grad_tokens,
        sums[:2],
        sums[2:].T,
        jnp.stack([first_own[:, :model_width], gate_own_grads[:, :model_width]]),
        grad_conv,
        grad_x,
        grad_dt,
        grad_bias[:, 0],
        grad_alog,
        grad_skip[:, 0],
        gate_own_grads[:, model_width:],
        hidden_own[:hidden_rows].reshape(expert_count, hidden, model_width),
        hidden_own[hidden_rows:].reshape(expert_count, hidden, model_width),
    )


def solution(mesh):
    both = ("grp", "seq")
    in_specs = (
        P(both, None),
        P(both),
        P("grp", None),
        P(both, None),
        P(),
        P(),
        P(None, both, None),
        P(both, None),
        P(both, None),
        P(both, None),
        P(both),
        P(both, None),
        P(both),
        P(both, None),
        P(None, both, None),
        P(None, both, None),
    )
    out_specs = (
        P(both, None),
        P(both, None),
        P(),
        P(),
        P(None, both, None),
        P(both, None),
        P(both, None),
        P(both, None),
        P(both),
        P(both, None),
        P(both),
        P(both, None),
        P(None, both, None),
        P(None, both, None),
    )
    return jax.shard_map(shards, mesh=mesh, in_specs=in_specs, out_specs=out_specs, check_vma=False)
```

time: 3120 us -> 549 us (0.18)
  waiting for transfers between devices: 1180 us -> 187 us
  other arithmetic: 798 us -> 43.4 us
  local copies, waits for them, and re-layouts: 518 us -> 51.2 us
  blocking collectives: 352 us -> 0 us
  Pallas kernels: 0 us -> 133 us
  matrix products: 131 us -> 24.4 us
  starting transfers between devices: 5.87 us -> 97.4 us
  loops' own time: 84.1 us -> 0 us
    unnamed x11 -> x0, waiting for transfers between devices: 794 us -> none
    reduce_sum x130 -> x4, other arithmetic: 476 us -> 0.48 us  [the longest x1 0.35 us: norm_rows(): values * lax.rsqrt(jnp.mean(values * values, -1, keepdims=True) + eps_norm)]
    all_gather x7 -> x0, waiting for transfers between devices: 385 us -> none  [the longest x3 169 us: entering(): gathered = jax.tree.map(lambda a: lax.all_gather(a, axis), part)]
    all_gather x4 -> x0, blocking collectives: 276 us -> none  [the longest x1 73.8 us: shards(): lax.all_gather(dt_weight, ('grp', 'seq'), axis=0, tiled=True)]
    ppermute x2 -> x61, waiting for transfers between devices: 3.37 us -> 187 us  [the longest x31 94.3 us: swap_low(): return lax.ppermute(value, 'seq', [(s, s ^ k) for s in range(count)])]
    add x58 -> x11, other arithmetic: 158 us -> 5.99 us  [the longest x4 4.5 us: fold_high(): return sum((a.astype(jnp.float32) for a in [block(high)] + arrived))]
    another operation x323 -> x5, local copies, waits for them, and re-layouts: 144 us -> 0.28 us  [the longest x3 0.18 us: gather_high(): jnp.stack(line)]
    pallas_call x0 -> x5, Pallas kernels: none -> 133 us  [the longest x2 52.1 us: scan_ends(): pl.pallas_call(functools.partial(ends_kernel, first, reverse, states, ste...]
  transfers between devices with their start and end apart: 11 -> 61, of which waited for: 9 -> 25; matrix products, arithmetic and copies ran while one was open for 7% -> 14% of each run, Pallas kernels for 0% -> 21%
where the time goes in v1:
time: 549 us; the launch traced here: 540 us
  waiting for transfers between devices  187 us (34%)
  Pallas kernels  133 us (24%)
  starting transfers between devices  97.4 us (18%)
  local copies, waits for them, and re-layouts  51.2 us (9%)
  other arithmetic  43.4 us (8%)
  matrix products  24.4 us (4%)
    ppermute x31, waiting for transfers between devices, swap_low(): return lax.ppermute(value, 'seq', [(s, s ^ k) for s in range(count)])  94.3 us
    ppermute x21, waiting for transfers between devices, turn_high(): lax.ppermute(value, 'seq', [(s, (s + split * k) % count) for s in range(c...  68.4 us
    ppermute x21, starting transfers between devices, turn_high(): lax.ppermute(value, 'seq', [(s, (s + split * k) % count) for s in range(c...  54.2 us
    pallas_call x2, Pallas kernels, scan_ends(): pl.pallas_call(functools.partial(ends_kernel, first, reverse, states, ste...  52.1 us
    pallas_call x1, Pallas kernels, scan_backward(): pl.pallas_call(functools.partial(backward_kernel, first_in, first_out, st...  43.3 us
    ppermute x31, starting transfers between devices, swap_low(): return lax.ppermute(value, 'seq', [(s, s ^ k) for s in range(count)])  37 us
    ppermute x2, waiting for transfers between devices, from_high(): return lax.ppermute(value, 'seq', pairs)  24.4 us
    pallas_call x1, Pallas kernels, run_experts(): pl.pallas_call(functools.partial(experts_kernel, expert_count), grid=(blo...  20.6 us
  transfers between devices with their start and end apart: 61, of which 25 were waited for; matrix products, arithmetic and copies ran while one was open for 14% of the time, Pallas kernels for 21%

profile of v1, /device:TPU:0, one launch (start us, length us, event | category | flops | bytes accessed | tf_op | source)
XLA Modules:
  0.0 539.7 jit_solution(16344746221672183754)
XLA Ops:
  5.9 5.1 collective-permute-start
  19.5 6.8 %collective-permute-done.4 = bf16[16,1152]{1,0:T(8,128)(2,1)S(1)} collective-permute-done((bf16[16,1152]{1,0:T(8,128)(2,1)S(1)}, bf16[16,1152]{1,0:T(8,128)(2,1)S(1)}, u32[]{:S(2)}, u32[]{:S(2)}) %collective-permute-start.4) | collective-permute-done | bytes 36896 | tf_op jit(solution)/shard_map/ppermute | solution.py:429
  30.6 7.7 %collective-permute-done.5 = bf16[144,1152]{1,0:T(8,128)(2,1)S(1)} collective-permute-done((bf16[144,1152]{1,0:T(8,128)(2,1)S(1)}, bf16[144,1152]{1,0:T(8,128)(2,1)S(1)}, u32[]{:S(2)}, u32[]{:S(2)}) %collective-permute-start.5) | collective-permute-done | bytes 331808 | tf_op jit(solution)/shard_map/ppermute | solution.py:418
  38.3 5.0 collective-permute-done.6
  67.2 7.7 %collective-permute-start.12 = (bf16[256,1152]{1,0:T(8,128)(2,1)}, bf16[256,1152]{1,0:T(8,128)(2,1)S(1)}, u32[]{:S(2)}, u32[]{:S(2)}) collective-permute-start(bf16[256,1152]{1,0:T(8,128)(2,1)} %fusion.35), channel_id=1, source_target_pairs={{0,8},{1,9},{2,10},{3,11},{4,12},{5,13},{6,14},{7,15},{8,0},{9,1},... | collective-permute-start | bytes 1769480 | tf_op jit(solution)/shard_map/ppermute | solution.py:423
  78.3 34.2 %shard_map.263 = (f32[16,8,640]{2,1,0:T(8,128)S(1)}, f32[16,8,640]{2,1,0:T(8,128)S(1)}, f32[16,640]{1,0:T(8,128)S(1)}) custom-call(f32[512,640]{1,0:T(8,128)S(1)} %get-tuple-element.180.delta_ref, f32[512,128]{1,0:T(8,128)S(1)} %mul.481.reset_ref, f32[512,640]{1,0:T(8,128)S(1)} %get-tuple-element.179.drive_ref, f32[512,128]{1,0:T(8,128)S(1)} %add_add_fusion.2.coef_ref, ...), custom_call_target="tpu_custom_call" | custom-call | flops 1000 | bytes 1000 | tf_op jit(solution)/shard_map/pallas_call | solution.py:137
  113.5 13.3 %collective-permute-done.13 = bf16[256,1152]{1,0:T(8,128)(2,1)S(1)} collective-permute-done((bf16[256,1152]{1,0:T(8,128)(2,1)}, bf16[256,1152]{1,0:T(8,128)(2,1)S(1)}, u32[]{:S(2)}, u32[]{:S(2)}) %collective-permute-start.13) | collective-permute-done | bytes 589856 | tf_op jit(solution)/shard_map/ppermute | solution.py:423
  134.5 17.3 %shard_map.264 = (f32[512,640]{1,0:T(8,128)S(1)}, f32[16,8,640]{2,1,0:T(8,128)S(1)}, f32[5,64,16,8,128]{4,3,2,1,0:T(8,128)}) custom-call(f32[512,640]{1,0:T(8,128)S(1)} %get-tuple-element.180.delta_ref, f32[512,128]{1,0:T(8,128)S(1)} %mul.481.reset_ref, f32[512,640]{1,0:T(8,128)S(1)} %get-tuple-element.179.drive_ref, f32[512,128]{1,0:T(8,128)S(1)} %add_add_fusion.2.coef_ref, ...), custom_call_target="tpu_custom_call" | custom-call | flops 1000 | bytes 1000 | tf_op jit(solution)/shard_map/pallas_call | solution.py:197
  153.5 33.2 %collective-permute-done.19 = bf16[288,1152]{1,0:T(8,128)(2,1)S(1)} collective-permute-done((bf16[288,1152]{1,0:T(8,128)(2,1)}, bf16[288,1152]{1,0:T(8,128)(2,1)S(1)}, u32[]{:S(2)}, u32[]{:S(2)}) %collective-permute-start.19) | collective-permute-done | bytes 663584 | tf_op jit(solution)/shard_map/ppermute | solution.py:423
  204.2 6.2 %collective-permute-done.15 = bf16[128,1152]{1,0:T(8,128)(2,1)S(1)} collective-permute-done((bf16[128,1152]{1,0:T(8,128)(2,1)S(1)}, bf16[128,1152]{1,0:T(8,128)(2,1)S(1)}, u32[]{:S(2)}, u32[]{:S(2)}) %collective-permute-start.15) | collective-permute-done | bytes 294944 | tf_op jit(solution)/shard_map/ppermute | solution.py:418
  226.9 5.9 %collective-permute-done.22 = bf16[128,1152]{1,0:T(8,128)(2,1)S(1)} collective-permute-done((bf16[128,1152]{1,0:T(8,128)(2,1)S(1)}, bf16[128,1152]{1,0:T(8,128)(2,1)S(1)}, u32[]{:S(2)}, u32[]{:S(2)}) %collective-permute-start.22) | collective-permute-done | bytes 294944 | tf_op jit(solution)/shard_map/ppermute | solution.py:418
  237.8 20.6 %shard_map.265 = (bf16[512,2304]{1,0:T(8,128)(2,1)}, bf16[8,384,1152]{2,1,0:T(8,128)(2,1)}) custom-call(bf16[512,1152]{1,0:T(8,128)(2,1)} %copy-done.29, bf16[512,1152]{1,0:T(8,128)(2,1)} %multiply_convert_fusion.routed_ref, f32[512,128]{1,0:T(8,128)} %maximum_convert_fusion.route_ref, bf16[8,96,1152]{2,1,0:T(8,128)(2,1)} %slice.249.refs_0_, ...), custom_call_target="tpu_custom_call" | custom-call | flops 1000 | bytes 1000 | tf_op jit(solution)/shard_map/pallas_call | solution.py:371
  268.5 11.8 %collective-permute-done.28 = bf16[128,2304]{1,0:T(8,128)(2,1)S(1)} collective-permute-done((bf16[128,2304]{1,0:T(8,128)(2,1)S(1)}, bf16[128,2304]{1,0:T(8,128)(2,1)S(1)}, u32[]{:S(2)}, u32[]{:S(2)}) %collective-permute-start.28) | collective-permute-done | bytes 589856 | tf_op jit(solution)/shard_map/ppermute | solution.py:418
  280.3 12.4 %collective-permute-done.29 = bf16[128,2304]{1,0:T(8,128)(2,1)S(1)} collective-permute-done((bf16[128,2304]{1,0:T(8,128)(2,1)S(1)}, bf16[128,2304]{1,0:T(8,128)(2,1)S(1)}, u32[]{:S(2)}, u32[]{:S(2)}) %collective-permute-start.29) | collective-permute-done | bytes 589856 | tf_op jit(solution)/shard_map/ppermute | solution.py:418
  325.4 17.9 %shard_map.266 = (f32[16,8,640]{2,1,0:T(8,128)S(1)}, f32[16,8,640]{2,1,0:T(8,128)S(1)}, f32[16,640]{1,0:T(8,128)S(1)}) custom-call(f32[512,640]{1,0:T(8,128)S(1)} %get-tuple-element.180.delta_ref, f32[512,128]{1,0:T(8,128)S(1)} %mul.481.reset_ref, f32[512,640]{1,0:T(8,128)S(1)} %get-tuple-element.141.drive_ref.dy_ref, ...), custom_call_target="tpu_custom_call" | custom-call | flops 1000 | bytes 1000 | tf_op jit(solution)/shard_map/pallas_call | solution.py:137
  345.4 43.3 %shard_map.267 = (f32[512,640]{1,0:T(8,128)}, f32[512,640]{1,0:T(8,128)}, f32[16,640]{1,0:T(8,128)}, f32[64,128]{1,0:T(8,128)}, f32[64,128]{1,0:T(8,128)}) custom-call(f32[512,640]{1,0:T(8,128)} %copy-done.2, f32[512,128]{1,0:T(8,128)} %copy-done.6, f32[512,640]{1,0:T(8,128)} %copy-done.3, f32[512,640]{1,0:T(8,128)} %copy-done.7, f32[512,128]{1,0:T(8,128)} %copy-done.4, ...), custom_call_target="tpu_custom_call" | custom-call | flops 1000 | bytes 1000 | tf_op jit(solution)/shard_map/pallas_call | solution.py:294
  424.4 17.7 %collective-permute-done.38 = f32[3,640]{1,0:T(4,128)S(1)} collective-permute-done((f32[3,640]{1,0:T(4,128)S(1)}, f32[3,640]{1,0:T(4,128)S(1)}, u32[]{:S(2)}, u32[]{:S(2)}) %collective-permute-start.38) | collective-permute-done | bytes 7712 | tf_op jit(solution)/shard_map/ppermute | solution.py:429
  454.9 6.0 %collective-permute-done.43 = bf16[128,1152]{1,0:T(8,128)(2,1)S(1)} collective-permute-done((bf16[128,1152]{1,0:T(8,128)(2,1)S(1)}, bf16[128,1152]{1,0:T(8,128)(2,1)S(1)}, u32[]{:S(2)}, u32[]{:S(2)}) %collective-permute-start.43) | collective-permute-done | bytes 294944 | tf_op jit(solution)/shard_map/ppermute | solution.py:418
  460.9 5.6 %collective-permute-done.44 = bf16[128,1152]{1,0:T(8,128)(2,1)S(1)} collective-permute-done((bf16[128,1152]{1,0:T(8,128)(2,1)S(1)}, bf16[128,1152]{1,0:T(8,128)(2,1)S(1)}, u32[]{:S(2)}, u32[]{:S(2)}) %collective-permute-start.44) | collective-permute-done | bytes 294944 | tf_op jit(solution)/shard_map/ppermute | solution.py:418
  467.0 14.1 %collective-permute-start.55 = (bf16[80,2304]{1,0:T(8,128)(2,1)S(1)}, bf16[80,2304]{1,0:T(8,128)(2,1)S(1)}, u32[]{:S(2)}, u32[]{:S(2)}) collective-permute-start(bf16[80,2304]{1,0:T(8,128)(2,1)S(1)} %get-tuple-element.164), channel_id=1, source_target_pairs={{0,4},{1,5},{2,6},{3,7},{4,8},{5,9},{6,10},{7,11},{8,12},{9,13},{1... | collective-permute-start | bytes 1105928 | tf_op jit(solution)/shard_map/ppermute | solution.py:423
  491.8 14.1 %collective-permute-done.49 = f32[4,1152]{1,0:T(4,128)S(1)} collective-permute-done((f32[4,1152]{1,0:T(4,128)S(1)}, f32[4,1152]{1,0:T(4,128)S(1)}, u32[]{:S(2)}, u32[]{:S(2)}) %collective-permute-start.49) | collective-permute-done | bytes 18464 | tf_op jit(solution)/shard_map/ppermute | solution.py:418
  507.2 7.2 %collective-permute-done.56 = bf16[80,2304]{1,0:T(8,128)(2,1)S(1)} collective-permute-done((bf16[80,2304]{1,0:T(8,128)(2,1)S(1)}, bf16[80,2304]{1,0:T(8,128)(2,1)S(1)}, u32[]{:S(2)}, u32[]{:S(2)}) %collective-permute-start.56) | collective-permute-done | bytes 368672 | tf_op jit(solution)/shard_map/ppermute | solution.py:423
  520.1 5.9 %collective-permute-done.52 = bf16[80,1408]{1,0:T(8,128)(2,1)S(1)} collective-permute-done((bf16[80,1408]{1,0:T(8,128)(2,1)S(1)}, bf16[80,1408]{1,0:T(8,128)(2,1)S(1)}, u32[]{:S(2)}, u32[]{:S(2)}) %collective-permute-start.52) | collective-permute-done | bytes 225312 | tf_op jit(solution)/shard_map/ppermute | solution.py:423
  526.0 8.8 %collective-permute-done.53 = bf16[80,1408]{1,0:T(8,128)(2,1)S(1)} collective-permute-done((bf16[80,1408]{1,0:T(8,128)(2,1)S(1)}, bf16[80,1408]{1,0:T(8,128)(2,1)S(1)}, u32[]{:S(2)}, u32[]{:S(2)}) %collective-permute-start.53) | collective-permute-done | bytes 225312 | tf_op jit(solution)/shard_map/ppermute | solution.py:423
  (440 shorter events, 209.0 us)
Async XLA Ops:
  5.9 23.7 %collective-permute-start = (bf16[80,1408]{1,0:T(8,128)(2,1)S(1)}, bf16[80,1408]{1,0:T(8,128)(2,1)S(1)}, u32[]{:S(2)}, u32[]{:S(2)}) collective-permute-start(bf16[80,1408]{1,0:T(8,128)(2,1)S(1)} %pad.48), channel_id=1, source_target_pairs={{0,12},{1,13},{2,14},{3,15},{4,0},{5,1},{6,2},{7,3},{8,4},{9,5},{1... | collective-permute-start | bytes 675848 | tf_op jit(solution)/shard_map/ppermute | solution.py:423
  43.9 87.5 %collective-permute-start.24 = (bf16[128,1280]{1,0:T(8,128)(2,1)}, bf16[128,1280]{1,0:T(8,128)(2,1)}, u32[]{:S(2)}, u32[]{:S(2)}) collective-permute-start(bf16[128,1280]{1,0:T(8,128)(2,1)} %pad_maximum_fusion.12), channel_id=1, source_target_pairs={{0,3},{1,2},{2,1},{3,0},{4,7},{5,6},{6,5},{7,4},{8,11},{9,10},{10,... | collective-permute-start | bytes 983048 | tf_op jit(solution)/shard_map/ppermute | solution.py:418
  45.6 85.8 %collective-permute-start.25 = (bf16[128,1280]{1,0:T(8,128)(2,1)}, bf16[128,1280]{1,0:T(8,128)(2,1)}, u32[]{:S(2)}, u32[]{:S(2)}) collective-permute-start(bf16[128,1280]{1,0:T(8,128)(2,1)} %pad_maximum_fusion.12), channel_id=1, source_target_pairs={{0,2},{1,3},{2,0},{3,1},{4,6},{5,7},{6,4},{7,5},{8,10},{9,11},{10,... | collective-permute-start | bytes 983048 | tf_op jit(solution)/shard_map/ppermute | solution.py:418
  60.0 71.4 %collective-permute-start.26 = (bf16[128,1280]{1,0:T(8,128)(2,1)}, bf16[128,1280]{1,0:T(8,128)(2,1)}, u32[]{:S(2)}, u32[]{:S(2)}) collective-permute-start(bf16[128,1280]{1,0:T(8,128)(2,1)} %pad_maximum_fusion.12), channel_id=1, source_target_pairs={{0,1},{1,0},{2,3},{3,2},{4,5},{5,4},{6,7},{7,6},{8,9},{9,8},{10,11... | collective-permute-start | bytes 983048 | tf_op jit(solution)/shard_map/ppermute | solution.py:418
  60.9 51.6 %collective-permute-start.11 = (bf16[256,1152]{1,0:T(8,128)(2,1)}, bf16[256,1152]{1,0:T(8,128)(2,1)S(1)}, u32[]{:S(2)}, u32[]{:S(2)}) collective-permute-start(bf16[256,1152]{1,0:T(8,128)(2,1)} %fusion.35), channel_id=1, source_target_pairs={{0,12},{1,13},{2,14},{3,15},{4,0},{5,1},{6,2},{7,3},{8,4},{9,5},{1... | collective-permute-start | bytes 1769480 | tf_op jit(solution)/shard_map/ppermute | solution.py:423
  67.2 46.2 %collective-permute-start.12 = (bf16[256,1152]{1,0:T(8,128)(2,1)}, bf16[256,1152]{1,0:T(8,128)(2,1)S(1)}, u32[]{:S(2)}, u32[]{:S(2)}) collective-permute-start(bf16[256,1152]{1,0:T(8,128)(2,1)} %fusion.35), channel_id=1, source_target_pairs={{0,8},{1,9},{2,10},{3,11},{4,12},{5,13},{6,14},{7,15},{8,0},{9,1},... | collective-permute-start | bytes 1769480 | tf_op jit(solution)/shard_map/ppermute | solution.py:423
  131.3 55.3 %collective-permute-start.19 = (bf16[288,1152]{1,0:T(8,128)(2,1)}, bf16[288,1152]{1,0:T(8,128)(2,1)S(1)}, u32[]{:S(2)}, u32[]{:S(2)}) collective-permute-start(bf16[288,1152]{1,0:T(8,128)(2,1)} %pad_maximum_fusion.10), channel_id=1, source_target_pairs={{0,8},{1,9},{2,10},{3,11},{4,12},{5,13},{6,14},{7,15},{8,0},{9,1},... | collective-permute-start | bytes 1990664 | tf_op jit(solution)/shard_map/ppermute | solution.py:423
  133.6 53.2 %collective-permute-start.20 = (bf16[288,1152]{1,0:T(8,128)(2,1)}, bf16[288,1152]{1,0:T(8,128)(2,1)S(1)}, u32[]{:S(2)}, u32[]{:S(2)}) collective-permute-start(bf16[288,1152]{1,0:T(8,128)(2,1)} %pad_maximum_fusion.10), channel_id=1, source_target_pairs={{0,4},{1,5},{2,6},{3,7},{4,8},{5,9},{6,10},{7,11},{8,12},{9,13},{1... | collective-permute-start | bytes 1990664 | tf_op jit(solution)/shard_map/ppermute | solution.py:423
  134.5 54.9 %collective-permute-start.14 = (bf16[4,256,1152]{2,1,0:T(8,128)(2,1)}, bf16[4,256,1152]{2,1,0:T(8,128)(2,1)S(1)}, u32[]{:S(2)}, u32[]{:S(2)}) collective-permute-start(bf16[4,256,1152]{2,1,0:T(8,128)(2,1)} %constant_dynamic-slice_fusion.4), channel_id=1, source_target_pairs={{0,16},{16,0},{1,17},{17,1},{2,18},{18,2},{3,19},{19,3},{4,20},{20... | collective-permute-start | bytes 7077896 | tf_op jit(solution)/shard_map/ppermute | solution.py:433
  262.4 33.1 %collective-permute-start.31 = (bf16[4,384,1152]{2,1,0:T(8,128)(2,1)}, bf16[4,384,1152]{2,1,0:T(8,128)(2,1)}, u32[]{:S(2)}, u32[]{:S(2)}) collective-permute-start(bf16[4,384,1152]{2,1,0:T(8,128)(2,1)} %slice.253), channel_id=1, source_target_pairs={{0,16},{16,0},{1,17},{17,1},{2,18},{18,2},{3,19},{19,3},{4,20},{20... | collective-permute-start | bytes 10616840 | tf_op jit(solution)/shard_map/ppermute | solution.py:433
  264.7 28.1 %collective-permute-start.29 = (bf16[128,2304]{1,0:T(8,128)(2,1)S(1)}, bf16[128,2304]{1,0:T(8,128)(2,1)S(1)}, u32[]{:S(2)}, u32[]{:S(2)}) collective-permute-start(bf16[128,2304]{1,0:T(8,128)(2,1)S(1)} %get-tuple-element.160), channel_id=1, source_target_pairs={{0,2},{1,3},{2,0},{3,1},{4,6},{5,7},{6,4},{7,5},{8,10},{9,11},{10,... | collective-permute-start | bytes 1769480 | tf_op jit(solution)/shard_map/ppermute | solution.py:418
  266.1 26.6 %collective-permute-start.30 = (bf16[128,2304]{1,0:T(8,128)(2,1)S(1)}, bf16[128,2304]{1,0:T(8,128)(2,1)S(1)}, u32[]{:S(2)}, u32[]{:S(2)}) collective-permute-start(bf16[128,2304]{1,0:T(8,128)(2,1)S(1)} %get-tuple-element.159), channel_id=1, source_target_pairs={{0,3},{1,2},{2,1},{3,0},{4,7},{5,6},{6,5},{7,4},{8,11},{9,10},{10,... | collective-permute-start | bytes 1769480 | tf_op jit(solution)/shard_map/ppermute | solution.py:418
  307.3 89.9 %collective-permute-start.58 = (bf16[128,1152]{1,0:T(8,128)(2,1)}, bf16[128,1152]{1,0:T(8,128)(2,1)}, u32[]{:S(2)}, u32[]{:S(2)}) collective-permute-start(bf16[128,1152]{1,0:T(8,128)(2,1)} %get-tuple-element.183), channel_id=1, source_target_pairs={{0,4},{1,5},{2,6},{3,7},{4,8},{5,9},{6,10},{7,11},{8,12},{9,13},{1... | collective-permute-start | bytes 884744 | tf_op jit(solution)/shard_map/ppermute | solution.py:423
  310.0 88.8 %collective-permute-start.59 = (bf16[128,1152]{1,0:T(8,128)(2,1)}, bf16[128,1152]{1,0:T(8,128)(2,1)}, u32[]{:S(2)}, u32[]{:S(2)}) collective-permute-start(bf16[128,1152]{1,0:T(8,128)(2,1)} %get-tuple-element.185), channel_id=1, source_target_pairs={{0,8},{1,9},{2,10},{3,11},{4,12},{5,13},{6,14},{7,15},{8,0},{9,1},... | collective-permute-start | bytes 884744 | tf_op jit(solution)/shard_map/ppermute | solution.py:423
  311.8 87.0 %collective-permute-start.60 = (bf16[128,1152]{1,0:T(8,128)(2,1)}, bf16[128,1152]{1,0:T(8,128)(2,1)}, u32[]{:S(2)}, u32[]{:S(2)}) collective-permute-start(bf16[128,1152]{1,0:T(8,128)(2,1)} %get-tuple-element.184), channel_id=1, source_target_pairs={{0,12},{1,13},{2,14},{3,15},{4,0},{5,1},{6,2},{7,3},{8,4},{9,5},{1... | collective-permute-start | bytes 884744 | tf_op jit(solution)/shard_map/ppermute | solution.py:423
  398.8 45.5 %collective-permute-start.42 = (bf16[4,80,2304]{2,1,0:T(8,128)(2,1)}, bf16[4,80,2304]{2,1,0:T(8,128)(2,1)}, u32[]{:S(2)}, u32[]{:S(2)}) collective-permute-start(bf16[4,80,2304]{2,1,0:T(8,128)(2,1)} %bitcast.44), channel_id=1, source_target_pairs={{0,16},{16,0},{1,17},{17,1},{2,18},{18,2},{3,19},{19,3},{4,20},{20... | collective-permute-start | bytes 4423688 | tf_op jit(solution)/shard_map/ppermute | solution.py:433
  398.9 43.4 %collective-permute-start.39 = (bf16[256,1152]{1,0:T(8,128)(2,1)}, bf16[256,1152]{1,0:T(8,128)(2,1)}, u32[]{:S(2)}, u32[]{:S(2)}) collective-permute-start(bf16[256,1152]{1,0:T(8,128)(2,1)} %get-tuple-element.155), channel_id=1, source_target_pairs={{0,4},{1,5},{2,6},{3,7},{4,8},{5,9},{6,10},{7,11},{8,12},{9,13},{1... | collective-permute-start | bytes 1769480 | tf_op jit(solution)/shard_map/ppermute | solution.py:423
  405.8 36.4 %collective-permute-start.40 = (bf16[256,1152]{1,0:T(8,128)(2,1)}, bf16[256,1152]{1,0:T(8,128)(2,1)}, u32[]{:S(2)}, u32[]{:S(2)}) collective-permute-start(bf16[256,1152]{1,0:T(8,128)(2,1)} %get-tuple-element.157), channel_id=1, source_target_pairs={{0,8},{1,9},{2,10},{3,11},{4,12},{5,13},{6,14},{7,15},{8,0},{9,1},... | collective-permute-start | bytes 1769480 | tf_op jit(solution)/shard_map/ppermute | solution.py:423
  409.1 33.2 %collective-permute-start.41 = (bf16[256,1152]{1,0:T(8,128)(2,1)}, bf16[256,1152]{1,0:T(8,128)(2,1)}, u32[]{:S(2)}, u32[]{:S(2)}) collective-permute-start(bf16[256,1152]{1,0:T(8,128)(2,1)} %get-tuple-element.156), channel_id=1, source_target_pairs={{0,12},{1,13},{2,14},{3,15},{4,0},{5,1},{6,2},{7,3},{8,4},{9,5},{1... | collective-permute-start | bytes 1769480 | tf_op jit(solution)/shard_map/ppermute | solution.py:423
  416.5 25.6 %collective-permute-start.38 = (f32[3,640]{1,0:T(4,128)S(1)}, f32[3,640]{1,0:T(4,128)S(1)}, u32[]{:S(2)}, u32[]{:S(2)}) collective-permute-start(f32[3,640]{1,0:T(4,128)S(1)} %pad_add_fusion.1), channel_id=1, source_target_pairs={{4,0},{5,1},{6,2},{7,3},{8,4},{9,5},{10,6},{11,7},{12,8},{13,9},{1... | collective-permute-start | bytes 23048 | tf_op jit(solution)/shard_map/ppermute | solution.py:429
  454.8 60.5 %collective-permute-start.51 = (bf16[4,80,1408]{2,1,0:T(8,128)(2,1)S(1)}, bf16[4,80,1408]{2,1,0:T(8,128)(2,1)S(1)}, u32[]{:S(2)}, u32[]{:S(2)}) collective-permute-start(bf16[4,80,1408]{2,1,0:T(8,128)(2,1)S(1)} %bitcast.179), channel_id=1, source_target_pairs={{0,16},{16,0},{1,17},{17,1},{2,18},{18,2},{3,19},{19,3},{4,20},{20... | collective-permute-start | bytes 2703368 | tf_op jit(solution)/shard_map/ppermute | solution.py:433
  467.0 40.1 %collective-permute-start.55 = (bf16[80,2304]{1,0:T(8,128)(2,1)S(1)}, bf16[80,2304]{1,0:T(8,128)(2,1)S(1)}, u32[]{:S(2)}, u32[]{:S(2)}) collective-permute-start(bf16[80,2304]{1,0:T(8,128)(2,1)S(1)} %get-tuple-element.164), channel_id=1, source_target_pairs={{0,4},{1,5},{2,6},{3,7},{4,8},{5,9},{6,10},{7,11},{8,12},{9,13},{1... | collective-permute-start | bytes 1105928 | tf_op jit(solution)/shard_map/ppermute | solution.py:423
  481.2 33.2 %collective-permute-start.57 = (bf16[80,2304]{1,0:T(8,128)(2,1)S(1)}, bf16[80,2304]{1,0:T(8,128)(2,1)S(1)}, u32[]{:S(2)}, u32[]{:S(2)}) collective-permute-start(bf16[80,2304]{1,0:T(8,128)(2,1)S(1)} %get-tuple-element.165), channel_id=1, source_target_pairs={{0,12},{1,13},{2,14},{3,15},{4,0},{5,1},{6,2},{7,3},{8,4},{9,5},{1... | collective-permute-start | bytes 1105928 | tf_op jit(solution)/shard_map/ppermute | solution.py:423
  483.3 31.0 %collective-permute-start.56 = (bf16[80,2304]{1,0:T(8,128)(2,1)S(1)}, bf16[80,2304]{1,0:T(8,128)(2,1)S(1)}, u32[]{:S(2)}, u32[]{:S(2)}) collective-permute-start(bf16[80,2304]{1,0:T(8,128)(2,1)S(1)} %get-tuple-element.166), channel_id=1, source_target_pairs={{0,8},{1,9},{2,10},{3,11},{4,12},{5,13},{6,14},{7,15},{8,0},{9,1},... | collective-permute-start | bytes 1105928 | tf_op jit(solution)/shard_map/ppermute | solution.py:423
  (118 other events, 2522.3 us)

commit v2 on v1

--- a/solution.py
+++ b/solution.py
@@ -389,6 +389,1268 @@
     )(second, routed, route_lanes, *[w for w, _ in parts])
 
 
+def kernel_place():
+    place = lax.axis_index("seq")
+    return lax.axis_index("grp"), place // split, place % split
+
+
+def remote(src, dst, send_sem, arrive_sem, core, high, low):
+    return pltpu.make_async_remote_copy(
+        src_ref=src,
+        dst_ref=dst,
+        send_sem=send_sem,
+        recv_sem=arrive_sem,
+        device_id=(core, high * split + low),
+        device_id_type=pl.DeviceIdType.MESH,
+    )
+
+
+def greet_all():
+    core, high, low = kernel_place()
+    barrier = pltpu.get_barrier_semaphore()
+    others = [(core, lax.rem(high + k, split), low) for k in range(1, split)]
+    others += [(core, high, lax.rem(low + k, split)) for k in range(1, split)]
+    others += [(1 - core, high, low)]
+    for c, h, l in others:
+        pl.semaphore_signal(
+            barrier, inc=1, device_id=(c, h * split + l), device_id_type=pl.DeviceIdType.MESH
+        )
+    return len(others)
+
+
+def plane_copies(src_of, dst, sems, slot_by_sender):
+    core, high, low = kernel_place()
+    copies = []
+    for k in range(1, split):
+        to = lax.rem(low + k, split)
+        slot = low if slot_by_sender else k - 1
+        copies.append(
+            remote(src_of(to, k), dst.at[slot], sems.at[0, k - 1], sems.at[1, k - 1], core, high, to)
+        )
+    return copies
+
+
+def line_copies(src, dst_of, sems):
+    core, high, low = kernel_place()
+    return [
+        remote(
+            src, dst_of(high), sems.at[0, k - 1], sems.at[1, k - 1], core, lax.rem(high + k, split), low
+        )
+        for k in range(1, split)
+    ]
+
+
+def line_arrived(src, dst_of, sems, k):
+    core, high, low = kernel_place()
+    at = lax.rem(high + split - k, split)
+    remote(src, dst_of(at), sems.at[0, k - 1], sems.at[1, k - 1], core, high, low).wait_recv()
+
+
+def core_copy(dst_of, sems, k):
+    core, high, low = kernel_place()
+    at = lax.rem(high + split - k, split)
+    return remote(dst_of(at), dst_of(split + at), sems.at[0, k], sems.at[1, k], 1 - core, high, low)
+
+
+def softplus_of(value):
+    return jnp.maximum(value, 0.0) + jnp.log1p(jnp.exp(-jnp.abs(value)))
+
+
+def sigmoid_of(value):
+    return 1.0 / (1.0 + jnp.exp(-value))
+
+
+def row_loop(count, size, body):
+    def one(i, _):
+        body(pl.multiple_of(i * size, size))
+        return 0
+
+    lax.fori_loop(0, count // size, one, 0)
+
+
+def scan_one_way(j, first_sub, reverse, states, steps, step_ref, reset_ref, drive_ref, spread_ref, rates):
+    def one(turn, carry):
+        s = steps - 1 - turn if reverse else turn
+        total, held = carry
+        step = step_ref[j, pl.ds(s, subs, stride=steps), :] + reset_ref[pl.ds(s, subs, stride=steps), :]
+        drive = drive_ref[j, pl.ds(s, subs, stride=steps), :]
+        after_step = []
+        for n in range(states):
+            factor = jnp.exp2(step * rates[n])
+            if reverse:
+                after_step.append(factor * (held[n] + spread_ref[s, n] * drive))
+            else:
+                after_step.append(factor * held[n] + spread_ref[s, n] * drive)
+        return total + step, tuple(after_step)
+
+    zero = jnp.zeros((subs, lanes), jnp.float32)
+    total, held = lax.fori_loop(0, steps, one, (zero, (zero,) * states), unroll=2)
+    return [chain_rows(jnp.exp2(total * rates[n]), held[n], reverse) for n in range(states)]
+
+
+def chain_enter(arrive_ref, j, states, reverse):
+    _, high, _ = kernel_place()
+    total = jnp.zeros((states, lanes), jnp.float32)
+    for k in range(split - 1, 0, -1):
+        piece = arrive_ref[k - 1, j]
+        has = high + k < split if reverse else high >= k
+        total = jnp.where(has, piece[states:] + piece[:states] * total, 0.0)
+    return total
+
+
+def tile_rates(rows_ref, j, states):
+    decay = -jnp.exp(rows_ref[j, alog_row : alog_row + states, :])
+    return decay
+
+
+def ends_copies(send_ref, arrive_ref, sems, j, reverse):
+    core, high, low = kernel_place()
+    copies = []
+    for k in range(1, split):
+        to = lax.rem(high + split - k, split) if reverse else lax.rem(high + k, split)
+        copies.append(
+            remote(
+                send_ref.at[j],
+                arrive_ref.at[k - 1, j],
+                sems.at[0, k - 1, j],
+                sems.at[1, k - 1, j],
+                core,
+                to,
+                low,
+            )
+        )
+    return copies
+
+
+alog_row = 8
+bias_row = 4
+skip_row = 5
+early_hidden = 96
+
+
+def mixer_kernel(
+    dt_rank, states, tap_count,
+    tokens_ref, gains_ref, lengths_ref, a_ref, b_ref, c_ref, g_ref,
+    first_ref, gate_ref, hidden_ref, normed_ref, edge_ref, routed_ref, input_ref, coef_ref,
+    step_ref, z_ref, y_ref, gated_ref, start_ref, resid_ref, second_ref, rows_ref,
+    in_ref, out_ref, drive_ref, reset_ref, mixed_ref, partial_ref, arrive_ref, coef_send_ref,
+    coef_arrive_ref, send_ref, ends_ref, grow_ref, state_ref,
+    a_sems, b_sems, c_sems, d_sems, a_core, b_core, c_core, d_core, token_sems, route_sems,
+    second_sems, coef_sems, sum_sems, edge_send, edge_arrive, ends_sems, local_sems,
+):
+    core, high, low = kernel_place()
+    own_rows, model_width = tokens_ref.shape
+    row_count = own_rows * split
+    steps = row_count // subs
+    tiles = step_ref.shape[0]
+    width = tiles * lanes
+    edge = edge_ref.shape[0]
+    first_b, first_c = dt_rank, dt_rank + states
+    greeted = greet_all()
+
+    def edge_copy(l):
+        return remote(
+            normed_ref.at[low, pl.ds(own_rows - edge, edge)],
+            edge_ref,
+            edge_send.at[l],
+            edge_arrive,
+            core,
+            lax.rem(high + 1, split),
+            l,
+        )
+
+    barrier = pltpu.get_barrier_semaphore()
+    for k in range(1, split):
+        pl.semaphore_signal(
+            barrier,
+            inc=1,
+            device_id=(core, lax.rem(high + split - 1, split) * split + lax.rem(low + k, split)),
+            device_id_type=pl.DeviceIdType.MESH,
+        )
+    greeted += split - 1
+    tokens = tokens_ref[...].astype(jnp.float32)
+    normed_ref[low] = low_bits(norm_rows(tokens, gains_ref[0:1, :]))
+    local = [
+        pltpu.make_async_copy(a_ref, first_ref.at[high], local_sems.at[0]),
+        pltpu.make_async_copy(b_ref, gate_ref.at[high], local_sems.at[1]),
+        pltpu.make_async_copy(c_ref, hidden_ref.at[high], local_sems.at[2]),
+        pltpu.make_async_copy(g_ref, routed_ref.at[low], local_sems.at[3]),
+    ]
+    for copy in local:
+        copy.start()
+    pl.semaphore_wait(barrier, greeted)
+
+    @pl.when((low == split - 1) & (high < split - 1))
+    def _():
+        for l in range(split):
+            edge_copy(l).start()
+
+    hidden_count = c_ref.shape[0]
+    c_src = c_ref.at[pl.ds(0, early_hidden)]
+    d_src = c_ref.at[pl.ds(early_hidden, hidden_count - early_hidden)]
+
+    def a_dst(at):
+        return first_ref.at[at]
+
+    def b_dst(at):
+        return gate_ref.at[at]
+
+    def c_dst(at):
+        return hidden_ref.at[at, pl.ds(0, early_hidden)]
+
+    def d_dst(at):
+        return hidden_ref.at[at, pl.ds(early_hidden, hidden_count - early_hidden)]
+
+    token_copies = plane_copies(lambda to, k: normed_ref.at[low], normed_ref, token_sems, True)
+    a_copies = line_copies(a_ref, a_dst, a_sems)
+    b_copies = line_copies(b_ref, b_dst, b_sems)
+    c_copies = line_copies(c_src, c_dst, c_sems)
+    d_copies = line_copies(d_src, d_dst, d_sems)
+    route_copies = plane_copies(lambda to, k: g_ref, routed_ref, route_sems, True)
+    for copy in token_copies + a_copies + b_copies + c_copies + route_copies:
+        copy.start()
+    for copy in local:
+        copy.wait()
+    core_copies = [core_copy(a_dst, a_core, 0), core_copy(b_dst, b_core, 0)]
+    core_copies += [core_copy(c_dst, c_core, 0), core_copy(d_dst, d_core, 0)]
+    for copy in core_copies:
+        copy.start()
+
+    first_len = lengths_ref[0, 0]
+
+    def offsets(at, rows):
+        place = high * row_count + at + lax.broadcasted_iota(jnp.int32, (rows, lanes), 0)
+        return jnp.where(place < first_len, place, place - first_len)
+
+    def fill_reset(at):
+        reset_ref[pl.ds(at, 64), :] = jnp.where(offsets(at, 64) == 0, 1e30, 0.0)
+
+    row_loop(row_count, 64, fill_reset)
+
+    @pl.when(high == 0)
+    def _():
+        edge_ref[...] = jnp.zeros_like(edge_ref)
+
+    for k in range(1, split):
+        line_arrived(a_ref, a_dst, a_sems, k)
+        copy = core_copy(a_dst, a_core, k)
+        copy.start()
+        core_copies.append(copy)
+    for copy in token_copies:
+        copy.wait()
+
+    @pl.when(high > 0)
+    def _():
+        edge_copy(0).wait_recv()
+
+    @pl.when((low == split - 1) & (high < split - 1))
+    def _():
+        for l in range(split):
+            edge_copy(l).wait_send()
+
+    for k in range(split):
+        core_copy(a_dst, a_core, k).wait_recv()
+
+    weights = first_ref[:, :, :model_width].reshape(width, model_width)
+    input_ref[:edge, :] = low_bits(matmul_nt(edge_ref[...], weights)).astype(jnp.float32)
+    for l in range(split):
+        block = low_bits(matmul_nt(normed_ref[l], weights)).astype(jnp.float32)
+        input_ref[edge + l * own_rows : edge + (l + 1) * own_rows, :] = block
+    small = first_ref[:, :, model_width + 2 * lanes :].reshape(width, lanes).astype(jnp.float32)
+    for j in range(tiles):
+        rows_ref[j] = small[j * lanes : (j + 1) * lanes].T
+
+    def convolve(at):
+        offset = offsets(at, 32)
+        for j in range(tiles):
+            span = input_ref[pl.ds(at, 32 + edge), j * lanes : (j + 1) * lanes]
+            conv_sum = jnp.zeros((32, lanes), jnp.float32)
+            for k in range(tap_count):
+                shift = edge - (tap_count - 1) + k
+                term = rows_ref[j, k : k + 1, :] * span[shift : shift + 32]
+                conv_sum = conv_sum + jnp.where(offset >= tap_count - 1 - k, term, 0.0)
+            mixed_ref[pl.ds(at, 32), j * lanes : (j + 1) * lanes] = low_bits(
+                conv_sum * sigmoid_of(conv_sum)
+            )
+
+    row_loop(row_count, 32, convolve)
+
+    x_full = first_ref[:, :, model_width : model_width + lanes].reshape(width, lanes)
+    part = matmul(mixed_ref[...], x_full)
+    coef_ref[...] = part
+    coef_send_ref[...] = low_bits(part)
+    coef_copies = plane_copies(lambda to, k: coef_send_ref, coef_arrive_ref, coef_sems, False)
+    for copy in coef_copies:
+        copy.start()
+    for copy in coef_copies:
+        copy.wait()
+    total = coef_ref[...]
+    for k in range(1, split):
+        total = total + coef_arrive_ref[k - 1].astype(jnp.float32)
+    coef_ref[...] = total
+    dt_full = first_ref[:, :, model_width + lanes : model_width + 2 * lanes].reshape(width, lanes)
+
+    def step_sizes(at):
+        pre = matmul_nt(low_bits(coef_ref[pl.ds(at, 128), :]), dt_full)
+        for j in range(tiles):
+            cols = slice(j * lanes, (j + 1) * lanes)
+            step = softplus_of(pre[:, cols] + rows_ref[j, bias_row : bias_row + 1, :])
+            step_ref[j, pl.ds(at, 128), :] = step
+            drive_ref[j, pl.ds(at, 128), :] = step * mixed_ref[pl.ds(at, 128), cols].astype(
+                jnp.float32
+            )
+
+    row_loop(row_count, 128, step_sizes)
+    spread(coef_ref, first_b, in_ref, steps, states)
+
+    def rates_of(j):
+        values = -jnp.exp(rows_ref[j, alog_row : alog_row + states, :]) * log2e
+        return [jnp.broadcast_to(values[n : n + 1, :], (subs, lanes)) for n in range(states)]
+
+    def ends_of(j, _):
+        found = scan_one_way(
+            j, None, False, states, steps, step_ref, reset_ref, drive_ref, in_ref, rates_of(j)
+        )
+        for n, (grow, state) in enumerate(found):
+            grow_ref[j, n] = grow
+            state_ref[j, n] = state
+            send_ref[j, n : n + 1] = grow[subs - 1 :]
+            send_ref[j, states + n : states + n + 1] = state[subs - 1 :]
+        for copy in ends_copies(send_ref, ends_ref, ends_sems, j, False):
+            copy.start()
+        return 0
+
+    lax.fori_loop(0, tiles, ends_of, 0)
+    for copy in d_copies:
+        copy.start()
+    spread(coef_ref, first_c, out_ref, steps, states)
+    for k in range(1, split):
+        line_arrived(b_ref, b_dst, b_sems, k)
+        copy = core_copy(b_dst, b_core, k)
+        copy.start()
+        core_copies.append(copy)
+    row = lax.broadcasted_iota(jnp.int32, (subs, lanes), 0)
+
+    def forward_of(j, _):
+        for copy in ends_copies(send_ref, ends_ref, ends_sems, j, False):
+            copy.wait()
+        enter = chain_enter(ends_ref, j, states, False)
+        rates = rates_of(j)
+        held = []
+        for n in range(states):
+            near_grow = jnp.where(row >= 1, pltpu.roll(grow_ref[j, n], 1, 0), 1.0)
+            near_state = jnp.where(row >= 1, pltpu.roll(state_ref[j, n], 1, 0), 0.0)
+            start = near_state + near_grow * jnp.broadcast_to(enter[n : n + 1, :], (subs, lanes))
+            start_ref[j, n] = start
+            held.append(start)
+
+        def one(s, held):
+            step = step_ref[j, pl.ds(s, subs, stride=steps), :]
+            step = step + reset_ref[pl.ds(s, subs, stride=steps), :]
+            drive = drive_ref[j, pl.ds(s, subs, stride=steps), :]
+            now_all = []
+            y = jnp.zeros((subs, lanes), jnp.float32)
+            for n in range(states):
+                now = jnp.exp2(step * rates[n]) * held[n] + in_ref[s, n] * drive
+                y = y + out_ref[s, n] * now
+                now_all.append(now)
+            y_ref[j, pl.ds(s, subs, stride=steps), :] = y
+            return tuple(now_all)
+
+        lax.fori_loop(0, steps, one, tuple(held), unroll=2)
+        return 0
+
+    lax.fori_loop(0, tiles, forward_of, 0)
+
+    for k in range(split):
+        core_copy(b_dst, b_core, k).wait_recv()
+    channel_rows = width // (2 * split)
+    second_in = gate_ref[:, :channel_rows].reshape(width, model_width)
+    for l in range(split):
+        z_block = matmul_nt(normed_ref[l], second_in)
+        rows = slice(l * own_rows, (l + 1) * own_rows)
+        for j in range(tiles):
+            z_ref[j, rows, :] = z_block[:, j * lanes : (j + 1) * lanes]
+
+    def gate(at):
+        for j in range(tiles):
+            cols = slice(j * lanes, (j + 1) * lanes)
+            mixed = mixed_ref[pl.ds(at, 32), cols].astype(jnp.float32)
+            y = y_ref[j, pl.ds(at, 32), :] + rows_ref[j, skip_row : skip_row + 1, :] * mixed
+            y_ref[j, pl.ds(at, 32), :] = y
+            z = z_ref[j, pl.ds(at, 32), :]
+            gated_ref[pl.ds(at, 32), cols] = low_bits(y * z * sigmoid_of(z))
+
+    row_loop(row_count, 32, gate)
+    out_full = gate_ref[:, channel_rows:].reshape(width, model_width)
+
+    def out_block(l):
+        at = pl.multiple_of(l * own_rows, own_rows)
+        return matmul(gated_ref[pl.ds(at, own_rows), :], out_full)
+
+    sum_copies = plane_copies(lambda to, k: partial_ref.at[k - 1], arrive_ref, sum_sems, False)
+    for k in range(1, split):
+        partial_ref[k - 1] = low_bits(out_block(lax.rem(low + k, split)))
+        sum_copies[k - 1].start()
+    resid = tokens_ref[...].astype(jnp.float32) + out_block(low)
+    for k in range(1, split):
+        line_arrived(c_src, c_dst, c_sems, k)
+        copy = core_copy(c_dst, c_core, k)
+        copy.start()
+        core_copies.append(copy)
+    for k in range(1, split):
+        sum_copies[k - 1].wait()
+        resid = resid + arrive_ref[k - 1].astype(jnp.float32)
+    resid_ref[...] = resid
+    second_ref[low] = low_bits(norm_rows(resid, gains_ref[1:2, :]))
+    second_copies = plane_copies(lambda to, k: second_ref.at[low], second_ref, second_sems, True)
+    for copy in second_copies:
+        copy.start()
+    for k in range(1, split):
+        line_arrived(d_src, d_dst, d_sems, k)
+        copy = core_copy(d_dst, d_core, k)
+        copy.start()
+        core_copies.append(copy)
+    for copy in second_copies + route_copies:
+        copy.wait()
+    for copy in a_copies + b_copies + c_copies + d_copies + core_copies:
+        copy.wait_send()
+    for dst_of, sems in ((c_dst, c_core), (d_dst, d_core)):
+        for k in range(split):
+            core_copy(dst_of, sems, k).wait_recv()
+
+
+def run_mixer(tokens, gains, lengths, a_part, b_part, c_part, g_part, dt_rank, states, tap_count):
+    own_rows, model_width = tokens.shape
+    row_count = own_rows * split
+    steps = row_count // subs
+    blocks = 2 * split
+    width = blocks * a_part.shape[0]
+    tiles = width // lanes
+    vmem = pl.BlockSpec(memory_space=pltpu.VMEM)
+    anywhere = pl.BlockSpec(memory_space=pl.ANY)
+    f32, bf16 = jnp.float32, jnp.bfloat16
+    tiled = (tiles, row_count, lanes)
+    outs = [
+        ((blocks,) + a_part.shape, bf16),
+        ((blocks,) + b_part.shape, bf16),
+        ((blocks,) + c_part.shape, bf16),
+        ((split, own_rows, model_width), bf16),
+        ((16, model_width), bf16),
+        ((split,) + g_part.shape, bf16),
+        ((row_count + 16, width), f32),
+        ((row_count, lanes), f32),
+        (tiled, f32),
+        (tiled, f32),
+        (tiled, f32),
+        ((row_count, width), bf16),
+        ((tiles, states, subs, lanes), f32),
+        ((own_rows, model_width), f32),
+        ((split, own_rows, model_width), bf16),
+        ((tiles, lanes, lanes), f32),
+    ]
+    spreads = pltpu.VMEM((steps, states, subs, lanes), f32)
+    dma = pltpu.SemaphoreType.DMA
+    others = split - 1
+    return pl.pallas_call(
+        functools.partial(mixer_kernel, dt_rank, states, tap_count),
+        in_specs=[vmem, vmem, pl.BlockSpec(memory_space=pltpu.SMEM), vmem, vmem, anywhere, vmem],
+        out_specs=[anywhere if i == 2 else vmem for i in range(len(outs))],
+        out_shape=[jax.ShapeDtypeStruct(shape, kind) for shape, kind in outs],
+        scratch_shapes=[
+            spreads,
+            spreads,
+            pltpu.VMEM(tiled, f32),
+            pltpu.VMEM((row_count, lanes), f32),
+            pltpu.VMEM((row_count, width), bf16),
+            pltpu.VMEM((others, own_rows, model_width), bf16),
+            pltpu.VMEM((others, own_rows, model_width), bf16),
+            pltpu.VMEM((row_count, lanes), bf16),
+            pltpu.VMEM((others, row_count, lanes), bf16),
+            pltpu.VMEM((tiles, 2 * states, lanes), f32),
+            pltpu.VMEM((others, tiles, 2 * states, lanes), f32),
+            pltpu.VMEM((tiles, states, subs, lanes), f32),
+            pltpu.VMEM((tiles, states, subs, lanes), f32),
+        ]
+        + [dma((2, others))] * 4
+        + [dma((2, split))] * 4
+        + [dma((2, others))] * 5
+        + [dma((split,)), dma, dma((2, others, tiles)), dma((4,))],
+        compiler_params=pltpu.CompilerParams(
+            collective_id=3, has_side_effects=True, vmem_limit_bytes=60 << 20
+        ),
+        cost_estimate=pl.CostEstimate(flops=1000, bytes_accessed=1000, transcendentals=0),
+    )(tokens, gains, lengths, a_part, b_part, c_part, g_part)
+
+
+def norm_back(values, gain_row, grads):
+    scale = lax.rsqrt(jnp.mean(values * values, -1, keepdims=True) + eps_norm)
+    unit = values * scale
+    inner = grads * gain_row
+    return scale * (inner - unit * jnp.mean(inner * unit, -1, keepdims=True)), grads * unit
+
+
+def route_probs(rows, router, route_lanes, expert_count):
+    logits = matmul(rows, router)
+    lane = lax.broadcasted_iota(jnp.int32, logits.shape, 1)
+    logits = jnp.where(lane < expert_count, logits, -1e30)
+    powers = jnp.exp(logits - jnp.max(logits, -1, keepdims=True))
+    probs = powers / jnp.sum(powers, -1, keepdims=True)
+    chosen = jnp.where(lane.astype(jnp.float32) == route_lanes, 1.0, 0.0)
+    return probs, chosen, jnp.sum(probs * chosen, -1, keepdims=True)
+
+
+def scatter_copies(src_of, arrive_ref, sems):
+    core, high, low = kernel_place()
+    copies = []
+    for k in range(1, split):
+        to = lax.rem(high + k, split)
+        copies.append(
+            remote(
+                src_of(to), arrive_ref.at[k - 1], sems.at[0, k - 1], sems.at[1, k - 1], core, to, low
+            )
+        )
+    return copies
+
+
+def half_copy(src, dst, sems, h):
+    core, high, low = kernel_place()
+    return remote(src, dst, sems.at[0, h], sems.at[1, h], 1 - core, high, low)
+
+
+def fill_offsets(reset_ref, lengths_ref, row_count):
+    _, high, _ = kernel_place()
+    first_len = lengths_ref[0, 0]
+
+    def fill(at):
+        place = high * row_count + at + lax.broadcasted_iota(jnp.int32, (64, lanes), 0)
+        reset_ref[pl.ds(at, 64), :] = jnp.where((place == 0) | (place == first_len), 1e30, 0.0)
+
+    row_loop(row_count, 64, fill)
+
+
+def turn_kernel(
+    dt_rank, states, expert_count, cut,
+    second_ref, routed_ref, hidden_ref, router_ref, resid_ref, grad_ref, gains_ref, lengths_ref,
+    gate_ref, normed_ref, coef_ref, step_ref, z_ref, y_ref, gated_ref, rows_ref,
+    mixed_out_ref, d_resid_ref, small_ref, dy_ref, gz_ref, later_ref, mine_ref, early_ref,
+    gate_mine_ref,
+    grads_ref, half_ref, y_sum_ref, d_sum_ref, dg_sum_ref, gates_ref, scaled_ref, act_ref, pre_ref,
+    part_ref, arrive_ref, y_part_ref, y_arrive_ref, branch_ref, out_ref, reset_ref, send_ref,
+    ends_ref, early_arrive_ref, gate_half_ref,
+    half_sems, sum_sems, y_sems, branch_sems, early_sems, ends_sems, gate_half_sems,
+):
+    core, high, low = kernel_place()
+    _, own_rows, model_width = second_ref.shape
+    row_count = own_rows * split
+    steps = row_count // subs
+    tiles = step_ref.shape[0]
+    width = tiles * lanes
+    hidden = hidden_ref.shape[1] // (2 * expert_count)
+    channel_rows = width // (2 * split)
+    greeted = greet_all()
+    router = router_ref[...]
+
+    for l in range(split):
+        rows = slice(l * own_rows, (l + 1) * own_rows)
+        route_lanes = routed_ref[l, :, model_width:].astype(jnp.float32)
+        _, _, gate = route_probs(second_ref[l], router, route_lanes, expert_count)
+        gates_ref[rows, :] = jnp.broadcast_to(gate, (own_rows, lanes))
+        scaled_ref[rows, :] = low_bits(gate * routed_ref[l, :, :model_width].astype(jnp.float32))
+    y_sum_ref[...] = jnp.zeros_like(y_sum_ref)
+    d_sum_ref[...] = jnp.zeros_like(d_sum_ref)
+    dg_sum_ref[...] = jnp.zeros_like(dg_sum_ref)
+    per_step = 2
+    span = per_step * hidden
+    column = lax.broadcasted_iota(jnp.int32, (1, expert_count * span), 1)
+    owner = jnp.zeros_like(column)
+    for e in range(1, expert_count):
+        owner = owner + (column >= e * span).astype(jnp.int32)
+    owner = owner.astype(jnp.float32)
+
+    def blocks_of(first):
+        def rows_of(part):
+            at = part * hidden
+            return hidden_ref[pl.ds(first, per_step), at : at + hidden].reshape(span, model_width)
+
+        up = jnp.concatenate([rows_of(e) for e in range(expert_count)], 0)
+        down = jnp.concatenate([rows_of(expert_count + e) for e in range(expert_count)], 0)
+
+        def token_block(l, _):
+            at = pl.multiple_of(l * own_rows, own_rows)
+            rows = pl.ds(at, own_rows)
+            pre = matmul_nt(second_ref[l], up)
+            picked = routed_ref[l, :, model_width : model_width + 1].astype(jnp.float32) == owner
+            half = 0.5 + 0.5 * lax.erf(pre * (0.5**0.5))
+            bell = jnp.exp(-0.5 * pre * pre) * (1.0 / (2.0 * math.pi) ** 0.5)
+            act = low_bits(jnp.where(picked, pre * half, 0.0))
+            d_raw = matmul_nt(routed_ref[l, :, :model_width], down)
+            weighted = act.astype(jnp.float32) * d_raw
+            dg_sum_ref[rows, :] += sum(
+                weighted[:, c : c + lanes] for c in range(0, expert_count * span, lanes)
+            )
+            d_pre = jnp.where(picked, gates_ref[rows, :1] * d_raw * (half + pre * bell), 0.0)
+            d_pre = low_bits(d_pre)
+            y_sum_ref[rows, :] += matmul(act, down)
+            d_sum_ref[rows, :] += matmul(d_pre, up)
+            act_ref[rows, :] = act
+            pre_ref[rows, :] = d_pre
+            return 0
+
+        lax.fori_loop(0, split, token_block, 0)
+        second = second_ref[...].reshape(row_count, model_width)
+        for e in range(expert_count):
+            cols = slice(e * span, (e + 1) * span)
+            up_grad = low_bits(matmul_tn(pre_ref[:, cols], second))
+            down_grad = low_bits(matmul_tn(act_ref[:, cols], scaled_ref[...]))
+            for b in range(per_step):
+                piece = slice(b * hidden, (b + 1) * hidden)
+                grads_ref[first + b, e * hidden : (e + 1) * hidden] = up_grad[piece]
+                to = (expert_count + e) * hidden
+                grads_ref[first + b, to : to + hidden] = down_grad[piece]
+
+    lax.fori_loop(0, split // per_step, lambda i, _: (blocks_of(split + per_step * i), 0)[1], 0)
+    pl.semaphore_wait(pltpu.get_barrier_semaphore(), greeted)
+    half_copies = [
+        half_copy(grads_ref.at[split + h], half_ref.at[h], half_sems, h) for h in range(split)
+    ]
+    for copy in half_copies:
+        copy.start()
+    lax.fori_loop(0, split // per_step, lambda i, _: (blocks_of(per_step * i), 0)[1], 0)
+
+    sum_copies = plane_copies(lambda to, k: part_ref.at[k - 1], arrive_ref, sum_sems, False)
+    y_copies = plane_copies(lambda to, k: y_part_ref.at[k - 1], y_arrive_ref, y_sems, False)
+    for k in range(1, split):
+        to = pl.ds(pl.multiple_of(lax.rem(low + k, split) * own_rows, own_rows), own_rows)
+        part_ref[k - 1, :, :model_width] = low_bits(d_sum_ref[to, :])
+        part_ref[k - 1, :, model_width:] = low_bits(dg_sum_ref[to, :])
+        sum_copies[k - 1].start()
+        y_part_ref[k - 1] = low_bits(y_sum_ref[to, :])
+
+    for h in range(split):
+        half_copies[h].wait()
+
+    def add_half(h, _):
+        mine_ref[h] = low_bits(
+            grads_ref[h].astype(jnp.float32) + half_ref[h].astype(jnp.float32)
+        )
+        return 0
+
+    lax.fori_loop(0, split, add_half, 0)
+    early_copies = scatter_copies(
+        lambda to: mine_ref.at[to, pl.ds(0, cut)], early_arrive_ref, early_sems
+    )
+    for copy in early_copies:
+        copy.start()
+    own = pl.ds(pl.multiple_of(low * own_rows, own_rows), own_rows)
+    d_second, dg_lanes = d_sum_ref[own, :], dg_sum_ref[own, :]
+    for k in range(1, split):
+        sum_copies[k - 1].wait()
+        d_second = d_second + arrive_ref[k - 1, :, :model_width].astype(jnp.float32)
+        dg_lanes = dg_lanes + arrive_ref[k - 1, :, model_width:].astype(jnp.float32)
+    d_gate = jnp.sum(dg_lanes, -1, keepdims=True)
+    second_own = second_ref[low]
+    route_lanes = routed_ref[low, :, model_width:].astype(jnp.float32)
+    probs, chosen, gate = route_probs(second_own, router, route_lanes, expert_count)
+    d_logits = low_bits(probs * (d_gate * (chosen - gate)))
+    d_second = d_second + matmul_nt(d_logits, router)
+    d_rows, d_gain = norm_back(resid_ref[...], gains_ref[1:2, :], d_second)
+    d_resid = grad_ref[...] + d_rows
+    d_resid_ref[...] = d_resid
+    branch_ref[low] = low_bits(d_resid)
+    branch_copies = plane_copies(lambda to, k: branch_ref.at[low], branch_ref, branch_sems, True)
+    for copy in branch_copies + y_copies:
+        copy.start()
+    small_ref[...] = jnp.zeros_like(small_ref)
+    small_ref[1:2, :] = jnp.sum(d_gain, 0, keepdims=True)
+    small_ref[2 : 2 + expert_count, :] = matmul_tn(d_logits, second_own)[:expert_count]
+
+    fill_offsets(reset_ref, lengths_ref, row_count)
+    spread(coef_ref, dt_rank + states, out_ref, steps, states)
+    out_full = gate_ref[:, channel_rows:].reshape(width, model_width)
+    for copy in branch_copies:
+        copy.wait()
+    for l in range(split):
+        d_gated = matmul_nt(branch_ref[l], out_full)
+        rows = slice(l * own_rows, (l + 1) * own_rows)
+        for j in range(tiles):
+            cols = slice(j * lanes, (j + 1) * lanes)
+            z = z_ref[j, rows, :]
+            sig = sigmoid_of(z)
+            d_tile = d_gated[:, cols]
+            dy_ref[j, rows, :] = d_tile * (z * sig)
+            d_z = d_tile * y_ref[j, rows, :] * (sig * (1.0 + z * (1.0 - sig)))
+            gz_ref[rows, cols] = low_bits(d_z)
+
+    def rates_of(j):
+        values = -jnp.exp(rows_ref[j, alog_row : alog_row + states, :]) * log2e
+        return [jnp.broadcast_to(values[n : n + 1, :], (subs, lanes)) for n in range(states)]
+
+    def ends_of(j, _):
+        found = scan_one_way(
+            j, None, True, states, steps, step_ref, reset_ref, dy_ref, out_ref, rates_of(j)
+        )
+        row = lax.broadcasted_iota(jnp.int32, (subs, lanes), 0)
+        for n, (grow, state) in enumerate(found):
+            send_ref[j, n : n + 1] = grow[:1]
+            send_ref[j, states + n : states + n + 1] = state[:1]
+            has = row < subs - 1
+            later_ref[0, j, n] = jnp.where(has, pltpu.roll(grow, subs - 1, 0), 1.0)
+            later_ref[1, j, n] = jnp.where(has, pltpu.roll(state, subs - 1, 0), 0.0)
+        for copy in ends_copies(send_ref, ends_ref, ends_sems, j, True):
+            copy.start()
+        return 0
+
+    lax.fori_loop(0, tiles, ends_of, 0)
+
+    normed = normed_ref[...].reshape(row_count, model_width)
+    branch = branch_ref[...].reshape(row_count, model_width)
+    for part, (first_op, second_op) in enumerate(((gz_ref, normed), (gated_ref, branch))):
+        half_width = width // 2
+        for at in (half_width, 0):
+            grad = low_bits(matmul_tn(first_op[:, at : at + half_width], second_op))
+            for b in range(split):
+                piece = grad[b * channel_rows : (b + 1) * channel_rows]
+                to = part * channel_rows
+                grads_ref[at // channel_rows + b, to : to + channel_rows] = piece
+    gate_rows = 2 * channel_rows
+    gate_copies = [
+        half_copy(
+            grads_ref.at[split + h, pl.ds(0, gate_rows)], gate_half_ref.at[h], gate_half_sems, h
+        )
+        for h in range(split)
+    ]
+    for copy in gate_copies:
+        copy.start()
+
+    def settle(j, _):
+        for copy in ends_copies(send_ref, ends_ref, ends_sems, j, True):
+            copy.wait()
+        enter = chain_enter(ends_ref, j, states, True)
+        for n in range(states):
+            entered = jnp.broadcast_to(enter[n : n + 1, :], (subs, lanes))
+            later_ref[1, j, n] += later_ref[0, j, n] * entered
+        return 0
+
+    lax.fori_loop(0, tiles, settle, 0)
+    y = y_sum_ref[own, :]
+    for k in range(1, split):
+        y_copies[k - 1].wait()
+        y = y + y_arrive_ref[k - 1].astype(jnp.float32)
+    mixed_out_ref[...] = low_bits(resid_ref[...] + gates_ref[own, :1] * y)
+    for h in range(split):
+        gate_copies[h].wait()
+
+        def add_gate(at, h=h):
+            rows = pl.ds(at, 16)
+            total = grads_ref[h, rows].astype(jnp.float32) + gate_half_ref[h, rows].astype(jnp.float32)
+            gate_mine_ref[h, rows] = low_bits(total)
+
+        row_loop(gate_rows, 16, add_gate)
+    early = mine_ref[high, :cut].astype(jnp.float32)
+    for k in range(1, split):
+        early_copies[k - 1].wait()
+        early = early + early_arrive_ref[k - 1].astype(jnp.float32)
+    early_ref[...] = early
+
+
+def run_turn(
+    second, routed, hidden_full, router_lanes, resid, grad_out, gains, lengths, gate_full, normed,
+    coef, step, z, y, gated, rows, dt_rank, states, expert_count, cut,
+):
+    _, own_rows, model_width = second.shape
+    row_count = own_rows * split
+    steps = row_count // subs
+    tiles = step.shape[0]
+    width = tiles * lanes
+    hidden_rows = hidden_full.shape[1]
+    gate_rows = gate_full.shape[1]
+    others = split - 1
+    vmem = pl.BlockSpec(memory_space=pltpu.VMEM)
+    f32, bf16 = jnp.float32, jnp.bfloat16
+    dma = pltpu.SemaphoreType.DMA
+    outs = [
+        ((own_rows, model_width), bf16),
+        ((own_rows, model_width), f32),
+        ((8, model_width), f32),
+        ((tiles, row_count, lanes), f32),
+        ((row_count, width), bf16),
+        ((2, tiles, states, subs, lanes), f32),
+        ((split, hidden_rows, model_width), bf16),
+        ((cut, model_width), f32),
+        ((split, gate_rows, model_width), bf16),
+    ]
+    span = 2 * hidden_rows // 2
+    return pl.pallas_call(
+        functools.partial(turn_kernel, dt_rank, states, expert_count, cut),
+        in_specs=[pl.BlockSpec(memory_space=pltpu.SMEM) if i == 7 else vmem for i in range(16)],
+        out_specs=[vmem] * len(outs),
+        out_shape=[jax.ShapeDtypeStruct(shape, kind) for shape, kind in outs],
+        scratch_shapes=[
+            pltpu.VMEM((2 * split, hidden_rows, model_width), bf16),
+            pltpu.VMEM((split, hidden_rows, model_width), bf16),
+            pltpu.VMEM((row_count, model_width), f32),
+            pltpu.VMEM((row_count, model_width), f32),
+            pltpu.VMEM((row_count, lanes), f32),
+            pltpu.VMEM((row_count, lanes), f32),
+            pltpu.VMEM((row_count, model_width), bf16),
+            pltpu.VMEM((row_count, span), bf16),
+            pltpu.VMEM((row_count, span), bf16),
+            pltpu.VMEM((others, own_rows, model_width + lanes), bf16),
+            pltpu.VMEM((others, own_rows, model_width + lanes), bf16),
+            pltpu.VMEM((others, own_rows, model_width), bf16),
+            pltpu.VMEM((others, own_rows, model_width), bf16),
+            pltpu.VMEM((split, own_rows, model_width), bf16),
+            pltpu.VMEM((steps, states, subs, lanes), f32),
+            pltpu.VMEM((row_count, lanes), f32),
+            pltpu.VMEM((tiles, 2 * states, lanes), f32),
+            pltpu.VMEM((others, tiles, 2 * states, lanes), f32),
+            pltpu.VMEM((others, cut, model_width), bf16),
+            pltpu.VMEM((split, gate_rows, model_width), bf16),
+            dma((2, split)),
+            dma((2, others)),
+            dma((2, others)),
+            dma((2, others)),
+            dma((2, others)),
+            dma((2, others, tiles)),
+            dma((2, split)),
+        ],
+        compiler_params=pltpu.CompilerParams(
+            collective_id=4, has_side_effects=True, vmem_limit_bytes=62 << 20
+        ),
+        cost_estimate=pl.CostEstimate(flops=1000, bytes_accessed=1000, transcendentals=0),
+    )(
+        second, routed, hidden_full, router_lanes, resid, grad_out, gains, lengths, gate_full, normed,
+        coef, step, z, y, gated, rows,
+    )
+
+
+def back_kernel(
+    dt_rank, states, tap_count, cut,
+    dy_ref, gz_ref, later_ref, mine_ref, gate_mine_ref, first_ref, gate_ref, normed_ref, input_ref,
+    coef_ref, step_ref, start_ref, rows_ref, d_resid_ref, tokens_ref, gains_ref, small_ref,
+    lengths_ref,
+    grad_tokens_ref, total_ref, late_ref, gate_own_ref, first_own_ref,
+    in_ref, out_ref, hist_ref, acc_in_ref, acc_out_ref, mixed_ref, conv_ref, q_ref, r_ref, reset_ref,
+    gdt_ref, gin_ref, dconv_ref, halo_ref, part_ref, arrive_ref, fold_ref, coef_send_ref,
+    coef_arrive_ref, gcoef_ref, misc_ref, select_ref, payload_ref, half_ref, mine_first_ref,
+    late_arrive_ref, gate_arrive_ref, first_arrive_ref, core_slots, plane_slots, line_slots,
+    late_sems, gate_sems, first_sems, half_sems, halo_sems, coef_sems, sum_sems, core_sems,
+    plane_sems, line_sems, local_sems,
+):
+    core, high, low = kernel_place()
+    _, own_rows, model_width = normed_ref.shape
+    row_count = own_rows * split
+    steps = row_count // subs
+    tiles = step_ref.shape[0]
+    width = tiles * lanes
+    channel_rows = width // (2 * split)
+    edge = input_ref.shape[0] - row_count
+    late_rows = late_ref.shape[0]
+    greeted = greet_all()
+    first_len = lengths_ref[0, 0]
+
+    def offsets(at, rows):
+        place = high * row_count + at + lax.broadcasted_iota(jnp.int32, (rows, lanes), 0)
+        return jnp.where(place < first_len, place, place - first_len)
+
+    fill_offsets(reset_ref, lengths_ref, row_count)
+    pl.semaphore_wait(pltpu.get_barrier_semaphore(), greeted)
+    late_copies = scatter_copies(
+        lambda to: mine_ref.at[to, pl.ds(cut, late_rows)], late_arrive_ref, late_sems
+    )
+    gate_copies = scatter_copies(lambda to: gate_mine_ref.at[to], gate_arrive_ref, gate_sems)
+    local = [
+        pltpu.make_async_copy(
+            mine_ref.at[high, pl.ds(cut, late_rows)], late_arrive_ref.at[split - 1], local_sems.at[0]
+        ),
+        pltpu.make_async_copy(
+            gate_mine_ref.at[high], gate_arrive_ref.at[split - 1], local_sems.at[1]
+        ),
+    ]
+    for copy in local + late_copies:
+        copy.start()
+
+    def convolve(at):
+        offset = offsets(at, 32)
+        for j in range(tiles):
+            span = input_ref[pl.ds(at, 32 + edge), j * lanes : (j + 1) * lanes]
+            conv_sum = jnp.zeros((32, lanes), jnp.float32)
+            for k in range(tap_count):
+                shift = edge - (tap_count - 1) + k
+                term = rows_ref[j, k : k + 1, :] * span[shift : shift + 32]
+                conv_sum = conv_sum + jnp.where(offset >= tap_count - 1 - k, term, 0.0)
+            conv_ref[j, pl.ds(at, 32), :] = conv_sum
+            mixed = low_bits(conv_sum * sigmoid_of(conv_sum)).astype(jnp.float32)
+            mixed_ref[j, pl.ds(at, 32), :] = mixed
+
+    row_loop(row_count, 32, convolve)
+    spread(coef_ref, dt_rank, in_ref, steps, states)
+    spread(coef_ref, dt_rank + states, out_ref, steps, states)
+    acc_in_ref[...] = jnp.zeros_like(acc_in_ref)
+    acc_out_ref[...] = jnp.zeros_like(acc_out_ref)
+    misc_ref[...] = jnp.zeros_like(misc_ref)
+
+    def back_of(j, _):
+        values = -jnp.exp(rows_ref[j, alog_row : alog_row + states, :]) * log2e
+        rates = [jnp.broadcast_to(values[n : n + 1, :], (subs, lanes)) for n in range(states)]
+
+        def forward(s, held):
+            step = step_ref[j, pl.ds(s, subs, stride=steps), :]
+            drive = step * mixed_ref[j, pl.ds(s, subs, stride=steps), :]
+            step = step + reset_ref[pl.ds(s, subs, stride=steps), :]
+            now_all = []
+            for n in range(states):
+                now = jnp.exp2(step * rates[n]) * held[n] + in_ref[s, n] * drive
+                hist_ref[s + 1, n] = now
+                now_all.append(now)
+            return tuple(now_all)
+
+        held = []
+        for n in range(states):
+            hist_ref[0, n] = start_ref[j, n]
+            held.append(start_ref[j, n])
+        lax.fori_loop(0, steps, forward, tuple(held), unroll=2)
+
+        def backward(turn, carry):
+            s = steps - 1 - turn
+            later, sums = carry
+            delta = step_ref[j, pl.ds(s, subs, stride=steps), :]
+            drive = delta * mixed_ref[j, pl.ds(s, subs, stride=steps), :]
+            step = delta + reset_ref[pl.ds(s, subs, stride=steps), :]
+            dy = dy_ref[j, pl.ds(s, subs, stride=steps), :]
+            rows = pl.ds(pl.multiple_of(s * subs, subs), subs)
+            q = jnp.zeros((subs, lanes), jnp.float32)
+            r = jnp.zeros((subs, lanes), jnp.float32)
+            later_next, sums_next = [], []
+            for n in range(states):
+                cols = slice(n * lanes, (n + 1) * lanes)
+                d_state = out_ref[s, n] * dy + later[n]
+                back = jnp.exp2(step * rates[n]) * d_state
+                scaled = back * hist_ref[s, n]
+                sums_next.append(sums[n] + scaled * delta)
+                q = q + scaled * rates[n]
+                r = r + d_state * in_ref[s, n]
+                acc_in_ref[rows, cols] += d_state * drive
+                acc_out_ref[rows, cols] += hist_ref[s + 1, n] * dy
+                later_next.append(back)
+            q_ref[j, pl.ds(s, subs, stride=steps), :] = q * (1.0 / log2e)
+            r_ref[j, pl.ds(s, subs, stride=steps), :] = r
+            return tuple(later_next), tuple(sums_next)
+
+        zero = jnp.zeros((subs, lanes), jnp.float32)
+        later = tuple(later_ref[1, j, n] for n in range(states))
+        _, sums = lax.fori_loop(0, steps, backward, (later, (zero,) * states))
+        for n in range(states):
+            total = jnp.sum(sums[n] * rates[n], 0, keepdims=True) * (1.0 / log2e)
+            misc_ref[j, alog_row + n : alog_row + n + 1, :] = total
+        return 0
+
+    lax.fori_loop(0, tiles, back_of, 0)
+
+    source = lax.broadcasted_iota(jnp.int32, select_ref.shape, 0) // lanes
+    target = lax.broadcasted_iota(jnp.int32, select_ref.shape, 1)
+
+    def fold(acc_ref, first, fresh):
+        select_ref[...] = jnp.where(target == first + source, 1.0, 0.0).astype(jnp.bfloat16)
+
+        def one(at):
+            values = acc_ref[pl.ds(at, 128), :]
+            coarse = low_bits(values)
+            fine = low_bits(values - coarse.astype(jnp.float32))
+            found = matmul(coarse, select_ref[...]) + matmul(fine, select_ref[...])
+            for i in range(128 // subs):
+                rows = pl.ds(at // subs + i, subs, stride=steps)
+                piece = found[i * subs : (i + 1) * subs]
+                fold_ref[rows, :] = piece if fresh else fold_ref[rows, :] + piece
+
+        row_loop(row_count, 128, one)
+
+    fold(acc_in_ref, dt_rank, True)
+    fold(acc_out_ref, dt_rank + states, False)
+    dt_full = first_ref[:, :, model_width + lanes : model_width + 2 * lanes].reshape(width, lanes)
+
+    def step_grads(at):
+        rows = pl.ds(at, 128)
+        pre = matmul_nt(low_bits(coef_ref[rows, :]), dt_full)
+        for j in range(tiles):
+            cols = slice(j * lanes, (j + 1) * lanes)
+            mixed = mixed_ref[j, rows, :]
+            d_step = q_ref[j, rows, :] + r_ref[j, rows, :] * mixed
+            d_dt = d_step * sigmoid_of(pre[:, cols] + rows_ref[j, bias_row : bias_row + 1, :])
+            gdt_ref[rows, cols] = low_bits(d_dt)
+            misc_ref[j, bias_row : bias_row + 1, :] += jnp.sum(d_dt, 0, keepdims=True)
+            misc_ref[j, skip_row : skip_row + 1, :] += jnp.sum(
+                dy_ref[j, rows, :] * mixed, 0, keepdims=True
+            )
+        part = fold_ref[rows, :] + matmul(gdt_ref[rows, :], dt_full)
+        fold_ref[rows, :] = part
+        coef_send_ref[rows, :] = low_bits(part)
+
+    row_loop(row_count, 128, step_grads)
+    coef_copies = plane_copies(lambda to, k: coef_send_ref, coef_arrive_ref, coef_sems, False)
+    for copy in coef_copies:
+        copy.start()
+    low_coef = low_bits(coef_ref[...])
+    for j in range(tiles):
+        rows = slice(j * lanes, (j + 1) * lanes)
+        payload_ref[rows, model_width + lanes : model_width + 2 * lanes] = low_bits(
+            matmul_tn(gdt_ref[:, rows], low_coef)
+        )
+    for copy in coef_copies:
+        copy.wait()
+    total = fold_ref[...]
+    for k in range(1, split):
+        total = total + coef_arrive_ref[k - 1].astype(jnp.float32)
+    gcoef_ref[...] = low_bits(total)
+    x_full = first_ref[:, :, model_width : model_width + lanes].reshape(width, lanes)
+
+    def conv_grads(at):
+        rows = pl.ds(at, 128)
+        from_coef = matmul_nt(gcoef_ref[rows, :], x_full)
+        for j in range(tiles):
+            cols = slice(j * lanes, (j + 1) * lanes)
+            d_mixed = rows_ref[j, skip_row : skip_row + 1, :] * dy_ref[j, rows, :]
+            d_mixed = d_mixed + r_ref[j, rows, :] * step_ref[j, rows, :] + from_coef[:, cols]
+            conv = conv_ref[j, rows, :]
+            sig = sigmoid_of(conv)
+            dconv_ref[rows, cols] = d_mixed * (sig * (1.0 + conv * (1.0 - sig)))
+
+    row_loop(row_count, 128, conv_grads)
+
+    def halo_copy():
+        return remote(
+            dconv_ref.at[pl.ds(0, subs)], halo_ref, halo_sems.at[0], halo_sems.at[1],
+            core, lax.rem(high + split - 1, split), low,
+        )
+
+    @pl.when(high > 0)
+    def _():
+        halo_copy().start()
+
+    for copy in gate_copies:
+        copy.start()
+
+    def tap_grads(at):
+        offset = offsets(at, 32)
+        for j in range(tiles):
+            cols = slice(j * lanes, (j + 1) * lanes)
+            span = input_ref[pl.ds(at, 32 + edge), cols]
+            d_conv = dconv_ref[pl.ds(at, 32), cols]
+            for k in range(tap_count):
+                shift = edge - (tap_count - 1) + k
+                term = jnp.where(offset >= tap_count - 1 - k, d_conv * span[shift : shift + 32], 0.0)
+                misc_ref[j, k : k + 1, :] += jnp.sum(term, 0, keepdims=True)
+
+    row_loop(row_count, 32, tap_grads)
+
+    @pl.when(high < split - 1)
+    def _():
+        halo_copy().wait_recv()
+        dconv_ref[row_count:, :] = halo_ref[...]
+
+    @pl.when(high == split - 1)
+    def _():
+        dconv_ref[row_count:, :] = jnp.zeros_like(halo_ref)
+
+    def input_grads(at):
+        masks = [offsets(at + m, 32) >= m for m in range(tap_count)]
+        for j in range(tiles):
+            cols = slice(j * lanes, (j + 1) * lanes)
+            span = dconv_ref[pl.ds(at, 32 + subs), cols]
+            d_input = jnp.zeros((32, lanes), jnp.float32)
+            for m in range(tap_count):
+                k = tap_count - 1 - m
+                term = rows_ref[j, k : k + 1, :] * span[m : m + 32]
+                d_input = d_input + jnp.where(masks[m], term, 0.0)
+            gin_ref[pl.ds(at, 32), cols] = low_bits(d_input)
+
+    row_loop(row_count, 32, input_grads)
+
+    first_in = first_ref[:, :, :model_width].reshape(width, model_width)
+    second_in = gate_ref[:, :channel_rows].reshape(width, model_width)
+
+    def normed_block(l):
+        rows = pl.ds(pl.multiple_of(l * own_rows, own_rows), own_rows)
+        return matmul(gin_ref[rows, :], first_in) + matmul(gz_ref[rows, :], second_in)
+
+    sum_copies = plane_copies(lambda to, k: part_ref.at[k - 1], arrive_ref, sum_sems, False)
+    for k in range(1, split):
+        part_ref[k - 1] = low_bits(normed_block(lax.rem(low + k, split)))
+        sum_copies[k - 1].start()
+
+    normed = normed_ref[...].reshape(row_count, model_width)
+    for j in range(tiles):
+        rows = slice(j * lanes, (j + 1) * lanes)
+        payload_ref[rows, model_width : model_width + lanes] = low_bits(
+            matmul_tn(low_bits(mixed_ref[j]), gcoef_ref[...])
+        )
+        payload_ref[rows, model_width + 2 * lanes :] = low_bits(misc_ref[j].T)
+    half_width = width // 2
+    for at in (half_width, 0):
+        payload_ref[at : at + half_width, :model_width] = low_bits(
+            matmul_tn(gin_ref[:, at : at + half_width], normed)
+        )
+        if at:
+            half = remote(
+                payload_ref.at[pl.ds(half_width, half_width)], half_ref, half_sems.at[0],
+                half_sems.at[1], 1 - core, high, low,
+            )
+            half.start()
+    d_normed = normed_block(low)
+    for k in range(1, split):
+        sum_copies[k - 1].wait()
+        d_normed = d_normed + arrive_ref[k - 1].astype(jnp.float32)
+    tokens = tokens_ref[...].astype(jnp.float32)
+    d_rows, d_gain = norm_back(tokens, gains_ref[0:1, :], d_normed)
+    grad_tokens_ref[...] = d_resid_ref[...] + d_rows
+
+    core_slots[core] = small_ref[...]
+    core_slots[core, 0:1, :] = jnp.sum(d_gain, 0, keepdims=True)
+    hop = remote(
+        core_slots.at[core], core_slots.at[core], core_sems.at[0], core_sems.at[1], 1 - core, high, low
+    )
+    hop.start()
+    half.wait()
+
+    def add_half(at):
+        rows = pl.ds(at, 64)
+        both = payload_ref[rows, :].astype(jnp.float32) + half_ref[rows, :].astype(jnp.float32)
+        mine_first_ref[rows, :] = low_bits(both)
+
+    row_loop(half_width, 64, add_half)
+    hop.wait()
+    plane_slots[low] = core_slots[0] + core_slots[1]
+    plane = plane_copies(lambda to, k: plane_slots.at[low], plane_slots, plane_sems, True)
+    for copy in plane:
+        copy.start()
+    for copy in plane:
+        copy.wait()
+    line_slots[high] = (plane_slots[0] + plane_slots[1]) + (plane_slots[2] + plane_slots[3])
+    line = line_copies(line_slots.at[high], lambda at: line_slots.at[at], line_sems)
+    for copy in line:
+        copy.start()
+    first_copies = scatter_copies(
+        lambda to: mine_first_ref.at[pl.ds(pl.multiple_of(to * channel_rows, 16), channel_rows)],
+        first_arrive_ref,
+        first_sems,
+    )
+    for copy in first_copies:
+        copy.start()
+
+    for copy in local:
+        copy.wait()
+    finish(late_copies, late_arrive_ref, late_ref)
+    finish(gate_copies, gate_arrive_ref, gate_own_ref)
+    for k in range(1, split):
+        line_arrived(line_slots.at[high], lambda at: line_slots.at[at], line_sems, k)
+    for copy in line:
+        copy.wait_send()
+    total_ref[...] = (line_slots[0] + line_slots[1]) + (line_slots[2] + line_slots[3])
+    own = pl.ds(pl.multiple_of(high * channel_rows, 16), channel_rows)
+    first_arrive_ref[split - 1] = mine_first_ref[own, :]
+    finish(first_copies, first_arrive_ref, first_own_ref)
+
+    @pl.when(high > 0)
+    def _():
+        halo_copy().wait_send()
+
+
+def finish(copies, arrive_ref, out_ref):
+    for copy in copies:
+        copy.wait()
+
+    def one(at):
+        rows = pl.ds(at, 16)
+        total = arrive_ref[split - 1, rows].astype(jnp.float32)
+        for k in range(split - 1):
+            total = total + arrive_ref[k, rows].astype(jnp.float32)
+        out_ref[rows, :] = total
+
+    row_loop(out_ref.shape[0], 16, one)
+
+
+def run_back(
+    dy, gz, later, mine, gate_mine, first_full, gate_full, normed, input_all, coef, step, start, rows,
+    d_resid, tokens, gains, small, lengths, dt_rank, states, tap_count, cut,
+):
+    _, own_rows, model_width = normed.shape
+    row_count = own_rows * split
+    steps = row_count // subs
+    tiles = step.shape[0]
+    width = tiles * lanes
+    channel_rows = width // (2 * split)
+    others = split - 1
+    late_rows = mine.shape[1] - cut
+    gate_rows = gate_mine.shape[1]
+    first_columns = first_full.shape[2]
+    vmem = pl.BlockSpec(memory_space=pltpu.VMEM)
+    anywhere = pl.BlockSpec(memory_space=pl.ANY)
+    specs = [anywhere if i in (3, 4) else vmem for i in range(17)]
+    specs.append(pl.BlockSpec(memory_space=pltpu.SMEM))
+    f32, bf16 = jnp.float32, jnp.bfloat16
+    dma = pltpu.SemaphoreType.DMA
+    outs = [
+        (own_rows, model_width),
+        (8, model_width),
+        (late_rows, model_width),
+        (gate_rows, model_width),
+        (channel_rows, first_columns),
+    ]
+    tiled = pltpu.VMEM((tiles, row_count, lanes), f32)
+    spreads = pltpu.VMEM((steps, states, subs, lanes), f32)
+    summed = pltpu.VMEM((row_count, states * lanes), f32)
+    return pl.pallas_call(
+        functools.partial(back_kernel, dt_rank, states, tap_count, cut),
+        in_specs=specs,
+        out_specs=[vmem] * len(outs),
+        out_shape=[jax.ShapeDtypeStruct(shape, f32) for shape in outs],
+        scratch_shapes=[
+            spreads,
+            spreads,
+            pltpu.VMEM((steps + 1, states, subs, lanes), f32),
+            summed,
+            summed,
+            tiled,
+            tiled,
+            tiled,
+            tiled,
+            pltpu.VMEM((row_count, lanes), f32),
+            pltpu.VMEM((row_count, width), bf16),
+            pltpu.VMEM((row_count, width), bf16),
+            pltpu.VMEM((row_count + subs, width), f32),
+            pltpu.VMEM((subs, width), f32),
+            pltpu.VMEM((others, own_rows, model_width), bf16),
+            pltpu.VMEM((others, own_rows, model_width), bf16),
+            pltpu.VMEM((row_count, lanes), f32),
+            pltpu.VMEM((row_count, lanes), bf16),
+            pltpu.VMEM((others, row_count, lanes), bf16),
+            pltpu.VMEM((row_count, lanes), bf16),
+            pltpu.VMEM((tiles, lanes, lanes), f32),
+            pltpu.VMEM((states * lanes, lanes), bf16),
+            pltpu.VMEM((width, first_columns), bf16),
+            pltpu.VMEM((width // 2, first_columns), bf16),
+            pltpu.VMEM((width // 2, first_columns), bf16),
+            pltpu.VMEM((split, late_rows, model_width), bf16),
+            pltpu.VMEM((split, gate_rows, model_width), bf16),
+            pltpu.VMEM((split, channel_rows, first_columns), bf16),
+            pltpu.VMEM((2, 8, model_width), f32),
+            pltpu.VMEM((split, 8, model_width), f32),
+            pltpu.VMEM((split, 8, model_width), f32),
+        ]
+        + [dma((2, others))] * 3
+        + [dma((2,)), dma((2,)), dma((2, others)), dma((2, others)), dma((2,))]
+        + [dma((2, others)), dma((2, others)), dma((2,))],
+        compiler_params=pltpu.CompilerParams(
+            collective_id=5, has_side_effects=True, vmem_limit_bytes=62 << 20
+        ),
+        cost_estimate=pl.CostEstimate(flops=1000, bytes_accessed=1000, transcendentals=0),
+    )(
+        dy, gz, later, mine, gate_mine, first_full, gate_full, normed, input_all, coef, step, start,
+        rows, d_resid, tokens, gains, small, lengths,
+    )
+
+
 def norm_rows(values, gain_row):
     return values * lax.rsqrt(jnp.mean(values * values, -1, keepdims=True) + eps_norm) * gain_row
 
@@ -547,7 +1809,7 @@
     return total
 
 
-def shards(
+def shards_general(
     tokens,
     routes,
     lengths,
@@ -818,6 +2080,109 @@
     )
 
 
+def shards_plane(
+    tokens,
+    routes,
+    lengths,
+    grad_out,
+    norm_gains,
+    router,
+    in_weight,
+    conv_weight,
+    x_weight,
+    dt_weight,
+    dt_bias,
+    a_log,
+    skip_gain,
+    out_weight,
+    expert_in,
+    expert_out,
+):
+    channels, tap_count = conv_weight.shape
+    dt_rank = dt_weight.shape[1]
+    states = a_log.shape[1]
+    expert_count, hidden, model_width = expert_in.shape
+    own_rows = tokens.shape[0]
+    row_count = own_rows * split
+    high_count = lax.axis_size("seq") // split
+    low = lax.axis_index("seq") % split
+    high = lax.axis_index("seq") // split
+    coef_count = dt_rank + 2 * states
+    channel_rows = -(-channels // 16) * 16
+    width = 2 * high_count * channel_rows
+    hidden_rows = expert_count * hidden
+    small_width = -(-(coef_count + dt_rank + tap_count + 2 + states) // lanes) * lanes
+
+    small = jnp.concatenate(
+        [x_weight, dt_weight, conv_weight, dt_bias[:, None], a_log, skip_gain[:, None]], 1
+    )
+    small = jnp.pad(small, ((0, 0), (0, small_width - small.shape[1])))
+    inputs = tokens.astype(jnp.float32)
+    def wide(parts, columns):
+        part = jnp.concatenate(parts, 1)
+        return jnp.pad(part, ((0, 0), (0, columns - part.shape[1])))
+
+    gap = jnp.zeros((channels, 2), jnp.bfloat16)
+    a_part = pad_rows(
+        jnp.concatenate(
+            [
+                in_weight[0],
+                wide([x_weight], lanes),
+                wide([dt_weight], lanes),
+                wide([conv_weight, dt_bias[:, None], skip_gain[:, None], gap, a_log], lanes),
+            ],
+            1,
+        ),
+        channel_rows,
+    )
+    b_part = jnp.concatenate(
+        [pad_rows(in_weight[1], channel_rows), pad_rows(out_weight, channel_rows)], 0
+    )
+    c_part = jnp.concatenate(
+        [expert_in.reshape(-1, model_width), expert_out.reshape(-1, model_width)], 0
+    )
+    g_part = low_bits(
+        jnp.concatenate(
+            [grad_out, routes[:, None].astype(jnp.float32) * jnp.ones((1, lanes), jnp.float32)], 1
+        )
+    )
+    (
+        first_full, gate_full, hidden_full, normed, _, routed, input_all, coef, step, z, y, gated, start,
+        resid, second, rows,
+    ) = run_mixer(
+        tokens, norm_gains, lengths, a_part, b_part, c_part, g_part, dt_rank, states, tap_count
+    )
+    cut = hidden_rows * 2 // 3
+    router_lanes = jnp.pad(router, ((0, 0), (0, lanes - expert_count)))
+    mixed_out, d_resid, small_sums, dy, gz, later, mine, early, gate_mine = run_turn(
+        second, routed, hidden_full, router_lanes, resid, grad_out, norm_gains, lengths, gate_full,
+        normed, coef, step, z, y, gated, rows, dt_rank, states, expert_count, cut,
+    )
+    grad_tokens, sums, late, gate_own, first_own = run_back(
+        dy, gz, later, mine, gate_mine, first_full, gate_full, normed, input_all, coef, step, start,
+        rows, d_resid, tokens, norm_gains, small_sums, lengths, dt_rank, states, tap_count, cut,
+    )
+    hidden_own = jnp.concatenate([early, late], 0)
+    first_own, gate_first = first_own[:channels], gate_own[:channels]
+    misc = first_own[:, model_width + 2 * lanes :]
+    return (
+        mixed_out,
+        grad_tokens,
+        sums[:2],
+        sums[2 : 2 + expert_count].T,
+        jnp.stack([first_own[:, :model_width], gate_first]),
+        misc[:, :tap_count],
+        first_own[:, model_width : model_width + coef_count],
+        first_own[:, model_width + lanes : model_width + lanes + dt_rank],
+        misc[:, bias_row],
+        misc[:, alog_row : alog_row + states],
+        misc[:, skip_row],
+        gate_own[channel_rows : channel_rows + channels],
+        hidden_own[:hidden_rows].reshape(expert_count, hidden, model_width),
+        hidden_own[hidden_rows:].reshape(expert_count, hidden, model_width),
+    )
+
+
 def solution(mesh):
     both = ("grp", "seq")
     in_specs = (
@@ -854,4 +2219,5 @@
         P(None, both, None),
         P(None, both, None),
     )
+    shards = shards_plane if mesh.shape["seq"] == split * split else shards_general
     return jax.shard_map(shards, mesh=mesh, in_specs=in_specs, out_specs=out_specs, check_vma=False)

time: 549 us -> 383 us (0.70); the launches traced: 540 us -> 380 us
  Pallas kernels: 133 us -> 357 us
  waiting for transfers between devices: 187 us -> 0 us
  starting transfers between devices: 97.4 us -> 0 us
  other arithmetic: 43.4 us -> 5.61 us
  local copies, waits for them, and re-layouts: 51.2 us -> 16.1 us
  matrix products: 24.4 us -> 0 us
    pallas_call x5 -> x3, Pallas kernels: 133 us -> 357 us  [the longest x1 162 us: run_mixer(): pl.pallas_call(functools.partial(mixer_kernel, dt_rank, states, tap_count...]
    ppermute x61 -> x0, waiting for transfers between devices: 187 us -> none  [the longest x31 94.3 us: swap_low(): return lax.ppermute(value, 'seq', [(s, s ^ k) for s in range(count)])]
    ppermute x61 -> x0, starting transfers between devices: 97.4 us -> none  [the longest x21 54.2 us: turn_high(): lax.ppermute(value, 'seq', [(s, (s + split * k) % count) for s in range(c...]
    dot_general x19 -> x0, matrix products: 24.4 us -> none  [the longest x6 13.9 us: matmul_nt(): lax.dot_general(first_op, second_op, (((1,), (1,)), ((), ())), preferred_...]
    unnamed x183 -> x29, local copies, waits for them, and re-layouts: 20.1 us -> 3.83 us
    convert_element_type x18 -> x0, other arithmetic: 12.5 us -> none  [the longest x10 10.6 us: low_bits(): return value.astype(jnp.bfloat16)]
    add x13 -> x0, other arithmetic: 7.39 us -> none  [the longest x4 4.5 us: fold_high(): return sum((a.astype(jnp.float32) for a in [block(high)] + arrived))]
    another operation x8 -> x3, other arithmetic: 8.41 us -> 1.69 us  [the longest x1 0.92 us: shards_plane(): jnp.stack([first_own[:, :model_width], gate_first])]
  transfers between devices with their start and end apart: 61 -> 0, of which waited for: 25 -> 0; matrix products, arithmetic and copies ran while one was open for 14% -> 0% of each run, Pallas kernels for 21% -> 0%
where the time goes in v2:
time: 383 us; the launch traced here: 380 us
  Pallas kernels  357 us (93%)
  local copies, waits for them, and re-layouts  16.1 us (4%)
  other arithmetic  5.61 us (1%)
    pallas_call x1, Pallas kernels, run_mixer(): pl.pallas_call(functools.partial(mixer_kernel, dt_rank, states, tap_count...  162 us
    pallas_call x1, Pallas kernels, run_back(): pl.pallas_call(functools.partial(back_kernel, dt_rank, states, tap_count,...  113 us
    pallas_call x1, Pallas kernels, run_turn(): pl.pallas_call(functools.partial(turn_kernel, dt_rank, states, expert_cou...  81.9 us

profile of v2, /device:TPU:0, one launch (start us, length us, event | category | flops | bytes accessed | tf_op | source)
XLA Modules:
  0.0 380.0 jit_solution(16547592290279035064)
XLA Ops:
  0.7 0.7 convert_convert_fusion
  1.4 1.4 concatenate.19
  3.0 0.9 copy.45
  3.9 0.8 pad.33.router_ref
  4.8 0.8 pad_maximum_fusion.3.g_ref
  5.6 0.8 fusion.7.b_ref
  6.4 0.7 pad.30.a_ref
  7.1 1.0 pad_maximum_fusion.1.c_ref
  8.1 162.3 %shard_map.263 = (bf16[8,80,1536]{2,1,0:T(8,128)(2,1)}, bf16[8,160,1152]{2,1,0:T(8,128)(2,1)}, bf16[8,384,1152]{2,1,0:T(8,128)(2,1)}, bf16[4,128,1152]{2,1,0:T(8...) custom-call(bf16[128,1152]{1,0:T(8,128)(2,1)} %tokens_ref.3, ...), custom_call_target="tpu_custom_call" | custom-call | flops 1000 | bytes 1000 | tf_op jit(solution)/shard_map/pallas_call | solution.py:855
  170.4 81.9 %shard_map.264 = (bf16[128,1152]{1,0:T(8,128)(2,1)}, f32[128,1152]{1,0:T(8,128)}, f32[8,1152]{1,0:T(8,128)}, f32[5,512,128]{2,1,0:T(8,128)}, bf16[512,640]{1,0:T...) custom-call(bf16[4,128,1152]{2,1,0:T(8,128)(2,1)} %get-tuple-element, ...), custom_call_target="tpu_custom_call" | custom-call | flops 1000 | bytes 1000 | tf_op jit(solution)/shard_map/pallas_call | solution.py:1184
  252.3 113.3 %shard_map.265 = (f32[128,1152]{1,0:T(8,128)}, f32[8,1152]{1,0:T(8,128)}, f32[256,1152]{1,0:T(8,128)}, f32[160,1152]{1,0:T(8,128)}, f32[80,1536]{1,0:T(8,128)}) custom-call(f32[5,512,128]{2,1,0:T(8,128)} %get-tuple-element.56.dy_ref, bf16[512,640]{1,0:T(8,128)(2,1)} %get-tuple-element.57.gz_ref, f32[2,5,16,8,128]{4,3,2,1,0:T(8,128)} %get-tuple-element.58.later_ref, ...), custom_call_target="tpu_custom_call" | custom-call | flops 1000 | bytes 1000 | tf_op jit(solution)/shard_map/pallas_call | solution.py:1603
  365.6 1.6 slice_reduce_fusion
  367.1 1.5 slice_bitcast_fusion.4
  368.6 0.8 slice.65
  369.4 0.7 copy.47
  370.1 1.4 slice.63
  371.5 1.4 slice.62
  372.9 0.8 slice.61
  373.6 1.0 slice_bitcast_fusion.1
  375.3 0.8 fusion.12
  376.1 0.9 pad_maximum_fusion.2
  377.0 1.4 fusion.11
  378.4 0.7 copy.50
  379.1 0.8 copy.51
  (31 shorter events, 1.0 us)
Async XLA Ops:
  0.6 4.1 %copy-start.1 = (f32[128,1152]{1,0:T(8,128)S(1)}, f32[128,1152]{1,0:T(8,128)}, u32[]{:S(2)}) copy-start(f32[128,1152]{1,0:T(8,128)} %grad_ref.1) | copy-start | bytes 1769476
  0.7 4.9 %copy-start.7 = (bf16[2,72,1152]{2,1,0:T(8,128)(2,1)S(1)}, bf16[2,72,1152]{2,1,0:T(8,128)(2,1)}, u32[]{:S(2)}) copy-start(bf16[2,72,1152]{2,1,0:T(8,128)(2,1)} %param.22) | copy-start | bytes 995332
  3.9 1.6 copy-start.9
  4.7 1.6 copy-start.10
  4.7 1.6 copy-start.11
  4.8 2.3 copy-start.5
  4.8 2.3 copy-start.6
  365.5 9.8 %copy-start.2 = (f32[160,1152]{1,0:T(8,128)S(1)}, f32[160,1152]{1,0:T(8,128)}, u32[]{:S(2)}) copy-start(f32[160,1152]{1,0:T(8,128)} %get-tuple-element.69) | copy-start | bytes 2211844
  374.6 2.4 copy-start
  374.7 2.4 copy-start.3
  377.0 1.4 copy-start.8
  377.0 2.1 copy-start.4

commit v3 on v2

--- a/solution.py
+++ b/solution.py
@@ -430,14 +430,26 @@
     return copies
 
 
-def line_copies(src, dst_of, sems):
+def at_ends():
+    _, high, _ = kernel_place()
+    return (high == 0) | (high == split - 1)
+
+
+def line_copies(src, dst_of, sems, both=False):
     core, high, low = kernel_place()
     return [
         remote(
             src, dst_of(high), sems.at[0, k - 1], sems.at[1, k - 1], core, lax.rem(high + k, split), low
         )
-        for k in range(1, split)
+        for k in ((1, 2, 3) if both else (1, 3))
     ]
+
+
+def line_relay(dst_of, sems):
+    core, high, low = kernel_place()
+    block = lax.rem(high * 2, 3) + 3 * (high // 3)
+    to = lax.rem(block + 2, split)
+    return remote(dst_of(block), dst_of(block), sems.at[0, 1], sems.at[1, 1], core, to, low)
 
 
 def line_arrived(src, dst_of, sems, k):
@@ -536,7 +548,7 @@
     in_ref, out_ref, drive_ref, reset_ref, mixed_ref, partial_ref, arrive_ref, coef_send_ref,
     coef_arrive_ref, send_ref, ends_ref, grow_ref, state_ref,
     a_sems, b_sems, c_sems, d_sems, a_core, b_core, c_core, d_core, token_sems, route_sems,
-    second_sems, coef_sems, sum_sems, edge_send, edge_arrive, ends_sems, local_sems,
+    second_sems, coef_sems, sum_sems, edge_send, edge_arrive, ends_sems, local_sem,
 ):
     core, high, low = kernel_place()
     own_rows, model_width = tokens_ref.shape
@@ -570,14 +582,11 @@
     greeted += split - 1
     tokens = tokens_ref[...].astype(jnp.float32)
     normed_ref[low] = low_bits(norm_rows(tokens, gains_ref[0:1, :]))
-    local = [
-        pltpu.make_async_copy(a_ref, first_ref.at[high], local_sems.at[0]),
-        pltpu.make_async_copy(b_ref, gate_ref.at[high], local_sems.at[1]),
-        pltpu.make_async_copy(c_ref, hidden_ref.at[high], local_sems.at[2]),
-        pltpu.make_async_copy(g_ref, routed_ref.at[low], local_sems.at[3]),
-    ]
-    for copy in local:
-        copy.start()
+    local = pltpu.make_async_copy(c_ref, hidden_ref.at[high], local_sem)
+    local.start()
+    first_ref[high] = a_ref[...]
+    gate_ref[high] = b_ref[...]
+    routed_ref[low] = g_ref[...]
     pl.semaphore_wait(barrier, greeted)
 
     @pl.when((low == split - 1) & (high < split - 1))
@@ -607,12 +616,30 @@
     c_copies = line_copies(c_src, c_dst, c_sems)
     d_copies = line_copies(d_src, d_dst, d_sems)
     route_copies = plane_copies(lambda to, k: g_ref, routed_ref, route_sems, True)
-    for copy in token_copies + a_copies + b_copies + c_copies + route_copies:
+    relays = [line_relay(a_dst, a_sems), line_relay(b_dst, b_sems)]
+    relays += [line_relay(c_dst, c_sems), line_relay(d_dst, d_sems)]
+    for copy in token_copies + a_copies + route_copies:
         copy.start()
-    for copy in local:
-        copy.wait()
+
+    def relay_from_end(i):
+        @pl.when(at_ends())
+        def _():
+            relays[i].start()
+
+    def relay_inside(i):
+        @pl.when(jnp.logical_not(at_ends()))
+        def _():
+            relays[i].start()
+
+    def arrived(src, dst_of, sems, core_sems, ks):
+        for k in ks:
+            line_arrived(src, dst_of, sems, k)
+            copy = core_copy(dst_of, core_sems, k)
+            copy.start()
+            core_copies.append(copy)
+
+    relay_from_end(0)
     core_copies = [core_copy(a_dst, a_core, 0), core_copy(b_dst, b_core, 0)]
-    core_copies += [core_copy(c_dst, c_core, 0), core_copy(d_dst, d_core, 0)]
     for copy in core_copies:
         copy.start()
 
@@ -631,13 +658,14 @@
     def _():
         edge_ref[...] = jnp.zeros_like(edge_ref)
 
-    for k in range(1, split):
-        line_arrived(a_ref, a_dst, a_sems, k)
-        copy = core_copy(a_dst, a_core, k)
+    arrived(a_ref, a_dst, a_sems, a_core, (1, 3))
+    relay_inside(0)
+    for copy in b_copies:
         copy.start()
-        core_copies.append(copy)
+    relay_from_end(1)
     for copy in token_copies:
         copy.wait()
+    arrived(a_ref, a_dst, a_sems, a_core, (2,))
 
     @pl.when(high > 0)
     def _():
@@ -674,6 +702,15 @@
             )
 
     row_loop(row_count, 32, convolve)
+    arrived(b_ref, b_dst, b_sems, b_core, (1, 3))
+    relay_inside(1)
+    local.wait()
+    for copy in (core_copy(c_dst, c_core, 0), core_copy(d_dst, d_core, 0)):
+        copy.start()
+        core_copies.append(copy)
+    for copy in c_copies:
+        copy.start()
+    relay_from_end(2)
 
     x_full = first_ref[:, :, model_width : model_width + lanes].reshape(width, lanes)
     part = matmul(mixed_ref[...], x_full)
@@ -721,14 +758,13 @@
         return 0
 
     lax.fori_loop(0, tiles, ends_of, 0)
+    arrived(c_src, c_dst, c_sems, c_core, (1, 3))
+    relay_inside(2)
     for copy in d_copies:
         copy.start()
+    relay_from_end(3)
     spread(coef_ref, first_c, out_ref, steps, states)
-    for k in range(1, split):
-        line_arrived(b_ref, b_dst, b_sems, k)
-        copy = core_copy(b_dst, b_core, k)
-        copy.start()
-        core_copies.append(copy)
+    arrived(b_ref, b_dst, b_sems, b_core, (2,))
     row = lax.broadcasted_iota(jnp.int32, (subs, lanes), 0)
 
     def forward_of(j, _):
@@ -793,11 +829,7 @@
         partial_ref[k - 1] = low_bits(out_block(lax.rem(low + k, split)))
         sum_copies[k - 1].start()
     resid = tokens_ref[...].astype(jnp.float32) + out_block(low)
-    for k in range(1, split):
-        line_arrived(c_src, c_dst, c_sems, k)
-        copy = core_copy(c_dst, c_core, k)
-        copy.start()
-        core_copies.append(copy)
+    arrived(c_src, c_dst, c_sems, c_core, (2,))
     for k in range(1, split):
         sum_copies[k - 1].wait()
         resid = resid + arrive_ref[k - 1].astype(jnp.float32)
@@ -806,14 +838,12 @@
     second_copies = plane_copies(lambda to, k: second_ref.at[low], second_ref, second_sems, True)
     for copy in second_copies:
         copy.start()
-    for k in range(1, split):
-        line_arrived(d_src, d_dst, d_sems, k)
-        copy = core_copy(d_dst, d_core, k)
-        copy.start()
-        core_copies.append(copy)
+    arrived(d_src, d_dst, d_sems, d_core, (1, 3))
+    relay_inside(3)
+    arrived(d_src, d_dst, d_sems, d_core, (2,))
     for copy in second_copies + route_copies:
         copy.wait()
-    for copy in a_copies + b_copies + c_copies + d_copies + core_copies:
+    for copy in a_copies + b_copies + c_copies + d_copies + relays + core_copies:
         copy.wait_send()
     for dst_of, sems in ((c_dst, c_core), (d_dst, d_core)):
         for k in range(split):
@@ -854,7 +884,7 @@
     others = split - 1
     return pl.pallas_call(
         functools.partial(mixer_kernel, dt_rank, states, tap_count),
-        in_specs=[vmem, vmem, pl.BlockSpec(memory_space=pltpu.SMEM), vmem, vmem, anywhere, vmem],
+        in_specs=[vmem, vmem, pl.BlockSpec(memory_space=pltpu.SMEM), vmem, vmem, vmem, vmem],
         out_specs=[anywhere if i == 2 else vmem for i in range(len(outs))],
         out_shape=[jax.ShapeDtypeStruct(shape, kind) for shape, kind in outs],
         scratch_shapes=[
@@ -875,7 +905,7 @@
         + [dma((2, others))] * 4
         + [dma((2, split))] * 4
         + [dma((2, others))] * 5
-        + [dma((split,)), dma, dma((2, others, tiles)), dma((4,))],
+        + [dma((split,)), dma, dma((2, others, tiles)), dma],
         compiler_params=pltpu.CompilerParams(
             collective_id=3, has_side_effects=True, vmem_limit_bytes=60 << 20
         ),
@@ -900,17 +930,98 @@
     return probs, chosen, jnp.sum(probs * chosen, -1, keepdims=True)
 
 
-def scatter_copies(src_of, arrive_ref, sems):
-    core, high, low = kernel_place()
-    copies = []
-    for k in range(1, split):
-        to = lax.rem(high + k, split)
-        copies.append(
-            remote(
-                src_of(to), arrive_ref.at[k - 1], sems.at[0, k - 1], sems.at[1, k - 1], core, to, low
-            )
-        )
-    return copies
+class LineScatter:
+    def __init__(self, src_of, arrive_ref, sems):
+        core, high, low = kernel_place()
+        self.src_of, self.arrive, self.high = src_of, arrive_ref, high
+        relay = split
+
+        def send(src, to, slot, index):
+            return remote(src, arrive_ref.at[slot], sems.at[0, index], sems.at[1, slot], core, to, low)
+
+        def slot_at(to, sender):
+            return lax.rem(to - sender + split, split) - 1
+
+        way = 1 - 2 * (high // (split - 1))
+        near, mid, far = high + way, high + 2 * way, high + 3 * way
+        self.end_sends = [
+            send(src_of(far), near, relay, 0),
+            send(src_of(mid), mid, slot_at(mid, high), 1),
+            send(src_of(near), near, slot_at(near, high), 2),
+        ]
+        self.empty_slot = slot_at(high, far)
+        self.end_slots = [slot_at(high, near), slot_at(high, mid)]
+        beside, other = (split - 1) * (high - 1), split - 1 - high
+        self.far_end = split - 1 - beside
+        self.inner_sends = [
+            send(src_of(other), other, slot_at(other, high), 1),
+            send(src_of(beside), beside, slot_at(beside, high), 2),
+        ]
+        self.relay_send = send(arrive_ref.at[relay], self.far_end, slot_at(self.far_end, high), 0)
+        self.inner_slots = [0, 1, 2]
+        self.relay = relay
+        self.sems = sems
+
+    def landed(self, slot):
+        core, high, low = kernel_place()
+        remote(
+            self.arrive.at[slot], self.arrive.at[slot], self.sems.at[0, 0], self.sems.at[1, slot],
+            core, high, low,
+        ).wait_recv()
+
+    def start(self):
+        @pl.when(at_ends())
+        def _():
+            for copy in self.end_sends:
+                copy.start()
+            self.arrive[self.empty_slot] = jnp.zeros(self.arrive.shape[1:], self.arrive.dtype)
+
+        @pl.when(jnp.logical_not(at_ends()))
+        def _():
+            for copy in self.inner_sends:
+                copy.start()
+
+    def pass_on(self):
+        @pl.when(jnp.logical_not(at_ends()))
+        def _():
+            self.landed(self.relay)
+            own = self.src_of(self.far_end)
+            rows = self.arrive.shape[1]
+
+            def add(at):
+                here = pl.ds(at, 16)
+                total = self.arrive[self.relay, here].astype(jnp.float32)
+                total = total + own[here, :].astype(jnp.float32)
+                self.arrive[self.relay, here] = low_bits(total)
+
+            row_loop(rows, 16, add)
+            self.relay_send.start()
+
+    def finish(self, out_ref):
+        @pl.when(at_ends())
+        def _():
+            for copy in self.end_sends:
+                copy.wait_send()
+            for slot in self.end_slots:
+                self.landed(slot)
+
+        @pl.when(jnp.logical_not(at_ends()))
+        def _():
+            for copy in self.inner_sends + [self.relay_send]:
+                copy.wait_send()
+            for slot in self.inner_slots:
+                self.landed(slot)
+
+        own = self.src_of(self.high)
+
+        def one(at):
+            rows = pl.ds(at, 16)
+            total = own[rows, :].astype(jnp.float32)
+            for k in range(split - 1):
+                total = total + self.arrive[k, rows].astype(jnp.float32)
+            out_ref[rows, :] = total
+
+        row_loop(out_ref.shape[0], 16, one)
 
 
 def half_copy(src, dst, sems, h):
@@ -930,15 +1041,16 @@
 
 
 def turn_kernel(
-    dt_rank, states, expert_count, cut,
-    second_ref, routed_ref, hidden_ref, router_ref, resid_ref, grad_ref, gains_ref, lengths_ref,
+    dt_rank, states, expert_count,
+    second_ref, routed_ref, hidden_ref, last_ref, router_ref, resid_ref, grad_ref, gains_ref, lengths_ref,
     gate_ref, normed_ref, coef_ref, step_ref, z_ref, y_ref, gated_ref, rows_ref,
     mixed_out_ref, d_resid_ref, small_ref, dy_ref, gz_ref, later_ref, mine_ref, early_ref,
     gate_mine_ref,
     grads_ref, half_ref, y_sum_ref, d_sum_ref, dg_sum_ref, gates_ref, scaled_ref, act_ref, pre_ref,
-    part_ref, arrive_ref, y_part_ref, y_arrive_ref, branch_ref, out_ref, reset_ref, send_ref,
-    ends_ref, early_arrive_ref, gate_half_ref,
-    half_sems, sum_sems, y_sems, branch_sems, early_sems, ends_sems, gate_half_sems,
+    part_ref, arrive_ref, y_arrive_ref, branch_ref, out_ref, reset_ref, send_ref,
+    ends_ref, early_arrive_ref, gate_half_ref, down_ref, mine_early_ref, growth_ref,
+    half_sems, sum_sems, y_sems, branch_sems, early_sems, ends_sems, gate_half_sems, last_sems,
+    last_core,
 ):
     core, high, low = kernel_place()
     _, own_rows, model_width = second_ref.shape
@@ -946,7 +1058,8 @@
     steps = row_count // subs
     tiles = step_ref.shape[0]
     width = tiles * lanes
-    hidden = hidden_ref.shape[1] // (2 * expert_count)
+    hidden = last_ref.shape[0]
+    hidden_rows = 2 * expert_count * hidden
     channel_rows = width // (2 * split)
     greeted = greet_all()
     router = router_ref[...]
@@ -960,35 +1073,52 @@
     y_sum_ref[...] = jnp.zeros_like(y_sum_ref)
     d_sum_ref[...] = jnp.zeros_like(d_sum_ref)
     dg_sum_ref[...] = jnp.zeros_like(dg_sum_ref)
-    per_step = 2
-    span = per_step * hidden
-    column = lax.broadcasted_iota(jnp.int32, (1, expert_count * span), 1)
-    owner = jnp.zeros_like(column)
-    for e in range(1, expert_count):
-        owner = owner + (column >= e * span).astype(jnp.int32)
-    owner = owner.astype(jnp.float32)
-
-    def blocks_of(first):
-        def rows_of(part):
-            at = part * hidden
-            return hidden_ref[pl.ds(first, per_step), at : at + hidden].reshape(span, model_width)
-
-        up = jnp.concatenate([rows_of(e) for e in range(expert_count)], 0)
-        down = jnp.concatenate([rows_of(expert_count + e) for e in range(expert_count)], 0)
+    span = split * hidden
+
+    pl.semaphore_wait(pltpu.get_barrier_semaphore(), greeted)
+
+    def down_at(at):
+        return down_ref.at[at]
+
+    down_ref[high] = last_ref[...]
+    last_copies = line_copies(last_ref, down_at, last_sems)
+    last_relay = line_relay(down_at, last_sems)
+    own_copy = core_copy(down_at, last_core, 0)
+    for copy in last_copies + [own_copy]:
+        copy.start()
+    last_copies.append(own_copy)
+
+    @pl.when(at_ends())
+    def _():
+        last_relay.start()
+
+    def last_arrived(ks):
+        for k in ks:
+            line_arrived(last_ref, down_at, last_sems, k)
+            copy = core_copy(down_at, last_core, k)
+            copy.start()
+            last_copies.append(copy)
+
+    def blocks_of(e, first):
+        up = hidden_ref[first : first + split, 2 * e * hidden : (2 * e + 1) * hidden]
+        up = up.reshape(span, model_width)
+        if e < expert_count - 1:
+            down = hidden_ref[first : first + split, (2 * e + 1) * hidden : (2 * e + 2) * hidden]
+        else:
+            down = down_ref[first : first + split]
+        down = down.reshape(span, model_width)
 
         def token_block(l, _):
             at = pl.multiple_of(l * own_rows, own_rows)
             rows = pl.ds(at, own_rows)
             pre = matmul_nt(second_ref[l], up)
-            picked = routed_ref[l, :, model_width : model_width + 1].astype(jnp.float32) == owner
+            picked = routed_ref[l, :, model_width : model_width + 1].astype(jnp.float32) == e
             half = 0.5 + 0.5 * lax.erf(pre * (0.5**0.5))
             bell = jnp.exp(-0.5 * pre * pre) * (1.0 / (2.0 * math.pi) ** 0.5)
             act = low_bits(jnp.where(picked, pre * half, 0.0))
             d_raw = matmul_nt(routed_ref[l, :, :model_width], down)
             weighted = act.astype(jnp.float32) * d_raw
-            dg_sum_ref[rows, :] += sum(
-                weighted[:, c : c + lanes] for c in range(0, expert_count * span, lanes)
-            )
+            dg_sum_ref[rows, :] += sum(weighted[:, c : c + lanes] for c in range(0, span, lanes))
             d_pre = jnp.where(picked, gates_ref[rows, :1] * d_raw * (half + pre * bell), 0.0)
             d_pre = low_bits(d_pre)
             y_sum_ref[rows, :] += matmul(act, down)
@@ -999,49 +1129,82 @@
 
         lax.fori_loop(0, split, token_block, 0)
         second = second_ref[...].reshape(row_count, model_width)
-        for e in range(expert_count):
-            cols = slice(e * span, (e + 1) * span)
-            up_grad = low_bits(matmul_tn(pre_ref[:, cols], second))
-            down_grad = low_bits(matmul_tn(act_ref[:, cols], scaled_ref[...]))
-            for b in range(per_step):
-                piece = slice(b * hidden, (b + 1) * hidden)
-                grads_ref[first + b, e * hidden : (e + 1) * hidden] = up_grad[piece]
-                to = (expert_count + e) * hidden
-                grads_ref[first + b, to : to + hidden] = down_grad[piece]
-
-    lax.fori_loop(0, split // per_step, lambda i, _: (blocks_of(split + per_step * i), 0)[1], 0)
-    pl.semaphore_wait(pltpu.get_barrier_semaphore(), greeted)
-    half_copies = [
-        half_copy(grads_ref.at[split + h], half_ref.at[h], half_sems, h) for h in range(split)
-    ]
-    for copy in half_copies:
-        copy.start()
-    lax.fori_loop(0, split // per_step, lambda i, _: (blocks_of(per_step * i), 0)[1], 0)
+        up_grad = low_bits(matmul_tn(pre_ref[...], second))
+        down_grad = low_bits(matmul_tn(act_ref[...], scaled_ref[...]))
+        for b in range(split):
+            piece = slice(b * hidden, (b + 1) * hidden)
+            to = 2 * e * hidden
+            grads_ref[first + b, to : to + hidden] = up_grad[piece]
+            grads_ref[first + b, to + hidden : to + 2 * hidden] = down_grad[piece]
+
+    def part_of(e):
+        return pl.ds(2 * e * hidden, 2 * hidden)
+
+    half_copies = {}
+
+    def send_half(e):
+        half_copies[e] = [
+            half_copy(
+                grads_ref.at[split + h, part_of(e)],
+                half_ref.at[h, part_of(e)],
+                half_sems.at[e],
+                h,
+            )
+            for h in range(split)
+        ]
+        for copy in half_copies[e]:
+            copy.start()
+
+    def add_half(e):
+        for copy in half_copies[e]:
+            copy.wait()
+
+        target, base = (mine_early_ref, 0) if e == 0 else (mine_ref, 2 * (e - 1) * hidden)
+
+        def one(i, _):
+            h, at = i // (2 * hidden // 32), lax.rem(i, 2 * hidden // 32) * 32
+            rows = pl.ds(2 * e * hidden + at, 32)
+            target[h, pl.ds(base + at, 32)] = low_bits(
+                grads_ref[h, rows].astype(jnp.float32) + half_ref[h, rows].astype(jnp.float32)
+            )
+            return 0
+
+        lax.fori_loop(0, split * (2 * hidden // 32), one, 0)
+
+    early = LineScatter(lambda to: mine_early_ref.at[to], early_arrive_ref, early_sems)
+    for e in range(expert_count):
+        blocks_of(e, split)
+        send_half(e)
+        if e == 0:
+            last_arrived((1, 3))
+
+            @pl.when(jnp.logical_not(at_ends()))
+            def _():
+                last_relay.start()
+
+        blocks_of(e, 0)
+        if e == 0:
+            last_arrived((2,))
+            for k in range(split):
+                core_copy(down_at, last_core, k).wait_recv()
+            add_half(0)
+            early.start()
+    for copy in last_copies + [last_relay]:
+        copy.wait_send()
 
     sum_copies = plane_copies(lambda to, k: part_ref.at[k - 1], arrive_ref, sum_sems, False)
-    y_copies = plane_copies(lambda to, k: y_part_ref.at[k - 1], y_arrive_ref, y_sems, False)
+    y_copies = plane_copies(
+        lambda to, k: part_ref.at[k - 1, :, pl.ds(0, model_width)], y_arrive_ref, y_sems, False
+    )
     for k in range(1, split):
         to = pl.ds(pl.multiple_of(lax.rem(low + k, split) * own_rows, own_rows), own_rows)
         part_ref[k - 1, :, :model_width] = low_bits(d_sum_ref[to, :])
         part_ref[k - 1, :, model_width:] = low_bits(dg_sum_ref[to, :])
         sum_copies[k - 1].start()
-        y_part_ref[k - 1] = low_bits(y_sum_ref[to, :])
-
-    for h in range(split):
-        half_copies[h].wait()
-
-    def add_half(h, _):
-        mine_ref[h] = low_bits(
-            grads_ref[h].astype(jnp.float32) + half_ref[h].astype(jnp.float32)
-        )
-        return 0
-
-    lax.fori_loop(0, split, add_half, 0)
-    early_copies = scatter_copies(
-        lambda to: mine_ref.at[to, pl.ds(0, cut)], early_arrive_ref, early_sems
-    )
-    for copy in early_copies:
-        copy.start()
+
+    early.pass_on()
+    for e in range(1, expert_count):
+        add_half(e)
     own = pl.ds(pl.multiple_of(low * own_rows, own_rows), own_rows)
     d_second, dg_lanes = d_sum_ref[own, :], dg_sum_ref[own, :]
     for k in range(1, split):
@@ -1059,8 +1222,12 @@
     d_resid_ref[...] = d_resid
     branch_ref[low] = low_bits(d_resid)
     branch_copies = plane_copies(lambda to, k: branch_ref.at[low], branch_ref, branch_sems, True)
-    for copy in branch_copies + y_copies:
+    for copy in branch_copies:
         copy.start()
+    for k in range(1, split):
+        to = pl.ds(pl.multiple_of(lax.rem(low + k, split) * own_rows, own_rows), own_rows)
+        part_ref[k - 1, :, :model_width] = low_bits(y_sum_ref[to, :])
+        y_copies[k - 1].start()
     small_ref[...] = jnp.zeros_like(small_ref)
     small_ref[1:2, :] = jnp.sum(d_gain, 0, keepdims=True)
     small_ref[2 : 2 + expert_count, :] = matmul_tn(d_logits, second_own)[:expert_count]
@@ -1095,8 +1262,8 @@
             send_ref[j, n : n + 1] = grow[:1]
             send_ref[j, states + n : states + n + 1] = state[:1]
             has = row < subs - 1
-            later_ref[0, j, n] = jnp.where(has, pltpu.roll(grow, subs - 1, 0), 1.0)
-            later_ref[1, j, n] = jnp.where(has, pltpu.roll(state, subs - 1, 0), 0.0)
+            growth_ref[j, n] = jnp.where(has, pltpu.roll(grow, subs - 1, 0), 1.0)
+            later_ref[j, n] = jnp.where(has, pltpu.roll(state, subs - 1, 0), 0.0)
         for copy in ends_copies(send_ref, ends_ref, ends_sems, j, True):
             copy.start()
         return 0
@@ -1129,7 +1296,7 @@
         enter = chain_enter(ends_ref, j, states, True)
         for n in range(states):
             entered = jnp.broadcast_to(enter[n : n + 1, :], (subs, lanes))
-            later_ref[1, j, n] += later_ref[0, j, n] * entered
+            later_ref[j, n] += growth_ref[j, n] * entered
         return 0
 
     lax.fori_loop(0, tiles, settle, 0)
@@ -1147,23 +1314,21 @@
             gate_mine_ref[h, rows] = low_bits(total)
 
         row_loop(gate_rows, 16, add_gate)
-    early = mine_ref[high, :cut].astype(jnp.float32)
-    for k in range(1, split):
-        early_copies[k - 1].wait()
-        early = early + early_arrive_ref[k - 1].astype(jnp.float32)
-    early_ref[...] = early
+    early.finish(early_ref)
 
 
 def run_turn(
-    second, routed, hidden_full, router_lanes, resid, grad_out, gains, lengths, gate_full, normed,
-    coef, step, z, y, gated, rows, dt_rank, states, expert_count, cut,
+    second, routed, hidden_full, last_part, router_lanes, resid, grad_out, gains, lengths, gate_full, normed,
+    coef, step, z, y, gated, rows, dt_rank, states, expert_count,
 ):
     _, own_rows, model_width = second.shape
     row_count = own_rows * split
     steps = row_count // subs
     tiles = step.shape[0]
     width = tiles * lanes
-    hidden_rows = hidden_full.shape[1]
+    hidden = last_part.shape[0]
+    hidden_rows = 2 * expert_count * hidden
+    cut = 2 * hidden
     gate_rows = gate_full.shape[1]
     others = split - 1
     vmem = pl.BlockSpec(memory_space=pltpu.VMEM)
@@ -1175,15 +1340,15 @@
         ((8, model_width), f32),
         ((tiles, row_count, lanes), f32),
         ((row_count, width), bf16),
-        ((2, tiles, states, subs, lanes), f32),
-        ((split, hidden_rows, model_width), bf16),
+        ((tiles, states, subs, lanes), f32),
+        ((split, hidden_rows - cut, model_width), bf16),
         ((cut, model_width), f32),
         ((split, gate_rows, model_width), bf16),
     ]
-    span = 2 * hidden_rows // 2
+    span = split * hidden
     return pl.pallas_call(
-        functools.partial(turn_kernel, dt_rank, states, expert_count, cut),
-        in_specs=[pl.BlockSpec(memory_space=pltpu.SMEM) if i == 7 else vmem for i in range(16)],
+        functools.partial(turn_kernel, dt_rank, states, expert_count),
+        in_specs=[pl.BlockSpec(memory_space=pltpu.SMEM) if i == 8 else vmem for i in range(17)],
         out_specs=[vmem] * len(outs),
         out_shape=[jax.ShapeDtypeStruct(shape, kind) for shape, kind in outs],
         scratch_shapes=[
@@ -1199,44 +1364,48 @@
             pltpu.VMEM((others, own_rows, model_width + lanes), bf16),
             pltpu.VMEM((others, own_rows, model_width + lanes), bf16),
             pltpu.VMEM((others, own_rows, model_width), bf16),
-            pltpu.VMEM((others, own_rows, model_width), bf16),
             pltpu.VMEM((split, own_rows, model_width), bf16),
             pltpu.VMEM((steps, states, subs, lanes), f32),
             pltpu.VMEM((row_count, lanes), f32),
             pltpu.VMEM((tiles, 2 * states, lanes), f32),
             pltpu.VMEM((others, tiles, 2 * states, lanes), f32),
-            pltpu.VMEM((others, cut, model_width), bf16),
+            pltpu.VMEM((split + 1, cut, model_width), bf16),
             pltpu.VMEM((split, gate_rows, model_width), bf16),
-            dma((2, split)),
+            pltpu.VMEM((2 * split, hidden, model_width), bf16),
+            pltpu.VMEM((split, cut, model_width), bf16),
+            pltpu.VMEM((tiles, states, subs, lanes), f32),
+            dma((expert_count, 2, split)),
             dma((2, others)),
             dma((2, others)),
             dma((2, others)),
+            dma((2, split + 1)),
+            dma((2, others, tiles)),
+            dma((2, split)),
             dma((2, others)),
-            dma((2, others, tiles)),
             dma((2, split)),
         ],
         compiler_params=pltpu.CompilerParams(
-            collective_id=4, has_side_effects=True, vmem_limit_bytes=62 << 20
+            collective_id=4, has_side_effects=True, vmem_limit_bytes=63 << 20
         ),
         cost_estimate=pl.CostEstimate(flops=1000, bytes_accessed=1000, transcendentals=0),
     )(
-        second, routed, hidden_full, router_lanes, resid, grad_out, gains, lengths, gate_full, normed,
+        second, routed, hidden_full, last_part, router_lanes, resid, grad_out, gains, lengths, gate_full, normed,
         coef, step, z, y, gated, rows,
     )
 
 
 def back_kernel(
-    dt_rank, states, tap_count, cut,
+    dt_rank, states, tap_count,
     dy_ref, gz_ref, later_ref, mine_ref, gate_mine_ref, first_ref, gate_ref, normed_ref, input_ref,
     coef_ref, step_ref, start_ref, rows_ref, d_resid_ref, tokens_ref, gains_ref, small_ref,
     lengths_ref,
     grad_tokens_ref, total_ref, late_ref, gate_own_ref, first_own_ref,
     in_ref, out_ref, hist_ref, acc_in_ref, acc_out_ref, mixed_ref, conv_ref, q_ref, r_ref, reset_ref,
-    gdt_ref, gin_ref, dconv_ref, halo_ref, part_ref, arrive_ref, fold_ref, coef_send_ref,
+    gdt_ref, gin_ref, halo_ref, part_ref, arrive_ref, fold_ref, coef_send_ref,
     coef_arrive_ref, gcoef_ref, misc_ref, select_ref, payload_ref, half_ref, mine_first_ref,
     late_arrive_ref, gate_arrive_ref, first_arrive_ref, core_slots, plane_slots, line_slots,
     late_sems, gate_sems, first_sems, half_sems, halo_sems, coef_sems, sum_sems, core_sems,
-    plane_sems, line_sems, local_sems,
+    plane_sems, line_sems,
 ):
     core, high, low = kernel_place()
     _, own_rows, model_width = normed_ref.shape
@@ -1246,7 +1415,6 @@
     width = tiles * lanes
     channel_rows = width // (2 * split)
     edge = input_ref.shape[0] - row_count
-    late_rows = late_ref.shape[0]
     greeted = greet_all()
     first_len = lengths_ref[0, 0]
 
@@ -1256,20 +1424,9 @@
 
     fill_offsets(reset_ref, lengths_ref, row_count)
     pl.semaphore_wait(pltpu.get_barrier_semaphore(), greeted)
-    late_copies = scatter_copies(
-        lambda to: mine_ref.at[to, pl.ds(cut, late_rows)], late_arrive_ref, late_sems
-    )
-    gate_copies = scatter_copies(lambda to: gate_mine_ref.at[to], gate_arrive_ref, gate_sems)
-    local = [
-        pltpu.make_async_copy(
-            mine_ref.at[high, pl.ds(cut, late_rows)], late_arrive_ref.at[split - 1], local_sems.at[0]
-        ),
-        pltpu.make_async_copy(
-            gate_mine_ref.at[high], gate_arrive_ref.at[split - 1], local_sems.at[1]
-        ),
-    ]
-    for copy in local + late_copies:
-        copy.start()
+    late = LineScatter(lambda to: mine_ref.at[to], late_arrive_ref, late_sems)
+    gate = LineScatter(lambda to: gate_mine_ref.at[to], gate_arrive_ref, gate_sems)
+    late.start()
 
     def convolve(at):
         offset = offsets(at, 32)
@@ -1287,6 +1444,8 @@
     row_loop(row_count, 32, convolve)
     spread(coef_ref, dt_rank, in_ref, steps, states)
     spread(coef_ref, dt_rank + states, out_ref, steps, states)
+    late.pass_on()
+    gate.start()
     acc_in_ref[...] = jnp.zeros_like(acc_in_ref)
     acc_out_ref[...] = jnp.zeros_like(acc_out_ref)
     misc_ref[...] = jnp.zeros_like(misc_ref)
@@ -1339,7 +1498,7 @@
             return tuple(later_next), tuple(sums_next)
 
         zero = jnp.zeros((subs, lanes), jnp.float32)
-        later = tuple(later_ref[1, j, n] for n in range(states))
+        later = tuple(later_ref[j, n] for n in range(states))
         _, sums = lax.fori_loop(0, steps, backward, (later, (zero,) * states))
         for n in range(states):
             total = jnp.sum(sums[n] * rates[n], 0, keepdims=True) * (1.0 / log2e)
@@ -1388,6 +1547,7 @@
         coef_send_ref[rows, :] = low_bits(part)
 
     row_loop(row_count, 128, step_grads)
+    gate.pass_on()
     coef_copies = plane_copies(lambda to, k: coef_send_ref, coef_arrive_ref, coef_sems, False)
     for copy in coef_copies:
         copy.start()
@@ -1414,29 +1574,26 @@
             d_mixed = d_mixed + r_ref[j, rows, :] * step_ref[j, rows, :] + from_coef[:, cols]
             conv = conv_ref[j, rows, :]
             sig = sigmoid_of(conv)
-            dconv_ref[rows, cols] = d_mixed * (sig * (1.0 + conv * (1.0 - sig)))
+            q_ref[j, rows, :] = d_mixed * (sig * (1.0 + conv * (1.0 - sig)))
 
     row_loop(row_count, 128, conv_grads)
 
     def halo_copy():
         return remote(
-            dconv_ref.at[pl.ds(0, subs)], halo_ref, halo_sems.at[0], halo_sems.at[1],
+            q_ref.at[:, pl.ds(0, subs)], halo_ref, halo_sems.at[0], halo_sems.at[1],
             core, lax.rem(high + split - 1, split), low,
         )
 
     @pl.when(high > 0)
     def _():
         halo_copy().start()
-
-    for copy in gate_copies:
-        copy.start()
 
     def tap_grads(at):
         offset = offsets(at, 32)
         for j in range(tiles):
             cols = slice(j * lanes, (j + 1) * lanes)
             span = input_ref[pl.ds(at, 32 + edge), cols]
-            d_conv = dconv_ref[pl.ds(at, 32), cols]
+            d_conv = q_ref[j, pl.ds(at, 32), :]
             for k in range(tap_count):
                 shift = edge - (tap_count - 1) + k
                 term = jnp.where(offset >= tap_count - 1 - k, d_conv * span[shift : shift + 32], 0.0)
@@ -1447,17 +1604,17 @@
     @pl.when(high < split - 1)
     def _():
         halo_copy().wait_recv()
-        dconv_ref[row_count:, :] = halo_ref[...]
+        q_ref[:, row_count:, :] = halo_ref[...]
 
     @pl.when(high == split - 1)
     def _():
-        dconv_ref[row_count:, :] = jnp.zeros_like(halo_ref)
+        q_ref[:, row_count:, :] = jnp.zeros_like(halo_ref)
 
     def input_grads(at):
         masks = [offsets(at + m, 32) >= m for m in range(tap_count)]
         for j in range(tiles):
             cols = slice(j * lanes, (j + 1) * lanes)
-            span = dconv_ref[pl.ds(at, 32 + subs), cols]
+            span = q_ref[j, pl.ds(at, 32 + subs), :]
             d_input = jnp.zeros((32, lanes), jnp.float32)
             for m in range(tap_count):
                 k = tap_count - 1 - m
@@ -1473,11 +1630,6 @@
     def normed_block(l):
         rows = pl.ds(pl.multiple_of(l * own_rows, own_rows), own_rows)
         return matmul(gin_ref[rows, :], first_in) + matmul(gz_ref[rows, :], second_in)
-
-    sum_copies = plane_copies(lambda to, k: part_ref.at[k - 1], arrive_ref, sum_sems, False)
-    for k in range(1, split):
-        part_ref[k - 1] = low_bits(normed_block(lax.rem(low + k, split)))
-        sum_copies[k - 1].start()
 
     normed = normed_ref[...].reshape(row_count, model_width)
     for j in range(tiles):
@@ -1487,17 +1639,42 @@
         )
         payload_ref[rows, model_width + 2 * lanes :] = low_bits(misc_ref[j].T)
     half_width = width // 2
-    for at in (half_width, 0):
+    half = remote(
+        payload_ref.at[pl.ds(half_width, half_width)], half_ref, half_sems.at[0], half_sems.at[1],
+        1 - core, high, low,
+    )
+
+    def first_half(at):
         payload_ref[at : at + half_width, :model_width] = low_bits(
             matmul_tn(gin_ref[:, at : at + half_width], normed)
         )
-        if at:
-            half = remote(
-                payload_ref.at[pl.ds(half_width, half_width)], half_ref, half_sems.at[0],
-                half_sems.at[1], 1 - core, high, low,
-            )
-            half.start()
-    d_normed = normed_block(low)
+
+    first_half(half_width)
+    half.start()
+    sum_copies = plane_copies(lambda to, k: part_ref.at[k - 1], arrive_ref, sum_sems, False)
+    for k in range(1, split):
+        part_ref[k - 1] = low_bits(normed_block(lax.rem(low + k, split)))
+        sum_copies[k - 1].start()
+    first_half(0)
+    half.wait()
+
+    def add_half(at):
+        rows = pl.ds(at, 64)
+        both = payload_ref[rows, :].astype(jnp.float32) + half_ref[rows, :].astype(jnp.float32)
+        mine_first_ref[rows, :] = low_bits(both)
+
+    row_loop(half_width, 64, add_half)
+    first = LineScatter(
+        lambda to: mine_first_ref.at[pl.ds(pl.multiple_of(to * channel_rows, 16), channel_rows)],
+        first_arrive_ref,
+        first_sems,
+    )
+    first.start()
+    grad_tokens_ref[...] = normed_block(low)
+    late.finish(late_ref)
+    first.pass_on()
+    gate.finish(gate_own_ref)
+    d_normed = grad_tokens_ref[...]
     for k in range(1, split):
         sum_copies[k - 1].wait()
         d_normed = d_normed + arrive_ref[k - 1].astype(jnp.float32)
@@ -1511,14 +1688,6 @@
         core_slots.at[core], core_slots.at[core], core_sems.at[0], core_sems.at[1], 1 - core, high, low
     )
     hop.start()
-    half.wait()
-
-    def add_half(at):
-        rows = pl.ds(at, 64)
-        both = payload_ref[rows, :].astype(jnp.float32) + half_ref[rows, :].astype(jnp.float32)
-        mine_first_ref[rows, :] = low_bits(both)
-
-    row_loop(half_width, 64, add_half)
     hop.wait()
     plane_slots[low] = core_slots[0] + core_slots[1]
     plane = plane_copies(lambda to, k: plane_slots.at[low], plane_slots, plane_sems, True)
@@ -1527,52 +1696,25 @@
     for copy in plane:
         copy.wait()
     line_slots[high] = (plane_slots[0] + plane_slots[1]) + (plane_slots[2] + plane_slots[3])
-    line = line_copies(line_slots.at[high], lambda at: line_slots.at[at], line_sems)
+    line = line_copies(line_slots.at[high], lambda at: line_slots.at[at], line_sems, True)
     for copy in line:
         copy.start()
-    first_copies = scatter_copies(
-        lambda to: mine_first_ref.at[pl.ds(pl.multiple_of(to * channel_rows, 16), channel_rows)],
-        first_arrive_ref,
-        first_sems,
-    )
-    for copy in first_copies:
-        copy.start()
-
-    for copy in local:
-        copy.wait()
-    finish(late_copies, late_arrive_ref, late_ref)
-    finish(gate_copies, gate_arrive_ref, gate_own_ref)
+
     for k in range(1, split):
         line_arrived(line_slots.at[high], lambda at: line_slots.at[at], line_sems, k)
     for copy in line:
         copy.wait_send()
     total_ref[...] = (line_slots[0] + line_slots[1]) + (line_slots[2] + line_slots[3])
-    own = pl.ds(pl.multiple_of(high * channel_rows, 16), channel_rows)
-    first_arrive_ref[split - 1] = mine_first_ref[own, :]
-    finish(first_copies, first_arrive_ref, first_own_ref)
+    first.finish(first_own_ref)
 
     @pl.when(high > 0)
     def _():
         halo_copy().wait_send()
 
 
-def finish(copies, arrive_ref, out_ref):
-    for copy in copies:
-        copy.wait()
-
-    def one(at):
-        rows = pl.ds(at, 16)
-        total = arrive_ref[split - 1, rows].astype(jnp.float32)
-        for k in range(split - 1):
-            total = total + arrive_ref[k, rows].astype(jnp.float32)
-        out_ref[rows, :] = total
-
-    row_loop(out_ref.shape[0], 16, one)
-
-
 def run_back(
     dy, gz, later, mine, gate_mine, first_full, gate_full, normed, input_all, coef, step, start, rows,
-    d_resid, tokens, gains, small, lengths, dt_rank, states, tap_count, cut,
+    d_resid, tokens, gains, small, lengths, dt_rank, states, tap_count,
 ):
     _, own_rows, model_width = normed.shape
     row_count = own_rows * split
@@ -1581,12 +1723,11 @@
     width = tiles * lanes
     channel_rows = width // (2 * split)
     others = split - 1
-    late_rows = mine.shape[1] - cut
+    late_rows = mine.shape[1]
     gate_rows = gate_mine.shape[1]
     first_columns = first_full.shape[2]
     vmem = pl.BlockSpec(memory_space=pltpu.VMEM)
-    anywhere = pl.BlockSpec(memory_space=pl.ANY)
-    specs = [anywhere if i in (3, 4) else vmem for i in range(17)]
+    specs = [vmem] * 17
     specs.append(pl.BlockSpec(memory_space=pltpu.SMEM))
     f32, bf16 = jnp.float32, jnp.bfloat16
     dma = pltpu.SemaphoreType.DMA
@@ -1601,7 +1742,7 @@
     spreads = pltpu.VMEM((steps, states, subs, lanes), f32)
     summed = pltpu.VMEM((row_count, states * lanes), f32)
     return pl.pallas_call(
-        functools.partial(back_kernel, dt_rank, states, tap_count, cut),
+        functools.partial(back_kernel, dt_rank, states, tap_count),
         in_specs=specs,
         out_specs=[vmem] * len(outs),
         out_shape=[jax.ShapeDtypeStruct(shape, f32) for shape in outs],
@@ -1613,13 +1754,12 @@
             summed,
             tiled,
             tiled,
-            tiled,
+            pltpu.VMEM((tiles, row_count + subs, lanes), f32),
             tiled,
             pltpu.VMEM((row_count, lanes), f32),
             pltpu.VMEM((row_count, width), bf16),
             pltpu.VMEM((row_count, width), bf16),
-            pltpu.VMEM((row_count + subs, width), f32),
-            pltpu.VMEM((subs, width), f32),
+            pltpu.VMEM((tiles, subs, lanes), f32),
             pltpu.VMEM((others, own_rows, model_width), bf16),
             pltpu.VMEM((others, own_rows, model_width), bf16),
             pltpu.VMEM((row_count, lanes), f32),
@@ -1631,18 +1771,18 @@
             pltpu.VMEM((width, first_columns), bf16),
             pltpu.VMEM((width // 2, first_columns), bf16),
             pltpu.VMEM((width // 2, first_columns), bf16),
-            pltpu.VMEM((split, late_rows, model_width), bf16),
-            pltpu.VMEM((split, gate_rows, model_width), bf16),
-            pltpu.VMEM((split, channel_rows, first_columns), bf16),
+            pltpu.VMEM((split + 1, late_rows, model_width), bf16),
+            pltpu.VMEM((split + 1, gate_rows, model_width), bf16),
+            pltpu.VMEM((split + 1, channel_rows, first_columns), bf16),
             pltpu.VMEM((2, 8, model_width), f32),
             pltpu.VMEM((split, 8, model_width), f32),
             pltpu.VMEM((split, 8, model_width), f32),
         ]
-        + [dma((2, others))] * 3
+        + [dma((2, split + 1))] * 3
         + [dma((2,)), dma((2,)), dma((2, others)), dma((2, others)), dma((2,))]
-        + [dma((2, others)), dma((2, others)), dma((2,))],
+        + [dma((2, others)), dma((2, others))],
         compiler_params=pltpu.CompilerParams(
-            collective_id=5, has_side_effects=True, vmem_limit_bytes=62 << 20
+            collective_id=5, has_side_effects=True, vmem_limit_bytes=63 << 20
         ),
         cost_estimate=pl.CostEstimate(flops=1000, bytes_accessed=1000, transcendentals=0),
     )(
@@ -2138,9 +2278,10 @@
     b_part = jnp.concatenate(
         [pad_rows(in_weight[1], channel_rows), pad_rows(out_weight, channel_rows)], 0
     )
-    c_part = jnp.concatenate(
-        [expert_in.reshape(-1, model_width), expert_out.reshape(-1, model_width)], 0
-    )
+    c_parts = []
+    for e in range(expert_count):
+        c_parts += [expert_in[e], expert_out[e]]
+    c_part, last_part = jnp.concatenate(c_parts[:-1], 0), c_parts[-1]
     g_part = low_bits(
         jnp.concatenate(
             [grad_out, routes[:, None].astype(jnp.float32) * jnp.ones((1, lanes), jnp.float32)], 1
@@ -2152,17 +2293,16 @@
     ) = run_mixer(
         tokens, norm_gains, lengths, a_part, b_part, c_part, g_part, dt_rank, states, tap_count
     )
-    cut = hidden_rows * 2 // 3
     router_lanes = jnp.pad(router, ((0, 0), (0, lanes - expert_count)))
     mixed_out, d_resid, small_sums, dy, gz, later, mine, early, gate_mine = run_turn(
-        second, routed, hidden_full, router_lanes, resid, grad_out, norm_gains, lengths, gate_full,
-        normed, coef, step, z, y, gated, rows, dt_rank, states, expert_count, cut,
+        second, routed, hidden_full, last_part, router_lanes, resid, grad_out, norm_gains, lengths, gate_full,
+        normed, coef, step, z, y, gated, rows, dt_rank, states, expert_count,
     )
     grad_tokens, sums, late, gate_own, first_own = run_back(
         dy, gz, later, mine, gate_mine, first_full, gate_full, normed, input_all, coef, step, start,
-        rows, d_resid, tokens, norm_gains, small_sums, lengths, dt_rank, states, tap_count, cut,
-    )
-    hidden_own = jnp.concatenate([early, late], 0)
+        rows, d_resid, tokens, norm_gains, small_sums, lengths, dt_rank, states, tap_count,
+    )
+    hidden_own = jnp.concatenate([early, late], 0).reshape(expert_count, 2, hidden, model_width)
     first_own, gate_first = first_own[:channels], gate_own[:channels]
     misc = first_own[:, model_width + 2 * lanes :]
     return (
@@ -2178,8 +2318,8 @@
         misc[:, alog_row : alog_row + states],
         misc[:, skip_row],
         gate_own[channel_rows : channel_rows + channels],
-        hidden_own[:hidden_rows].reshape(expert_count, hidden, model_width),
-        hidden_own[hidden_rows:].reshape(expert_count, hidden, model_width),
+        hidden_own[:, 0],
+        hidden_own[:, 1],
     )
 
 

time: 383 us -> 328 us (0.86)
  Pallas kernels: 357 us -> 304 us
    pallas_call x1, Pallas kernels: 162 us -> 119 us  [run_mixer(): pl.pallas_call(functools.partial(mixer_kernel, dt_rank, states, tap_count...]
    pallas_call x1, Pallas kernels: 113 us -> 92.1 us  [run_back(): pl.pallas_call(functools.partial(back_kernel, dt_rank, states, tap_count)...]
    pallas_call x1, Pallas kernels: 81.9 us -> 93 us  [run_turn(): pl.pallas_call(functools.partial(turn_kernel, dt_rank, states, expert_cou...]
where the time goes in v3:
time: 328 us
  Pallas kernels  304 us (93%)
  local copies, waits for them, and re-layouts  18.2 us (6%)
  other arithmetic  4.23 us (1%)
    pallas_call x1, Pallas kernels, run_mixer(): pl.pallas_call(functools.partial(mixer_kernel, dt_rank, states, tap_count...  119 us
    pallas_call x1, Pallas kernels, run_turn(): pl.pallas_call(functools.partial(turn_kernel, dt_rank, states, expert_cou...  93 us
    pallas_call x1, Pallas kernels, run_back(): pl.pallas_call(functools.partial(back_kernel, dt_rank, states, tap_count)...  92.1 us

profile of v3, /device:TPU:0, one launch (start us, length us, event | category | flops | bytes accessed | tf_op | source)
XLA Modules:
  0.0 327.7 jit_solution(4707342703418666777)
XLA Ops:
  0.7 0.7 convert_convert_fusion
  1.4 1.4 concatenate.19
  3.0 0.9 copy.49
  3.9 0.8 pad.33.router_ref
  4.8 0.8 pad_maximum_fusion.3.g_ref
  5.6 0.8 fusion.7.b_ref
  6.4 0.7 pad.30.a_ref
  7.1 0.8 slice_bitcast_fusion.4
  7.9 0.9 pad_maximum_fusion.1.c_ref
  8.7 119.3 %shard_map.263 = (bf16[8,80,1536]{2,1,0:T(8,128)(2,1)}, bf16[8,160,1152]{2,1,0:T(8,128)(2,1)}, bf16[8,288,1152]{2,1,0:T(8,128)(2,1)}, bf16[4,128,1152]{2,1,0:T(8...) custom-call(bf16[128,1152]{1,0:T(8,128)(2,1)} %tokens_ref.3, ...), custom_call_target="tpu_custom_call" | custom-call | flops 1000 | bytes 1000 | tf_op jit(solution)/shard_map/pallas_call | solution.py:885
  128.1 93.0 %shard_map.264 = (bf16[128,1152]{1,0:T(8,128)(2,1)}, f32[128,1152]{1,0:T(8,128)}, f32[8,1152]{1,0:T(8,128)}, f32[5,512,128]{2,1,0:T(8,128)}, bf16[512,640]{1,0:T...) custom-call(bf16[4,128,1152]{2,1,0:T(8,128)(2,1)} %get-tuple-element, ...), custom_call_target="tpu_custom_call" | custom-call | flops 1000 | bytes 1000 | tf_op jit(solution)/shard_map/pallas_call | solution.py:1349
  221.1 92.1 %shard_map.265 = (f32[128,1152]{1,0:T(8,128)}, f32[8,1152]{1,0:T(8,128)}, f32[192,1152]{1,0:T(8,128)}, f32[160,1152]{1,0:T(8,128)}, f32[80,1536]{1,0:T(8,128)}) custom-call(f32[5,512,128]{2,1,0:T(8,128)} %get-tuple-element.56.dy_ref, bf16[512,640]{1,0:T(8,128)(2,1)} %get-tuple-element.57.gz_ref, f32[5,16,8,128]{3,2,1,0:T(8,128)} %get-tuple-element.58.later_ref, ...), custom_call_target="tpu_custom_call" | custom-call | flops 1000 | bytes 1000 | tf_op jit(solution)/shard_map/pallas_call | solution.py:1744
  313.2 1.6 slice_reduce_fusion
  314.8 1.5 slice_bitcast_fusion.10
  316.3 0.8 slice.81
  317.8 1.4 slice.79
  319.2 1.4 slice.78
  320.5 0.8 slice.77
  321.3 1.0 slice_bitcast_fusion.3
  323.0 0.8 fusion.11
  323.7 0.9 pad_maximum_fusion.2
  324.8 1.3 slice_bitcast_fusion
  326.1 0.7 copy.58
  326.9 0.8 copy.59
  (33 shorter events, 1.8 us)
Async XLA Ops:
  0.6 4.1 %copy-start = (f32[128,1152]{1,0:T(8,128)S(1)}, f32[128,1152]{1,0:T(8,128)}, u32[]{:S(2)}) copy-start(f32[128,1152]{1,0:T(8,128)} %grad_ref.1) | copy-start | bytes 1769476
  0.7 4.9 %copy-start.7 = (bf16[2,72,1152]{2,1,0:T(8,128)(2,1)S(1)}, bf16[2,72,1152]{2,1,0:T(8,128)(2,1)}, u32[]{:S(2)}) copy-start(bf16[2,72,1152]{2,1,0:T(8,128)(2,1)} %param.22) | copy-start | bytes 995332
  3.9 1.6 copy-start.9
  4.7 1.6 copy-start.10
  4.7 1.6 copy-start.11
  4.8 2.3 copy-start.5
  4.8 2.3 copy-start.6
  313.2 9.8 %copy-start.3 = (f32[160,1152]{1,0:T(8,128)S(1)}, f32[160,1152]{1,0:T(8,128)}, u32[]{:S(2)}) copy-start(f32[160,1152]{1,0:T(8,128)} %get-tuple-element.69) | copy-start | bytes 2211844
  323.0 1.7 copy-start.1
  323.0 1.7 copy-start.2
  324.8 1.3 copy-start.8
  324.8 2.1 copy-start.4

commit v4 on v3

--- a/solution.py
+++ b/solution.py
@@ -542,9 +542,13 @@
 
 def mixer_kernel(
     dt_rank, states, tap_count,
-    tokens_ref, gains_ref, lengths_ref, a_ref, b_ref, c_ref, g_ref,
-    first_ref, gate_ref, hidden_ref, normed_ref, edge_ref, routed_ref, input_ref, coef_ref,
-    step_ref, z_ref, y_ref, gated_ref, start_ref, resid_ref, second_ref, rows_ref,
+    tokens_ref, gains_ref, lengths_ref, in_weight_ref, conv_weight_ref, x_weight_ref, dt_weight_ref,
+    dt_bias_ref, a_log_ref, skip_ref, out_weight_ref, expert_in_ref, expert_out_ref, grad_ref,
+    routes_ref,
+    first_out, gate_out, hidden_ref, normed_out, routed_out, input_out, coef_out, step_out, z_out,
+    y_out, gated_out, start_out, resid_ref, second_out, rows_out, in_out, out_out,
+    first_ref, gate_ref, normed_ref, edge_ref, routed_ref, input_ref, coef_ref, step_ref, z_ref,
+    y_ref, gated_ref, start_ref, second_ref, rows_ref, c_ref, out_sems,
     in_ref, out_ref, drive_ref, reset_ref, mixed_ref, partial_ref, arrive_ref, coef_send_ref,
     coef_arrive_ref, send_ref, ends_ref, grow_ref, state_ref,
     a_sems, b_sems, c_sems, d_sems, a_core, b_core, c_core, d_core, token_sems, route_sems,
@@ -558,7 +562,15 @@
     width = tiles * lanes
     edge = edge_ref.shape[0]
     first_b, first_c = dt_rank, dt_rank + states
+    channels = in_weight_ref.shape[1]
+    channel_rows = width // (2 * split)
     greeted = greet_all()
+    stores = []
+
+    def store(ref, out):
+        copy = pltpu.make_async_copy(ref, out, out_sems.at[len(stores)])
+        copy.start()
+        stores.append(copy)
 
     def edge_copy(l):
         return remote(
@@ -582,11 +594,30 @@
     greeted += split - 1
     tokens = tokens_ref[...].astype(jnp.float32)
     normed_ref[low] = low_bits(norm_rows(tokens, gains_ref[0:1, :]))
-    local = pltpu.make_async_copy(c_ref, hidden_ref.at[high], local_sem)
-    local.start()
-    first_ref[high] = a_ref[...]
-    gate_ref[high] = b_ref[...]
-    routed_ref[low] = g_ref[...]
+    gap = channel_rows - channels
+
+    def filled(value):
+        value = value.astype(jnp.float32)
+        if gap:
+            value = jnp.concatenate([value, jnp.zeros((gap, value.shape[1]), jnp.float32)], 0)
+        return low_bits(value)
+
+    def widened(value, first):
+        at = lax.broadcasted_iota(jnp.int32, (value.shape[1], lanes), 0) + first
+        to = lax.broadcasted_iota(jnp.int32, (value.shape[1], lanes), 1)
+        return matmul(value, jnp.where(at == to, 1.0, 0.0).astype(jnp.bfloat16))
+
+    first_ref[high, :, :model_width] = filled(in_weight_ref[0])
+    first_ref[high, :, model_width : model_width + lanes] = filled(widened(x_weight_ref[...], 0))
+    first_ref[high, :, model_width + lanes : model_width + 2 * lanes] = filled(
+        widened(dt_weight_ref[...], 0)
+    )
+    rows_ref[0] = jnp.zeros((lanes, lanes), jnp.float32)
+    for row, ref in (
+        (0, conv_weight_ref), (bias_row, dt_bias_ref), (skip_row, skip_ref), (alog_row, a_log_ref)
+    ):
+        rows_ref[0, row : row + ref.shape[0], :channels] = ref[...].astype(jnp.float32)
+    first_ref[high, :, model_width + 2 * lanes :] = filled(rows_ref[0].T[:channels])
     pl.semaphore_wait(barrier, greeted)
 
     @pl.when((low == split - 1) & (high < split - 1))
@@ -597,6 +628,7 @@
     hidden_count = c_ref.shape[0]
     c_src = c_ref.at[pl.ds(0, early_hidden)]
     d_src = c_ref.at[pl.ds(early_hidden, hidden_count - early_hidden)]
+    a_ref, b_ref, g_ref = first_ref.at[high], gate_ref.at[high], routed_ref.at[low]
 
     def a_dst(at):
         return first_ref.at[at]
@@ -618,7 +650,7 @@
     route_copies = plane_copies(lambda to, k: g_ref, routed_ref, route_sems, True)
     relays = [line_relay(a_dst, a_sems), line_relay(b_dst, b_sems)]
     relays += [line_relay(c_dst, c_sems), line_relay(d_dst, d_sems)]
-    for copy in token_copies + a_copies + route_copies:
+    for copy in token_copies + a_copies:
         copy.start()
 
     def relay_from_end(i):
@@ -639,8 +671,21 @@
             core_copies.append(copy)
 
     relay_from_end(0)
-    core_copies = [core_copy(a_dst, a_core, 0), core_copy(b_dst, b_core, 0)]
-    for copy in core_copies:
+    core_copies = [core_copy(a_dst, a_core, 0)]
+    core_copies[0].start()
+    routed_ref[low, :, :model_width] = low_bits(grad_ref[...])
+    routes = jnp.broadcast_to(routes_ref[...].astype(jnp.float32), (own_rows, own_rows)).T
+    routed_ref[low, :, model_width:] = low_bits(routes)
+    gate_ref[high, :channel_rows] = filled(in_weight_ref[1])
+    gate_ref[high, channel_rows:] = filled(out_weight_ref[...])
+    hidden = expert_in_ref.shape[1]
+    for part in range(hidden_count // hidden):
+        source = expert_out_ref if part % 2 else expert_in_ref
+        c_ref[part * hidden : (part + 1) * hidden] = source[part // 2]
+    local = pltpu.make_async_copy(c_ref, hidden_ref.at[high], local_sem)
+    local.start()
+    core_copies.append(core_copy(b_dst, b_core, 0))
+    for copy in core_copies[1:] + route_copies:
         copy.start()
 
     first_len = lengths_ref[0, 0]
@@ -684,9 +729,14 @@
     for l in range(split):
         block = low_bits(matmul_nt(normed_ref[l], weights)).astype(jnp.float32)
         input_ref[edge + l * own_rows : edge + (l + 1) * own_rows, :] = block
+    store(first_ref, first_out)
+    store(normed_ref, normed_out)
+    store(input_ref, input_out)
     small = first_ref[:, :, model_width + 2 * lanes :].reshape(width, lanes).astype(jnp.float32)
     for j in range(tiles):
         rows_ref[j] = small[j * lanes : (j + 1) * lanes].T
+
+    store(rows_ref, rows_out)
 
     def convolve(at):
         offset = offsets(at, 32)
@@ -738,7 +788,10 @@
             )
 
     row_loop(row_count, 128, step_sizes)
+    store(coef_ref, coef_out)
+    store(step_ref, step_out)
     spread(coef_ref, first_b, in_ref, steps, states)
+    store(in_ref, in_out)
 
     def rates_of(j):
         values = -jnp.exp(rows_ref[j, alog_row : alog_row + states, :]) * log2e
@@ -764,6 +817,7 @@
         copy.start()
     relay_from_end(3)
     spread(coef_ref, first_c, out_ref, steps, states)
+    store(out_ref, out_out)
     arrived(b_ref, b_dst, b_sems, b_core, (2,))
     row = lax.broadcasted_iota(jnp.int32, (subs, lanes), 0)
 
@@ -800,7 +854,8 @@
 
     for k in range(split):
         core_copy(b_dst, b_core, k).wait_recv()
-    channel_rows = width // (2 * split)
+    store(gate_ref, gate_out)
+    store(start_ref, start_out)
     second_in = gate_ref[:, :channel_rows].reshape(width, model_width)
     for l in range(split):
         z_block = matmul_nt(normed_ref[l], second_in)
@@ -818,6 +873,9 @@
             gated_ref[pl.ds(at, 32), cols] = low_bits(y * z * sigmoid_of(z))
 
     row_loop(row_count, 32, gate)
+    store(z_ref, z_out)
+    store(y_ref, y_out)
+    store(gated_ref, gated_out)
     out_full = gate_ref[:, channel_rows:].reshape(width, model_width)
 
     def out_block(l):
@@ -843,51 +901,63 @@
     arrived(d_src, d_dst, d_sems, d_core, (2,))
     for copy in second_copies + route_copies:
         copy.wait()
+    store(second_ref, second_out)
+    store(routed_ref, routed_out)
     for copy in a_copies + b_copies + c_copies + d_copies + relays + core_copies:
         copy.wait_send()
     for dst_of, sems in ((c_dst, c_core), (d_dst, d_core)):
         for k in range(split):
             core_copy(dst_of, sems, k).wait_recv()
-
-
-def run_mixer(tokens, gains, lengths, a_part, b_part, c_part, g_part, dt_rank, states, tap_count):
+    for copy in stores:
+        copy.wait()
+
+
+def run_mixer(
+    tokens, gains, lengths, in_weight, conv_weight, x_weight, dt_weight, dt_bias, a_log, skip_gain,
+    out_weight, expert_in, expert_out, grad_out, routes,
+):
     own_rows, model_width = tokens.shape
+    tap_count, channels = conv_weight.shape
+    dt_rank, states = dt_weight.shape[1], a_log.shape[0]
+    expert_count, hidden, _ = expert_in.shape
     row_count = own_rows * split
     steps = row_count // subs
     blocks = 2 * split
-    width = blocks * a_part.shape[0]
+    channel_rows = -(-channels // 16) * 16
+    width = blocks * channel_rows
     tiles = width // lanes
     vmem = pl.BlockSpec(memory_space=pltpu.VMEM)
     anywhere = pl.BlockSpec(memory_space=pl.ANY)
     f32, bf16 = jnp.float32, jnp.bfloat16
     tiled = (tiles, row_count, lanes)
-    outs = [
-        ((blocks,) + a_part.shape, bf16),
-        ((blocks,) + b_part.shape, bf16),
-        ((blocks,) + c_part.shape, bf16),
-        ((split, own_rows, model_width), bf16),
-        ((16, model_width), bf16),
-        ((split,) + g_part.shape, bf16),
-        ((row_count + 16, width), f32),
-        ((row_count, lanes), f32),
-        (tiled, f32),
-        (tiled, f32),
-        (tiled, f32),
-        ((row_count, width), bf16),
-        ((tiles, states, subs, lanes), f32),
-        ((own_rows, model_width), f32),
-        ((split, own_rows, model_width), bf16),
-        ((tiles, lanes, lanes), f32),
-    ]
+    hidden_part = ((2 * expert_count - 1) * hidden, model_width)
+    first = ((blocks, channel_rows, model_width + 3 * lanes), bf16)
+    gate = ((blocks, 2 * channel_rows, model_width), bf16)
+    normed = ((split, own_rows, model_width), bf16)
+    edge = ((16, model_width), bf16)
+    routed = ((split, own_rows, model_width + lanes), bf16)
+    inputs = ((row_count + 16, width), f32)
+    coef = ((row_count, lanes), f32)
+    gated = ((row_count, width), bf16)
+    start = ((tiles, states, subs, lanes), f32)
+    resid = ((own_rows, model_width), f32)
+    rows = ((tiles, lanes, lanes), f32)
+    kept = [first, gate, normed, edge, routed, inputs, coef, (tiled, f32), (tiled, f32)]
+    kept += [(tiled, f32), gated, start, normed, rows, (hidden_part, bf16)]
+    outs = [first, gate, ((blocks,) + hidden_part, bf16), normed, routed, inputs, coef]
+    spread_out = ((steps, states, subs, lanes), f32)
+    outs += [(tiled, f32)] * 3 + [gated, start, resid, normed, rows, spread_out, spread_out]
     spreads = pltpu.VMEM((steps, states, subs, lanes), f32)
     dma = pltpu.SemaphoreType.DMA
     others = split - 1
     return pl.pallas_call(
         functools.partial(mixer_kernel, dt_rank, states, tap_count),
-        in_specs=[vmem, vmem, pl.BlockSpec(memory_space=pltpu.SMEM), vmem, vmem, vmem, vmem],
-        out_specs=[anywhere if i == 2 else vmem for i in range(len(outs))],
+        in_specs=[pl.BlockSpec(memory_space=pltpu.SMEM) if i == 2 else vmem for i in range(15)],
+        out_specs=[vmem if i == 12 else anywhere for i in range(len(outs))],
         out_shape=[jax.ShapeDtypeStruct(shape, kind) for shape, kind in outs],
-        scratch_shapes=[
+        scratch_shapes=[pltpu.VMEM(shape, kind) for shape, kind in kept]
+        + [dma((len(outs),))]
+        + [
             spreads,
             spreads,
             pltpu.VMEM(tiled, f32),
@@ -910,7 +980,10 @@
             collective_id=3, has_side_effects=True, vmem_limit_bytes=60 << 20
         ),
         cost_estimate=pl.CostEstimate(flops=1000, bytes_accessed=1000, transcendentals=0),
-    )(tokens, gains, lengths, a_part, b_part, c_part, g_part)
+    )(
+        tokens, gains, lengths, in_weight, conv_weight, x_weight, dt_weight, dt_bias, a_log, skip_gain,
+        out_weight, expert_in, expert_out, grad_out, routes,
+    )
 
 
 def norm_back(values, gain_row, grads):
@@ -921,7 +994,7 @@
 
 
 def route_probs(rows, router, route_lanes, expert_count):
-    logits = matmul(rows, router)
+    logits = matmul_nt(rows, router)
     lane = lax.broadcasted_iota(jnp.int32, logits.shape, 1)
     logits = jnp.where(lane < expert_count, logits, -1e30)
     powers = jnp.exp(logits - jnp.max(logits, -1, keepdims=True))
@@ -1041,13 +1114,16 @@
 
 
 def turn_kernel(
-    dt_rank, states, expert_count,
-    second_ref, routed_ref, hidden_ref, last_ref, router_ref, resid_ref, grad_ref, gains_ref, lengths_ref,
-    gate_ref, normed_ref, coef_ref, step_ref, z_ref, y_ref, gated_ref, rows_ref,
-    mixed_out_ref, d_resid_ref, small_ref, dy_ref, gz_ref, later_ref, mine_ref, early_ref,
+    states, expert_count,
+    second_ref, routed_ref, hidden_hbm, weights_ref, router_ref, resid_ref, grad_ref, gains_ref,
+    lengths_ref,
+    gate_hbm, normed_hbm, out_hbm, step_hbm, z_hbm, y_hbm, gated_hbm, rows_hbm,
+    mixed_out_ref, d_resid_ref, small_ref, dy_out, gz_out, later_ref, mine_out, early_ref,
     gate_mine_ref,
+    hidden_ref, gate_ref, normed_ref, out_ref, step_ref, z_ref, y_ref, gated_ref, rows_ref, dy_ref,
+    gz_ref, mine_ref, load_sems, store_sems,
     grads_ref, half_ref, y_sum_ref, d_sum_ref, dg_sum_ref, gates_ref, scaled_ref, act_ref, pre_ref,
-    part_ref, arrive_ref, y_arrive_ref, branch_ref, out_ref, reset_ref, send_ref,
+    part_ref, arrive_ref, y_arrive_ref, branch_ref, reset_ref, send_ref,
     ends_ref, early_arrive_ref, gate_half_ref, down_ref, mine_early_ref, growth_ref,
     half_sems, sum_sems, y_sems, branch_sems, early_sems, ends_sems, gate_half_sems, last_sems,
     last_core,
@@ -1058,11 +1134,38 @@
     steps = row_count // subs
     tiles = step_ref.shape[0]
     width = tiles * lanes
-    hidden = last_ref.shape[0]
+    loads = [
+        pltpu.make_async_copy(source, target, load_sems.at[i])
+        for i, (source, target) in enumerate(
+            (
+                (hidden_hbm, hidden_ref),
+                (gate_hbm, gate_ref),
+                (z_hbm, z_ref),
+                (y_hbm, y_ref),
+                (step_hbm, step_ref),
+                (rows_hbm, rows_ref),
+                (out_hbm, out_ref),
+                (normed_hbm, normed_ref),
+                (gated_hbm, gated_ref),
+            )
+        )
+    ]
+    for copy in loads:
+        copy.start()
+    stores = [
+        pltpu.make_async_copy(source, target, store_sems.at[i])
+        for i, (source, target) in enumerate(((dy_ref, dy_out), (gz_ref, gz_out), (mine_ref, mine_out)))
+    ]
+    hidden = weights_ref.shape[1]
+    last_ref = weights_ref.at[expert_count - 1]
     hidden_rows = 2 * expert_count * hidden
     channel_rows = width // (2 * split)
     greeted = greet_all()
-    router = router_ref[...]
+    at = lax.broadcasted_iota(jnp.int32, (lanes, expert_count), 0)
+    to = lax.broadcasted_iota(jnp.int32, (lanes, expert_count), 1)
+    router = low_bits(
+        matmul(jnp.where(at == to, 1.0, 0.0).astype(jnp.bfloat16), router_ref[...])
+    )
 
     for l in range(split):
         rows = slice(l * own_rows, (l + 1) * own_rows)
@@ -1077,6 +1180,8 @@
 
     pl.semaphore_wait(pltpu.get_barrier_semaphore(), greeted)
 
+    loads[0].wait()
+
     def down_at(at):
         return down_ref.at[at]
 
@@ -1099,38 +1204,39 @@
             copy.start()
             last_copies.append(copy)
 
-    def blocks_of(e, first):
+    def halves_of(e, first):
         up = hidden_ref[first : first + split, 2 * e * hidden : (2 * e + 1) * hidden]
         up = up.reshape(span, model_width)
         if e < expert_count - 1:
             down = hidden_ref[first : first + split, (2 * e + 1) * hidden : (2 * e + 2) * hidden]
         else:
             down = down_ref[first : first + split]
-        down = down.reshape(span, model_width)
-
-        def token_block(l, _):
-            at = pl.multiple_of(l * own_rows, own_rows)
-            rows = pl.ds(at, own_rows)
-            pre = matmul_nt(second_ref[l], up)
-            picked = routed_ref[l, :, model_width : model_width + 1].astype(jnp.float32) == e
-            half = 0.5 + 0.5 * lax.erf(pre * (0.5**0.5))
-            bell = jnp.exp(-0.5 * pre * pre) * (1.0 / (2.0 * math.pi) ** 0.5)
-            act = low_bits(jnp.where(picked, pre * half, 0.0))
-            d_raw = matmul_nt(routed_ref[l, :, :model_width], down)
-            weighted = act.astype(jnp.float32) * d_raw
-            dg_sum_ref[rows, :] += sum(weighted[:, c : c + lanes] for c in range(0, span, lanes))
-            d_pre = jnp.where(picked, gates_ref[rows, :1] * d_raw * (half + pre * bell), 0.0)
-            d_pre = low_bits(d_pre)
-            y_sum_ref[rows, :] += matmul(act, down)
-            d_sum_ref[rows, :] += matmul(d_pre, up)
-            act_ref[rows, :] = act
-            pre_ref[rows, :] = d_pre
-            return 0
-
-        lax.fori_loop(0, split, token_block, 0)
+        return up, down.reshape(span, model_width)
+
+    def token_block(e, first, l):
+        up, down = halves_of(e, first)
+        cols = slice(0, span) if first else slice(span, 2 * span)
+        rows = pl.ds(pl.multiple_of(l * own_rows, own_rows), own_rows)
+        pre = matmul_nt(second_ref[l], up)
+        picked = routed_ref[l, :, model_width : model_width + 1].astype(jnp.float32) == e
+        half = 0.5 + 0.5 * lax.erf(pre * (0.5**0.5))
+        bell = jnp.exp(-0.5 * pre * pre) * (1.0 / (2.0 * math.pi) ** 0.5)
+        act = low_bits(jnp.where(picked, pre * half, 0.0))
+        d_raw = matmul_nt(routed_ref[l, :, :model_width], down)
+        weighted = act.astype(jnp.float32) * d_raw
+        dg_sum_ref[rows, :] += sum(weighted[:, c : c + lanes] for c in range(0, span, lanes))
+        d_pre = jnp.where(picked, gates_ref[rows, :1] * d_raw * (half + pre * bell), 0.0)
+        d_pre = low_bits(d_pre)
+        y_sum_ref[rows, :] += matmul(act, down)
+        d_sum_ref[rows, :] += matmul(d_pre, up)
+        act_ref[rows, cols] = act
+        pre_ref[rows, cols] = d_pre
+
+    def weight_grads(e, first):
+        cols = slice(0, span) if first else slice(span, 2 * span)
         second = second_ref[...].reshape(row_count, model_width)
-        up_grad = low_bits(matmul_tn(pre_ref[...], second))
-        down_grad = low_bits(matmul_tn(act_ref[...], scaled_ref[...]))
+        up_grad = low_bits(matmul_tn(pre_ref[:, cols], second))
+        down_grad = low_bits(matmul_tn(act_ref[:, cols], scaled_ref[...]))
         for b in range(split):
             piece = slice(b * hidden, (b + 1) * hidden)
             to = 2 * e * hidden
@@ -1172,43 +1278,62 @@
         lax.fori_loop(0, split * (2 * hidden // 32), one, 0)
 
     early = LineScatter(lambda to: mine_early_ref.at[to], early_arrive_ref, early_sems)
-    for e in range(expert_count):
-        blocks_of(e, split)
-        send_half(e)
-        if e == 0:
-            last_arrived((1, 3))
-
-            @pl.when(jnp.logical_not(at_ends()))
-            def _():
-                last_relay.start()
-
-        blocks_of(e, 0)
-        if e == 0:
-            last_arrived((2,))
-            for k in range(split):
-                core_copy(down_at, last_core, k).wait_recv()
-            add_half(0)
-            early.start()
+    final = expert_count - 1
+    for e in range(final):
+        for first in (split, 0):
+            lax.fori_loop(0, split, lambda l, _: (token_block(e, first, l), 0)[1], 0)
+            weight_grads(e, first)
+            if first:
+                send_half(e)
+                if e == 0:
+                    last_arrived((1, 3))
+
+                    @pl.when(jnp.logical_not(at_ends()))
+                    def _():
+                        last_relay.start()
+
+    last_arrived((2,))
+    for k in range(split):
+        core_copy(down_at, last_core, k).wait_recv()
+
+    def sum_copy(index):
+        to = lax.rem(low + 1 + index, split)
+        return remote(
+            part_ref.at[index], arrive_ref.at[index], sum_sems.at[0, index], sum_sems.at[1, index],
+            core, high, to,
+        )
+
+    def last_block(index, _):
+        l = lax.rem(low + 1 + index, split)
+        token_block(final, split, l)
+        token_block(final, 0, l)
+
+        @pl.when(index < split - 1)
+        def _():
+            rows = pl.ds(pl.multiple_of(l * own_rows, own_rows), own_rows)
+            part_ref[index, :, :model_width] = low_bits(d_sum_ref[rows, :])
+            part_ref[index, :, model_width:] = low_bits(dg_sum_ref[rows, :])
+            sum_copy(index).start()
+
+        return 0
+
+    lax.fori_loop(0, split, last_block, 0)
+    weight_grads(final, split)
+    send_half(final)
+    for e in range(final):
+        add_half(e)
+    early.start()
+    weight_grads(final, 0)
     for copy in last_copies + [last_relay]:
         copy.wait_send()
 
-    sum_copies = plane_copies(lambda to, k: part_ref.at[k - 1], arrive_ref, sum_sems, False)
     y_copies = plane_copies(
         lambda to, k: part_ref.at[k - 1, :, pl.ds(0, model_width)], y_arrive_ref, y_sems, False
     )
-    for k in range(1, split):
-        to = pl.ds(pl.multiple_of(lax.rem(low + k, split) * own_rows, own_rows), own_rows)
-        part_ref[k - 1, :, :model_width] = low_bits(d_sum_ref[to, :])
-        part_ref[k - 1, :, model_width:] = low_bits(dg_sum_ref[to, :])
-        sum_copies[k - 1].start()
-
-    early.pass_on()
-    for e in range(1, expert_count):
-        add_half(e)
     own = pl.ds(pl.multiple_of(low * own_rows, own_rows), own_rows)
     d_second, dg_lanes = d_sum_ref[own, :], dg_sum_ref[own, :]
     for k in range(1, split):
-        sum_copies[k - 1].wait()
+        sum_copy(k - 1).wait()
         d_second = d_second + arrive_ref[k - 1, :, :model_width].astype(jnp.float32)
         dg_lanes = dg_lanes + arrive_ref[k - 1, :, model_width:].astype(jnp.float32)
     d_gate = jnp.sum(dg_lanes, -1, keepdims=True)
@@ -1216,7 +1341,7 @@
     route_lanes = routed_ref[low, :, model_width:].astype(jnp.float32)
     probs, chosen, gate = route_probs(second_own, router, route_lanes, expert_count)
     d_logits = low_bits(probs * (d_gate * (chosen - gate)))
-    d_second = d_second + matmul_nt(d_logits, router)
+    d_second = d_second + matmul(d_logits, router)
     d_rows, d_gain = norm_back(resid_ref[...], gains_ref[1:2, :], d_second)
     d_resid = grad_ref[...] + d_rows
     d_resid_ref[...] = d_resid
@@ -1232,8 +1357,12 @@
     small_ref[1:2, :] = jnp.sum(d_gain, 0, keepdims=True)
     small_ref[2 : 2 + expert_count, :] = matmul_tn(d_logits, second_own)[:expert_count]
 
+    early.pass_on()
+    add_half(final)
+    stores[2].start()
+    for copy in loads[1:]:
+        copy.wait()
     fill_offsets(reset_ref, lengths_ref, row_count)
-    spread(coef_ref, dt_rank + states, out_ref, steps, states)
     out_full = gate_ref[:, channel_rows:].reshape(width, model_width)
     for copy in branch_copies:
         copy.wait()
@@ -1268,6 +1397,8 @@
             copy.start()
         return 0
 
+    stores[0].start()
+    stores[1].start()
     lax.fori_loop(0, tiles, ends_of, 0)
 
     normed = normed_ref[...].reshape(row_count, model_width)
@@ -1315,18 +1446,20 @@
 
         row_loop(gate_rows, 16, add_gate)
     early.finish(early_ref)
+    for copy in stores:
+        copy.wait()
 
 
 def run_turn(
     second, routed, hidden_full, last_part, router_lanes, resid, grad_out, gains, lengths, gate_full, normed,
-    coef, step, z, y, gated, rows, dt_rank, states, expert_count,
+    spread_out, step, z, y, gated, rows, states, expert_count,
 ):
     _, own_rows, model_width = second.shape
     row_count = own_rows * split
     steps = row_count // subs
     tiles = step.shape[0]
     width = tiles * lanes
-    hidden = last_part.shape[0]
+    hidden = last_part.shape[1]
     hidden_rows = 2 * expert_count * hidden
     cut = 2 * hidden
     gate_rows = gate_full.shape[1]
@@ -1346,12 +1479,19 @@
         ((split, gate_rows, model_width), bf16),
     ]
     span = split * hidden
+    anywhere = pl.BlockSpec(memory_space=pl.ANY)
+    specs = [anywhere if i == 2 or i > 8 else vmem for i in range(17)]
+    specs[8] = pl.BlockSpec(memory_space=pltpu.SMEM)
+    loaded = [hidden_full, gate_full, normed, spread_out, step, z, y, gated, rows]
     return pl.pallas_call(
-        functools.partial(turn_kernel, dt_rank, states, expert_count),
-        in_specs=[pl.BlockSpec(memory_space=pltpu.SMEM) if i == 8 else vmem for i in range(17)],
-        out_specs=[vmem] * len(outs),
+        functools.partial(turn_kernel, states, expert_count),
+        in_specs=specs,
+        out_specs=[anywhere if i in (3, 4, 6) else vmem for i in range(len(outs))],
         out_shape=[jax.ShapeDtypeStruct(shape, kind) for shape, kind in outs],
-        scratch_shapes=[
+        scratch_shapes=[pltpu.VMEM(value.shape, value.dtype) for value in loaded]
+        + [pltpu.VMEM(*outs[i]) for i in (3, 4, 6)]
+        + [dma((len(loaded),)), dma((3,))]
+        + [
             pltpu.VMEM((2 * split, hidden_rows, model_width), bf16),
             pltpu.VMEM((split, hidden_rows, model_width), bf16),
             pltpu.VMEM((row_count, model_width), f32),
@@ -1359,13 +1499,12 @@
             pltpu.VMEM((row_count, lanes), f32),
             pltpu.VMEM((row_count, lanes), f32),
             pltpu.VMEM((row_count, model_width), bf16),
-            pltpu.VMEM((row_count, span), bf16),
-            pltpu.VMEM((row_count, span), bf16),
+            pltpu.VMEM((row_count, 2 * span), bf16),
+            pltpu.VMEM((row_count, 2 * span), bf16),
             pltpu.VMEM((others, own_rows, model_width + lanes), bf16),
             pltpu.VMEM((others, own_rows, model_width + lanes), bf16),
             pltpu.VMEM((others, own_rows, model_width), bf16),
             pltpu.VMEM((split, own_rows, model_width), bf16),
-            pltpu.VMEM((steps, states, subs, lanes), f32),
             pltpu.VMEM((row_count, lanes), f32),
             pltpu.VMEM((tiles, 2 * states, lanes), f32),
             pltpu.VMEM((others, tiles, 2 * states, lanes), f32),
@@ -1390,17 +1529,19 @@
         cost_estimate=pl.CostEstimate(flops=1000, bytes_accessed=1000, transcendentals=0),
     )(
         second, routed, hidden_full, last_part, router_lanes, resid, grad_out, gains, lengths, gate_full, normed,
-        coef, step, z, y, gated, rows,
+        spread_out, step, z, y, gated, rows,
     )
 
 
 def back_kernel(
     dt_rank, states, tap_count,
-    dy_ref, gz_ref, later_ref, mine_ref, gate_mine_ref, first_ref, gate_ref, normed_ref, input_ref,
-    coef_ref, step_ref, start_ref, rows_ref, d_resid_ref, tokens_ref, gains_ref, small_ref,
-    lengths_ref,
+    dy_hbm, gz_hbm, later_hbm, mine_ref, gate_mine_hbm, first_hbm, gate_hbm, normed_hbm, input_ref,
+    coef_ref, step_hbm, start_hbm, rows_ref, d_resid_ref, tokens_ref, gains_ref, small_ref,
+    lengths_ref, in_hbm, out_hbm,
     grad_tokens_ref, total_ref, late_ref, gate_own_ref, first_own_ref,
-    in_ref, out_ref, hist_ref, acc_in_ref, acc_out_ref, mixed_ref, conv_ref, q_ref, r_ref, reset_ref,
+    dy_ref, gz_ref, later_ref, gate_mine_ref, first_ref, gate_ref, normed_ref, step_ref, start_ref,
+    in_ref, out_ref, load_sems,
+    hist_ref, acc_in_ref, acc_out_ref, mixed_ref, conv_ref, q_ref, r_ref, reset_ref,
     gdt_ref, gin_ref, halo_ref, part_ref, arrive_ref, fold_ref, coef_send_ref,
     coef_arrive_ref, gcoef_ref, misc_ref, select_ref, payload_ref, half_ref, mine_first_ref,
     late_arrive_ref, gate_arrive_ref, first_arrive_ref, core_slots, plane_slots, line_slots,
@@ -1412,6 +1553,26 @@
     row_count = own_rows * split
     steps = row_count // subs
     tiles = step_ref.shape[0]
+    loads = [
+        pltpu.make_async_copy(source, target, load_sems.at[i])
+        for i, (source, target) in enumerate(
+            (
+                (step_hbm, step_ref),
+                (start_hbm, start_ref),
+                (gate_mine_hbm, gate_mine_ref),
+                (in_hbm, in_ref),
+                (dy_hbm, dy_ref),
+                (later_hbm, later_ref),
+                (out_hbm, out_ref),
+                (first_hbm, first_ref),
+                (gate_hbm, gate_ref),
+                (gz_hbm, gz_ref),
+                (normed_hbm, normed_ref),
+            )
+        )
+    ]
+    for copy in loads:
+        copy.start()
     width = tiles * lanes
     channel_rows = width // (2 * split)
     edge = input_ref.shape[0] - row_count
@@ -1442,9 +1603,9 @@
             mixed_ref[j, pl.ds(at, 32), :] = mixed
 
     row_loop(row_count, 32, convolve)
-    spread(coef_ref, dt_rank, in_ref, steps, states)
-    spread(coef_ref, dt_rank + states, out_ref, steps, states)
     late.pass_on()
+    for copy in loads[:7]:
+        copy.wait()
     gate.start()
     acc_in_ref[...] = jnp.zeros_like(acc_in_ref)
     acc_out_ref[...] = jnp.zeros_like(acc_out_ref)
@@ -1507,6 +1668,9 @@
 
     lax.fori_loop(0, tiles, back_of, 0)
 
+    for copy in loads[7:]:
+        copy.wait()
+
     source = lax.broadcasted_iota(jnp.int32, select_ref.shape, 0) // lanes
     target = lax.broadcasted_iota(jnp.int32, select_ref.shape, 1)
 
@@ -1652,9 +1816,22 @@
     first_half(half_width)
     half.start()
     sum_copies = plane_copies(lambda to, k: part_ref.at[k - 1], arrive_ref, sum_sems, False)
-    for k in range(1, split):
-        part_ref[k - 1] = low_bits(normed_block(lax.rem(low + k, split)))
-        sum_copies[k - 1].start()
+    gain = jnp.zeros((1, model_width), jnp.float32)
+    for k in range(1, split + 1):
+        l = lax.rem(low + k, split)
+        block = normed_block(l)
+        gain = gain + jnp.sum(block * normed_ref[l].astype(jnp.float32), 0, keepdims=True)
+        if k < split:
+            part_ref[k - 1] = low_bits(block)
+            sum_copies[k - 1].start()
+        else:
+            grad_tokens_ref[...] = block
+
+    line_slots[high] = small_ref[...]
+    line_slots[high, 0:1, :] = gain / gains_ref[0:1, :]
+    line = line_copies(line_slots.at[high], lambda at: line_slots.at[at], line_sems, True)
+    for copy in line:
+        copy.start()
     first_half(0)
     half.wait()
 
@@ -1670,8 +1847,19 @@
         first_sems,
     )
     first.start()
-    grad_tokens_ref[...] = normed_block(low)
+    for k in range(1, split):
+        line_arrived(line_slots.at[high], lambda at: line_slots.at[at], line_sems, k)
+    core_slots[core] = (line_slots[0] + line_slots[1]) + (line_slots[2] + line_slots[3])
+    hop = remote(
+        core_slots.at[core], core_slots.at[core], core_sems.at[0], core_sems.at[1], 1 - core, high, low
+    )
+    hop.start()
     late.finish(late_ref)
+    hop.wait()
+    plane_slots[low] = core_slots[0] + core_slots[1]
+    plane = plane_copies(lambda to, k: plane_slots.at[low], plane_slots, plane_sems, True)
+    for copy in plane:
+        copy.start()
     first.pass_on()
     gate.finish(gate_own_ref)
     d_normed = grad_tokens_ref[...]
@@ -1679,32 +1867,13 @@
         sum_copies[k - 1].wait()
         d_normed = d_normed + arrive_ref[k - 1].astype(jnp.float32)
     tokens = tokens_ref[...].astype(jnp.float32)
-    d_rows, d_gain = norm_back(tokens, gains_ref[0:1, :], d_normed)
+    d_rows, _ = norm_back(tokens, gains_ref[0:1, :], d_normed)
     grad_tokens_ref[...] = d_resid_ref[...] + d_rows
-
-    core_slots[core] = small_ref[...]
-    core_slots[core, 0:1, :] = jnp.sum(d_gain, 0, keepdims=True)
-    hop = remote(
-        core_slots.at[core], core_slots.at[core], core_sems.at[0], core_sems.at[1], 1 - core, high, low
-    )
-    hop.start()
-    hop.wait()
-    plane_slots[low] = core_slots[0] + core_slots[1]
-    plane = plane_copies(lambda to, k: plane_slots.at[low], plane_slots, plane_sems, True)
-    for copy in plane:
-        copy.start()
     for copy in plane:
         copy.wait()
-    line_slots[high] = (plane_slots[0] + plane_slots[1]) + (plane_slots[2] + plane_slots[3])
-    line = line_copies(line_slots.at[high], lambda at: line_slots.at[at], line_sems, True)
-    for copy in line:
-        copy.start()
-
-    for k in range(1, split):
-        line_arrived(line_slots.at[high], lambda at: line_slots.at[at], line_sems, k)
     for copy in line:
         copy.wait_send()
-    total_ref[...] = (line_slots[0] + line_slots[1]) + (line_slots[2] + line_slots[3])
+    total_ref[...] = (plane_slots[0] + plane_slots[1]) + (plane_slots[2] + plane_slots[3])
     first.finish(first_own_ref)
 
     @pl.when(high > 0)
@@ -1714,7 +1883,7 @@
 
 def run_back(
     dy, gz, later, mine, gate_mine, first_full, gate_full, normed, input_all, coef, step, start, rows,
-    d_resid, tokens, gains, small, lengths, dt_rank, states, tap_count,
+    d_resid, tokens, gains, small, lengths, spread_in, spread_out, dt_rank, states, tap_count,
 ):
     _, own_rows, model_width = normed.shape
     row_count = own_rows * split
@@ -1727,8 +1896,11 @@
     gate_rows = gate_mine.shape[1]
     first_columns = first_full.shape[2]
     vmem = pl.BlockSpec(memory_space=pltpu.VMEM)
-    specs = [vmem] * 17
+    specs = [pl.BlockSpec(memory_space=pl.ANY) if i in (0, 1, 2, 4, 5, 6, 7, 10, 11) else vmem for i in range(17)]
+    loaded = [dy, gz, later, gate_mine, first_full, gate_full, normed, step, start]
+    loaded += [spread_in, spread_out]
     specs.append(pl.BlockSpec(memory_space=pltpu.SMEM))
+    specs += [pl.BlockSpec(memory_space=pl.ANY)] * 2
     f32, bf16 = jnp.float32, jnp.bfloat16
     dma = pltpu.SemaphoreType.DMA
     outs = [
@@ -1739,16 +1911,15 @@
         (channel_rows, first_columns),
     ]
     tiled = pltpu.VMEM((tiles, row_count, lanes), f32)
-    spreads = pltpu.VMEM((steps, states, subs, lanes), f32)
     summed = pltpu.VMEM((row_count, states * lanes), f32)
     return pl.pallas_call(
         functools.partial(back_kernel, dt_rank, states, tap_count),
         in_specs=specs,
         out_specs=[vmem] * len(outs),
         out_shape=[jax.ShapeDtypeStruct(shape, f32) for shape in outs],
-        scratch_shapes=[
-            spreads,
-            spreads,
+        scratch_shapes=[pltpu.VMEM(value.shape, value.dtype) for value in loaded]
+        + [dma((len(loaded),))]
+        + [
             pltpu.VMEM((steps + 1, states, subs, lanes), f32),
             summed,
             summed,
@@ -1787,8 +1958,69 @@
         cost_estimate=pl.CostEstimate(flops=1000, bytes_accessed=1000, transcendentals=0),
     )(
         dy, gz, later, mine, gate_mine, first_full, gate_full, normed, input_all, coef, step, start,
-        rows, d_resid, tokens, gains, small, lengths,
-    )
+        rows, d_resid, tokens, gains, small, lengths, spread_in, spread_out,
+    )
+
+
+def results_kernel(
+    tap_count, states, coef_count, dt_rank, expert_count,
+    mixed_ref, tokens_ref, total_ref, early_ref, late_ref, gate_ref, first_ref,
+    mixed_out, tokens_out, gains_out, router_out, in_out, conv_out, x_out, dt_out, bias_out, alog_out,
+    skip_out, out_out, up_out, down_out,
+):
+    channels, model_width = out_out.shape
+    hidden = up_out.shape[1]
+    channel_rows = first_ref.shape[0]
+    mixed_out[...] = mixed_ref[...]
+    tokens_out[...] = tokens_ref[...]
+    gains_out[...] = total_ref[:2]
+    router_out[...] = total_ref[2 : 2 + expert_count]
+    in_out[0] = first_ref[:channels, :model_width]
+    in_out[1] = gate_ref[:channels]
+    out_out[...] = gate_ref[channel_rows : channel_rows + channels]
+    at = model_width
+    x_out[...] = first_ref[:channels, at : at + lanes][:, :coef_count]
+    dt_out[...] = first_ref[:channels, at + lanes : at + 2 * lanes][:, :dt_rank]
+    misc = first_ref[:, at + 2 * lanes :]
+    rows = misc.T
+    conv_out[...] = rows[:tap_count, :channels]
+    alog_out[...] = rows[alog_row : alog_row + states, :channels]
+    bias_out[...] = rows[bias_row : bias_row + 1, :channels]
+    skip_out[...] = rows[skip_row : skip_row + 1, :channels]
+    for e in range(expert_count):
+        source, first = (early_ref, 0) if e == 0 else (late_ref, 2 * (e - 1) * hidden)
+        up_out[e] = source[first : first + hidden]
+        down_out[e] = source[first + hidden : first + 2 * hidden]
+
+
+def run_results(parts, channels, tap_count, states, coef_count, dt_rank, expert_count, hidden):
+    own_rows, model_width = parts[0].shape
+    f32 = jnp.float32
+    shapes = [
+        (own_rows, model_width),
+        (2, model_width),
+        (expert_count, model_width),
+        (2, channels, model_width),
+        (tap_count, channels),
+        (channels, coef_count),
+        (channels, dt_rank),
+        (1, channels),
+        (states, channels),
+        (1, channels),
+        (channels, model_width),
+        (expert_count, hidden, model_width),
+        (expert_count, hidden, model_width),
+    ]
+    vmem = pl.BlockSpec(memory_space=pltpu.VMEM)
+    return pl.pallas_call(
+        functools.partial(results_kernel, tap_count, states, coef_count, dt_rank, expert_count),
+        in_specs=[vmem] * len(parts),
+        out_specs=[vmem] * (len(shapes) + 1),
+        out_shape=[jax.ShapeDtypeStruct((own_rows, model_width), jnp.bfloat16)]
+        + [jax.ShapeDtypeStruct(shape, f32) for shape in shapes],
+        compiler_params=pltpu.CompilerParams(vmem_limit_bytes=62 << 20),
+        cost_estimate=pl.CostEstimate(flops=1000, bytes_accessed=1000, transcendentals=0),
+    )(*parts)
 
 
 def norm_rows(values, gain_row):
@@ -2239,87 +2471,47 @@
     expert_out,
 ):
     channels, tap_count = conv_weight.shape
-    dt_rank = dt_weight.shape[1]
-    states = a_log.shape[1]
-    expert_count, hidden, model_width = expert_in.shape
-    own_rows = tokens.shape[0]
-    row_count = own_rows * split
-    high_count = lax.axis_size("seq") // split
-    low = lax.axis_index("seq") % split
-    high = lax.axis_index("seq") // split
+    dt_rank, states = dt_weight.shape[1], a_log.shape[1]
+    expert_count, hidden, _ = expert_in.shape
     coef_count = dt_rank + 2 * states
-    channel_rows = -(-channels // 16) * 16
-    width = 2 * high_count * channel_rows
-    hidden_rows = expert_count * hidden
-    small_width = -(-(coef_count + dt_rank + tap_count + 2 + states) // lanes) * lanes
-
-    small = jnp.concatenate(
-        [x_weight, dt_weight, conv_weight, dt_bias[:, None], a_log, skip_gain[:, None]], 1
-    )
-    small = jnp.pad(small, ((0, 0), (0, small_width - small.shape[1])))
-    inputs = tokens.astype(jnp.float32)
-    def wide(parts, columns):
-        part = jnp.concatenate(parts, 1)
-        return jnp.pad(part, ((0, 0), (0, columns - part.shape[1])))
-
-    gap = jnp.zeros((channels, 2), jnp.bfloat16)
-    a_part = pad_rows(
-        jnp.concatenate(
-            [
-                in_weight[0],
-                wide([x_weight], lanes),
-                wide([dt_weight], lanes),
-                wide([conv_weight, dt_bias[:, None], skip_gain[:, None], gap, a_log], lanes),
-            ],
-            1,
-        ),
-        channel_rows,
-    )
-    b_part = jnp.concatenate(
-        [pad_rows(in_weight[1], channel_rows), pad_rows(out_weight, channel_rows)], 0
-    )
-    c_parts = []
-    for e in range(expert_count):
-        c_parts += [expert_in[e], expert_out[e]]
-    c_part, last_part = jnp.concatenate(c_parts[:-1], 0), c_parts[-1]
-    g_part = low_bits(
-        jnp.concatenate(
-            [grad_out, routes[:, None].astype(jnp.float32) * jnp.ones((1, lanes), jnp.float32)], 1
-        )
-    )
     (
-        first_full, gate_full, hidden_full, normed, _, routed, input_all, coef, step, z, y, gated, start,
-        resid, second, rows,
+        first_full, gate_full, hidden_full, normed, routed, input_all, coef, step, z, y, gated, start,
+        resid, second, rows, spread_in, spread_out,
     ) = run_mixer(
-        tokens, norm_gains, lengths, a_part, b_part, c_part, g_part, dt_rank, states, tap_count
-    )
-    router_lanes = jnp.pad(router, ((0, 0), (0, lanes - expert_count)))
+        tokens, norm_gains, lengths, in_weight, conv_weight.T, x_weight, dt_weight, dt_bias[None], a_log.T,
+        skip_gain[None], out_weight, expert_in, expert_out, grad_out, routes[None],
+    )
     mixed_out, d_resid, small_sums, dy, gz, later, mine, early, gate_mine = run_turn(
-        second, routed, hidden_full, last_part, router_lanes, resid, grad_out, norm_gains, lengths, gate_full,
-        normed, coef, step, z, y, gated, rows, dt_rank, states, expert_count,
+        second, routed, hidden_full, expert_out, router.T, resid, grad_out, norm_gains, lengths,
+        gate_full, normed, spread_out, step, z, y, gated, rows, states, expert_count,
     )
     grad_tokens, sums, late, gate_own, first_own = run_back(
         dy, gz, later, mine, gate_mine, first_full, gate_full, normed, input_all, coef, step, start,
-        rows, d_resid, tokens, norm_gains, small_sums, lengths, dt_rank, states, tap_count,
-    )
-    hidden_own = jnp.concatenate([early, late], 0).reshape(expert_count, 2, hidden, model_width)
-    first_own, gate_first = first_own[:channels], gate_own[:channels]
-    misc = first_own[:, model_width + 2 * lanes :]
+        rows, d_resid, tokens, norm_gains, small_sums, lengths, spread_in, spread_out, dt_rank, states,
+        tap_count,
+    )
+    (
+        mixed_out, grad_tokens, grad_gains, grad_router, grad_in, grad_conv, grad_x, grad_dt, grad_bias,
+        grad_alog, grad_skip, grad_out_w, grad_up, grad_down,
+    ) = run_results(
+        (mixed_out, grad_tokens, sums, early, late, gate_own, first_own),
+        channels, tap_count, states, coef_count, dt_rank, expert_count, hidden,
+    )
     return (
         mixed_out,
         grad_tokens,
-        sums[:2],
-        sums[2 : 2 + expert_count].T,
-        jnp.stack([first_own[:, :model_width], gate_first]),
-        misc[:, :tap_count],
-        first_own[:, model_width : model_width + coef_count],
-        first_own[:, model_width + lanes : model_width + lanes + dt_rank],
-        misc[:, bias_row],
-        misc[:, alog_row : alog_row + states],
-        misc[:, skip_row],
-        gate_own[channel_rows : channel_rows + channels],
-        hidden_own[:, 0],
-        hidden_own[:, 1],
+        grad_gains,
+        grad_router.T,
+        grad_in,
+        grad_conv.T,
+        grad_x,
+        grad_dt,
+        grad_bias[0],
+        grad_alog.T,
+        grad_skip[0],
+        grad_out_w,
+        grad_up,
+        grad_down,
     )
 
 

time: 328 us -> 286 us (0.87)
  local copies, waits for them, and re-layouts: 18.2 us -> 0 us
  Pallas kernels: 304 us -> 286 us
  other arithmetic: 4.23 us -> 0 us
    pallas_call x1 -> x2, Pallas kernels: 93 us -> 82.5 us  [the longest x1 78.5 us: run_turn(): pl.pallas_call(functools.partial(turn_kernel, states, expert_count), in_s...]
    slice x6 -> x0, local copies, waits for them, and re-layouts: 6.72 us -> none  [the longest x1 1.57 us: shards_plane(): misc[:, skip_row]]
    pallas_call x1, Pallas kernels: 92.1 us -> 86.9 us  [run_back(): pl.pallas_call(functools.partial(back_kernel, dt_rank, states, tap_count)...]
    unnamed x29 -> x0, local copies, waits for them, and re-layouts: 3.83 us -> none
where the time goes in v4:
time: 286 us
  Pallas kernels  286 us (100%)
    pallas_call x1, Pallas kernels, run_mixer(): pl.pallas_call(functools.partial(mixer_kernel, dt_rank, states, tap_count...  116 us
    pallas_call x1, Pallas kernels, run_back(): pl.pallas_call(functools.partial(back_kernel, dt_rank, states, tap_count)...  86.9 us
    pallas_call x1, Pallas kernels, run_turn(): pl.pallas_call(functools.partial(turn_kernel, states, expert_count), in_s...  78.5 us

profile of v4, /device:TPU:0, one launch (start us, length us, event | category | flops | bytes accessed | tf_op | source)
XLA Modules:
  0.0 286.3 jit_solution(3353143804525858352)
XLA Ops:
  0.6 116.2 %shard_map.263 = (bf16[8,80,1536]{2,1,0:T(8,128)(2,1)}, bf16[8,160,1152]{2,1,0:T(8,128)(2,1)}, bf16[8,288,1152]{2,1,0:T(8,128)(2,1)}, bf16[4,128,1152]{2,1,0:T(8...) custom-call(bf16[128,1152]{1,0:T(8,128)(2,1)} %tokens_ref.3, ...), custom_call_target="tpu_custom_call" | custom-call | flops 1000 | bytes 1000 | tf_op jit(solution)/shard_map/pallas_call | solution.py:953
  116.8 78.5 %shard_map.264 = (bf16[128,1152]{1,0:T(8,128)(2,1)}, f32[128,1152]{1,0:T(8,128)}, f32[8,1152]{1,0:T(8,128)}, f32[5,512,128]{2,1,0:T(8,128)}, bf16[512,640]{1,0:T...) custom-call(bf16[4,128,1152]{2,1,0:T(8,128)(2,1)} %get-tuple-element, ...), custom_call_target="tpu_custom_call" | custom-call | flops 1000 | bytes 1000 | tf_op jit(solution)/shard_map/pallas_call | solution.py:1486
  195.3 86.9 %shard_map.265 = (f32[128,1152]{1,0:T(8,128)}, f32[8,1152]{1,0:T(8,128)}, f32[192,1152]{1,0:T(8,128)}, f32[160,1152]{1,0:T(8,128)}, f32[80,1536]{1,0:T(8,128)}) custom-call(f32[5,512,128]{2,1,0:T(8,128)} %get-tuple-element.72.dy_hbm, bf16[512,640]{1,0:T(8,128)(2,1)} %get-tuple-element.73.gz_hbm, f32[5,16,8,128]{3,2,1,0:T(8,128)} %get-tuple-element.74.later_hbm, ...), custom_call_target="tpu_custom_call" | custom-call | flops 1000 | bytes 1000 | tf_op jit(solution)/shard_map/pallas_call | solution.py:1915
  282.3 4.0 %shard_map.266 = (bf16[128,1152]{1,0:T(8,128)(2,1)}, f32[128,1152]{1,0:T(8,128)}, f32[2,1152]{1,0:T(2,128)}, f32[2,1152]{1,0:T(2,128)}, f32[2,72,1152]{2,1,0:T(8...) custom-call(bf16[128,1152]{1,0:T(8,128)(2,1)} %get-tuple-element.71., ...), custom_call_target="tpu_custom_call" | custom-call | flops 1000 | bytes 1000 | tf_op jit(solution)/shard_map/pallas_call | solution.py:2015

commit v5 on v4

--- a/solution.py
+++ b/solution.py
@@ -480,12 +480,16 @@
     lax.fori_loop(0, count // size, one, 0)
 
 
-def scan_one_way(j, first_sub, reverse, states, steps, step_ref, reset_ref, drive_ref, spread_ref, rates):
+def step_rows(s):
+    return pl.ds(pl.multiple_of(s * subs, subs), subs)
+
+
+def scan_one_way(j, reverse, states, steps, step_ref, drive_of, spread_ref, rates):
     def one(turn, carry):
         s = steps - 1 - turn if reverse else turn
         total, held = carry
-        step = step_ref[j, pl.ds(s, subs, stride=steps), :] + reset_ref[pl.ds(s, subs, stride=steps), :]
-        drive = drive_ref[j, pl.ds(s, subs, stride=steps), :]
+        step = step_ref[j, step_rows(s), :]
+        drive = drive_of(s)
         after_step = []
         for n in range(states):
             factor = jnp.exp2(step * rates[n])
@@ -537,7 +541,7 @@
 alog_row = 8
 bias_row = 4
 skip_row = 5
-early_hidden = 96
+early_hidden = 64
 
 
 def mixer_kernel(
@@ -546,10 +550,10 @@
     dt_bias_ref, a_log_ref, skip_ref, out_weight_ref, expert_in_ref, expert_out_ref, grad_ref,
     routes_ref,
     first_out, gate_out, hidden_ref, normed_out, routed_out, input_out, coef_out, step_out, z_out,
-    y_out, gated_out, start_out, resid_ref, second_out, rows_out, in_out, out_out,
+    y_out, gated_out, start_out, resid_ref, second_out, rows_out, in_out, out_out, drive_out,
     first_ref, gate_ref, normed_ref, edge_ref, routed_ref, input_ref, coef_ref, step_ref, z_ref,
     y_ref, gated_ref, start_ref, second_ref, rows_ref, c_ref, out_sems,
-    in_ref, out_ref, drive_ref, reset_ref, mixed_ref, partial_ref, arrive_ref, coef_send_ref,
+    in_ref, out_ref, drive_ref, mixed_ref, partial_ref, arrive_ref, coef_send_ref,
     coef_arrive_ref, send_ref, ends_ref, grow_ref, state_ref,
     a_sems, b_sems, c_sems, d_sems, a_core, b_core, c_core, d_core, token_sems, route_sems,
     second_sems, coef_sems, sum_sems, edge_send, edge_arrive, ends_sems, local_sem,
@@ -694,20 +698,20 @@
         place = high * row_count + at + lax.broadcasted_iota(jnp.int32, (rows, lanes), 0)
         return jnp.where(place < first_len, place, place - first_len)
 
-    def fill_reset(at):
-        reset_ref[pl.ds(at, 64), :] = jnp.where(offsets(at, 64) == 0, 1e30, 0.0)
-
-    row_loop(row_count, 64, fill_reset)
-
     @pl.when(high == 0)
     def _():
         edge_ref[...] = jnp.zeros_like(edge_ref)
 
     arrived(a_ref, a_dst, a_sems, a_core, (1, 3))
     relay_inside(0)
-    for copy in b_copies:
+    for copy in b_copies + c_copies:
         copy.start()
+    local.wait()
     relay_from_end(1)
+    relay_from_end(2)
+    for copy in (core_copy(c_dst, c_core, 0), core_copy(d_dst, d_core, 0)):
+        copy.start()
+        core_copies.append(copy)
     for copy in token_copies:
         copy.wait()
     arrived(a_ref, a_dst, a_sems, a_core, (2,))
@@ -752,15 +756,6 @@
             )
 
     row_loop(row_count, 32, convolve)
-    arrived(b_ref, b_dst, b_sems, b_core, (1, 3))
-    relay_inside(1)
-    local.wait()
-    for copy in (core_copy(c_dst, c_core, 0), core_copy(d_dst, d_core, 0)):
-        copy.start()
-        core_copies.append(copy)
-    for copy in c_copies:
-        copy.start()
-    relay_from_end(2)
 
     x_full = first_ref[:, :, model_width : model_width + lanes].reshape(width, lanes)
     part = matmul(mixed_ref[...], x_full)
@@ -771,23 +766,27 @@
         copy.start()
     for copy in coef_copies:
         copy.wait()
+    arrived(b_ref, b_dst, b_sems, b_core, (1, 3))
+    relay_inside(1)
     total = coef_ref[...]
     for k in range(1, split):
         total = total + coef_arrive_ref[k - 1].astype(jnp.float32)
     coef_ref[...] = total
     dt_full = first_ref[:, :, model_width + lanes : model_width + 2 * lanes].reshape(width, lanes)
 
-    def step_sizes(at):
-        pre = matmul_nt(low_bits(coef_ref[pl.ds(at, 128), :]), dt_full)
+    def step_sizes(chunk):
+        at = pl.multiple_of(chunk * steps, steps)
+        pre = matmul_nt(low_bits(coef_ref[pl.ds(at, steps), :]), dt_full)
+        reset = jnp.where(offsets(at, steps) == 0, 1e30, 0.0)
+        rows = pl.ds(chunk, steps, stride=subs)
         for j in range(tiles):
             cols = slice(j * lanes, (j + 1) * lanes)
             step = softplus_of(pre[:, cols] + rows_ref[j, bias_row : bias_row + 1, :])
-            step_ref[j, pl.ds(at, 128), :] = step
-            drive_ref[j, pl.ds(at, 128), :] = step * mixed_ref[pl.ds(at, 128), cols].astype(
-                jnp.float32
-            )
-
-    row_loop(row_count, 128, step_sizes)
+            step_ref[j, rows, :] = step + reset
+            drive_ref[j, rows, :] = step * mixed_ref[pl.ds(at, steps), cols].astype(jnp.float32)
+
+    lax.fori_loop(0, subs, lambda chunk, _: (step_sizes(chunk), 0)[1], 0)
+    store(drive_ref, drive_out)
     store(coef_ref, coef_out)
     store(step_ref, step_out)
     spread(coef_ref, first_b, in_ref, steps, states)
@@ -799,7 +798,14 @@
 
     def ends_of(j, _):
         found = scan_one_way(
-            j, None, False, states, steps, step_ref, reset_ref, drive_ref, in_ref, rates_of(j)
+            j,
+            False,
+            states,
+            steps,
+            step_ref,
+            lambda s: drive_ref[j, step_rows(s), :],
+            in_ref,
+            rates_of(j),
         )
         for n, (grow, state) in enumerate(found):
             grow_ref[j, n] = grow
@@ -835,9 +841,8 @@
             held.append(start)
 
         def one(s, held):
-            step = step_ref[j, pl.ds(s, subs, stride=steps), :]
-            step = step + reset_ref[pl.ds(s, subs, stride=steps), :]
-            drive = drive_ref[j, pl.ds(s, subs, stride=steps), :]
+            step = step_ref[j, step_rows(s), :]
+            drive = drive_ref[j, step_rows(s), :]
             now_all = []
             y = jnp.zeros((subs, lanes), jnp.float32)
             for n in range(states):
@@ -888,6 +893,9 @@
         sum_copies[k - 1].start()
     resid = tokens_ref[...].astype(jnp.float32) + out_block(low)
     arrived(c_src, c_dst, c_sems, c_core, (2,))
+    for copy in route_copies:
+        copy.wait()
+    store(routed_ref, routed_out)
     for k in range(1, split):
         sum_copies[k - 1].wait()
         resid = resid + arrive_ref[k - 1].astype(jnp.float32)
@@ -899,10 +907,9 @@
     arrived(d_src, d_dst, d_sems, d_core, (1, 3))
     relay_inside(3)
     arrived(d_src, d_dst, d_sems, d_core, (2,))
-    for copy in second_copies + route_copies:
+    for copy in second_copies:
         copy.wait()
     store(second_ref, second_out)
-    store(routed_ref, routed_out)
     for copy in a_copies + b_copies + c_copies + d_copies + relays + core_copies:
         copy.wait_send()
     for dst_of, sems in ((c_dst, c_core), (d_dst, d_core)):
@@ -946,7 +953,7 @@
     kept += [(tiled, f32), gated, start, normed, rows, (hidden_part, bf16)]
     outs = [first, gate, ((blocks,) + hidden_part, bf16), normed, routed, inputs, coef]
     spread_out = ((steps, states, subs, lanes), f32)
-    outs += [(tiled, f32)] * 3 + [gated, start, resid, normed, rows, spread_out, spread_out]
+    outs += [(tiled, f32)] * 3 + [gated, start, resid, normed, rows, spread_out, spread_out, (tiled, f32)]
     spreads = pltpu.VMEM((steps, states, subs, lanes), f32)
     dma = pltpu.SemaphoreType.DMA
     others = split - 1
@@ -961,7 +968,6 @@
             spreads,
             spreads,
             pltpu.VMEM(tiled, f32),
-            pltpu.VMEM((row_count, lanes), f32),
             pltpu.VMEM((row_count, width), bf16),
             pltpu.VMEM((others, own_rows, model_width), bf16),
             pltpu.VMEM((others, own_rows, model_width), bf16),
@@ -1102,31 +1108,20 @@
     return remote(src, dst, sems.at[0, h], sems.at[1, h], 1 - core, high, low)
 
 
-def fill_offsets(reset_ref, lengths_ref, row_count):
-    _, high, _ = kernel_place()
-    first_len = lengths_ref[0, 0]
-
-    def fill(at):
-        place = high * row_count + at + lax.broadcasted_iota(jnp.int32, (64, lanes), 0)
-        reset_ref[pl.ds(at, 64), :] = jnp.where((place == 0) | (place == first_len), 1e30, 0.0)
-
-    row_loop(row_count, 64, fill)
-
-
 def turn_kernel(
     states, expert_count,
     second_ref, routed_ref, hidden_hbm, weights_ref, router_ref, resid_ref, grad_ref, gains_ref,
-    lengths_ref,
     gate_hbm, normed_hbm, out_hbm, step_hbm, z_hbm, y_hbm, gated_hbm, rows_hbm,
     mixed_out_ref, d_resid_ref, small_ref, dy_out, gz_out, later_ref, mine_out, early_ref,
-    gate_mine_ref,
+    gate_mine_ref, mid_ref,
     hidden_ref, gate_ref, normed_ref, out_ref, step_ref, z_ref, y_ref, gated_ref, rows_ref, dy_ref,
-    gz_ref, mine_ref, load_sems, store_sems,
+    gz_ref, load_sems, store_sems,
     grads_ref, half_ref, y_sum_ref, d_sum_ref, dg_sum_ref, gates_ref, scaled_ref, act_ref, pre_ref,
-    part_ref, arrive_ref, y_arrive_ref, branch_ref, reset_ref, send_ref,
-    ends_ref, early_arrive_ref, gate_half_ref, down_ref, mine_early_ref, growth_ref,
+    part_ref, arrive_ref, y_arrive_ref, branch_ref, send_ref,
+    ends_ref, early_arrive_ref, gate_half_ref, down_ref, growth_ref,
+    mid_arrive_ref,
     half_sems, sum_sems, y_sems, branch_sems, early_sems, ends_sems, gate_half_sems, last_sems,
-    last_core,
+    last_core, mid_sems,
 ):
     core, high, low = kernel_place()
     _, own_rows, model_width = second_ref.shape
@@ -1152,11 +1147,17 @@
     ]
     for copy in loads:
         copy.start()
+    hidden = weights_ref.shape[1]
     stores = [
         pltpu.make_async_copy(source, target, store_sems.at[i])
-        for i, (source, target) in enumerate(((dy_ref, dy_out), (gz_ref, gz_out), (mine_ref, mine_out)))
+        for i, (source, target) in enumerate(
+            (
+                (dy_ref, dy_out),
+                (gz_ref, gz_out),
+                (half_ref.at[:, pl.ds(3 * hidden, hidden)], mine_out),
+            )
+        )
     ]
-    hidden = weights_ref.shape[1]
     last_ref = weights_ref.at[expert_count - 1]
     hidden_rows = 2 * expert_count * hidden
     channel_rows = width // (2 * split)
@@ -1265,19 +1266,20 @@
         for copy in half_copies[e]:
             copy.wait()
 
-        target, base = (mine_early_ref, 0) if e == 0 else (mine_ref, 2 * (e - 1) * hidden)
-
         def one(i, _):
             h, at = i // (2 * hidden // 32), lax.rem(i, 2 * hidden // 32) * 32
             rows = pl.ds(2 * e * hidden + at, 32)
-            target[h, pl.ds(base + at, 32)] = low_bits(
+            half_ref[h, rows] = low_bits(
                 grads_ref[h, rows].astype(jnp.float32) + half_ref[h, rows].astype(jnp.float32)
             )
             return 0
 
         lax.fori_loop(0, split * (2 * hidden // 32), one, 0)
 
-    early = LineScatter(lambda to: mine_early_ref.at[to], early_arrive_ref, early_sems)
+    mid = LineScatter(
+        lambda to: half_ref.at[to, pl.ds(2 * hidden, hidden)], mid_arrive_ref, mid_sems
+    )
+    early = LineScatter(lambda to: half_ref.at[to, part_of(0)], early_arrive_ref, early_sems)
     final = expert_count - 1
     for e in range(final):
         for first in (split, 0):
@@ -1293,6 +1295,9 @@
                         last_relay.start()
 
     last_arrived((2,))
+    for e in range(final):
+        add_half(e)
+    early.start()
     for k in range(split):
         core_copy(down_at, last_core, k).wait_recv()
 
@@ -1320,10 +1325,8 @@
     lax.fori_loop(0, split, last_block, 0)
     weight_grads(final, split)
     send_half(final)
-    for e in range(final):
-        add_half(e)
-    early.start()
     weight_grads(final, 0)
+    early.pass_on()
     for copy in last_copies + [last_relay]:
         copy.wait_send()
 
@@ -1357,12 +1360,11 @@
     small_ref[1:2, :] = jnp.sum(d_gain, 0, keepdims=True)
     small_ref[2 : 2 + expert_count, :] = matmul_tn(d_logits, second_own)[:expert_count]
 
-    early.pass_on()
     add_half(final)
+    mid.start()
     stores[2].start()
     for copy in loads[1:]:
         copy.wait()
-    fill_offsets(reset_ref, lengths_ref, row_count)
     out_full = gate_ref[:, channel_rows:].reshape(width, model_width)
     for copy in branch_copies:
         copy.wait()
@@ -1384,7 +1386,14 @@
 
     def ends_of(j, _):
         found = scan_one_way(
-            j, None, True, states, steps, step_ref, reset_ref, dy_ref, out_ref, rates_of(j)
+            j,
+            True,
+            states,
+            steps,
+            step_ref,
+            lambda s: dy_ref[j, pl.ds(s, subs, stride=steps), :],
+            out_ref,
+            rates_of(j),
         )
         row = lax.broadcasted_iota(jnp.int32, (subs, lanes), 0)
         for n, (grow, state) in enumerate(found):
@@ -1399,6 +1408,7 @@
 
     stores[0].start()
     stores[1].start()
+    mid.pass_on()
     lax.fori_loop(0, tiles, ends_of, 0)
 
     normed = normed_ref[...].reshape(row_count, model_width)
@@ -1446,12 +1456,13 @@
 
         row_loop(gate_rows, 16, add_gate)
     early.finish(early_ref)
+    mid.finish(mid_ref)
     for copy in stores:
         copy.wait()
 
 
 def run_turn(
-    second, routed, hidden_full, last_part, router_lanes, resid, grad_out, gains, lengths, gate_full, normed,
+    second, routed, hidden_full, last_part, router_lanes, resid, grad_out, gains, gate_full, normed,
     spread_out, step, z, y, gated, rows, states, expert_count,
 ):
     _, own_rows, model_width = second.shape
@@ -1474,14 +1485,14 @@
         ((tiles, row_count, lanes), f32),
         ((row_count, width), bf16),
         ((tiles, states, subs, lanes), f32),
-        ((split, hidden_rows - cut, model_width), bf16),
+        ((split, hidden, model_width), bf16),
         ((cut, model_width), f32),
         ((split, gate_rows, model_width), bf16),
+        ((hidden, model_width), f32),
     ]
     span = split * hidden
     anywhere = pl.BlockSpec(memory_space=pl.ANY)
-    specs = [anywhere if i == 2 or i > 8 else vmem for i in range(17)]
-    specs[8] = pl.BlockSpec(memory_space=pltpu.SMEM)
+    specs = [anywhere if i == 2 or i > 7 else vmem for i in range(16)]
     loaded = [hidden_full, gate_full, normed, spread_out, step, z, y, gated, rows]
     return pl.pallas_call(
         functools.partial(turn_kernel, states, expert_count),
@@ -1489,7 +1500,7 @@
         out_specs=[anywhere if i in (3, 4, 6) else vmem for i in range(len(outs))],
         out_shape=[jax.ShapeDtypeStruct(shape, kind) for shape, kind in outs],
         scratch_shapes=[pltpu.VMEM(value.shape, value.dtype) for value in loaded]
-        + [pltpu.VMEM(*outs[i]) for i in (3, 4, 6)]
+        + [pltpu.VMEM(*outs[i]) for i in (3, 4)]
         + [dma((len(loaded),)), dma((3,))]
         + [
             pltpu.VMEM((2 * split, hidden_rows, model_width), bf16),
@@ -1505,14 +1516,13 @@
             pltpu.VMEM((others, own_rows, model_width + lanes), bf16),
             pltpu.VMEM((others, own_rows, model_width), bf16),
             pltpu.VMEM((split, own_rows, model_width), bf16),
-            pltpu.VMEM((row_count, lanes), f32),
             pltpu.VMEM((tiles, 2 * states, lanes), f32),
             pltpu.VMEM((others, tiles, 2 * states, lanes), f32),
             pltpu.VMEM((split + 1, cut, model_width), bf16),
             pltpu.VMEM((split, gate_rows, model_width), bf16),
             pltpu.VMEM((2 * split, hidden, model_width), bf16),
-            pltpu.VMEM((split, cut, model_width), bf16),
             pltpu.VMEM((tiles, states, subs, lanes), f32),
+            pltpu.VMEM((split + 1, hidden, model_width), bf16),
             dma((expert_count, 2, split)),
             dma((2, others)),
             dma((2, others)),
@@ -1522,13 +1532,14 @@
             dma((2, split)),
             dma((2, others)),
             dma((2, split)),
+            dma((2, split + 1)),
         ],
         compiler_params=pltpu.CompilerParams(
             collective_id=4, has_side_effects=True, vmem_limit_bytes=63 << 20
         ),
         cost_estimate=pl.CostEstimate(flops=1000, bytes_accessed=1000, transcendentals=0),
     )(
-        second, routed, hidden_full, last_part, router_lanes, resid, grad_out, gains, lengths, gate_full, normed,
+        second, routed, hidden_full, last_part, router_lanes, resid, grad_out, gains, gate_full, normed,
         spread_out, step, z, y, gated, rows,
     )
 
@@ -1537,15 +1548,15 @@
     dt_rank, states, tap_count,
     dy_hbm, gz_hbm, later_hbm, mine_ref, gate_mine_hbm, first_hbm, gate_hbm, normed_hbm, input_ref,
     coef_ref, step_hbm, start_hbm, rows_ref, d_resid_ref, tokens_ref, gains_ref, small_ref,
-    lengths_ref, in_hbm, out_hbm,
-    grad_tokens_ref, total_ref, late_ref, gate_own_ref, first_own_ref,
+    lengths_ref, in_hbm, out_hbm, drive_hbm,
+    grad_tokens_ref, total_ref, late_ref, second_own_ref, out_own_ref, first_own_ref,
     dy_ref, gz_ref, later_ref, gate_mine_ref, first_ref, gate_ref, normed_ref, step_ref, start_ref,
-    in_ref, out_ref, load_sems,
-    hist_ref, acc_in_ref, acc_out_ref, mixed_ref, conv_ref, q_ref, r_ref, reset_ref,
+    in_ref, out_ref, drive_ref, load_sems,
+    hist_ref, acc_in_ref, acc_out_ref, conv_ref, q_ref, r_ref,
     gdt_ref, gin_ref, halo_ref, part_ref, arrive_ref, fold_ref, coef_send_ref,
     coef_arrive_ref, gcoef_ref, misc_ref, select_ref, payload_ref, half_ref, mine_first_ref,
-    late_arrive_ref, gate_arrive_ref, first_arrive_ref, core_slots, plane_slots, line_slots,
-    late_sems, gate_sems, first_sems, half_sems, halo_sems, coef_sems, sum_sems, core_sems,
+    late_arrive_ref, second_arrive_ref, out_arrive_ref, first_arrive_ref, core_slots, plane_slots, line_slots,
+    late_sems, second_sems, out_sems, first_sems, half_sems, halo_sems, coef_sems, sum_sems, core_sems,
     plane_sems, line_sems,
 ):
     core, high, low = kernel_place()
@@ -1561,6 +1572,7 @@
                 (start_hbm, start_ref),
                 (gate_mine_hbm, gate_mine_ref),
                 (in_hbm, in_ref),
+                (drive_hbm, drive_ref),
                 (dy_hbm, dy_ref),
                 (later_hbm, later_ref),
                 (out_hbm, out_ref),
@@ -1583,12 +1595,15 @@
         place = high * row_count + at + lax.broadcasted_iota(jnp.int32, (rows, lanes), 0)
         return jnp.where(place < first_len, place, place - first_len)
 
-    fill_offsets(reset_ref, lengths_ref, row_count)
-    pl.semaphore_wait(pltpu.get_barrier_semaphore(), greeted)
     late = LineScatter(lambda to: mine_ref.at[to], late_arrive_ref, late_sems)
-    gate = LineScatter(lambda to: gate_mine_ref.at[to], gate_arrive_ref, gate_sems)
-    late.start()
-
+    gate_parts = [
+        LineScatter(
+            lambda to: gate_mine_ref.at[to, pl.ds(0, channel_rows)], second_arrive_ref, second_sems
+        ),
+        LineScatter(
+            lambda to: gate_mine_ref.at[to, pl.ds(channel_rows, channel_rows)], out_arrive_ref, out_sems
+        ),
+    ]
     def convolve(at):
         offset = offsets(at, 32)
         for j in range(tiles):
@@ -1599,26 +1614,29 @@
                 term = rows_ref[j, k : k + 1, :] * span[shift : shift + 32]
                 conv_sum = conv_sum + jnp.where(offset >= tap_count - 1 - k, term, 0.0)
             conv_ref[j, pl.ds(at, 32), :] = conv_sum
-            mixed = low_bits(conv_sum * sigmoid_of(conv_sum)).astype(jnp.float32)
-            mixed_ref[j, pl.ds(at, 32), :] = mixed
 
     row_loop(row_count, 32, convolve)
-    late.pass_on()
-    for copy in loads[:7]:
+    pl.semaphore_wait(pltpu.get_barrier_semaphore(), greeted)
+    late.start()
+    for copy in loads[:8]:
         copy.wait()
-    gate.start()
     acc_in_ref[...] = jnp.zeros_like(acc_in_ref)
     acc_out_ref[...] = jnp.zeros_like(acc_out_ref)
     misc_ref[...] = jnp.zeros_like(misc_ref)
 
     def back_of(j, _):
+        @pl.when(j == 2)
+        def _():
+            late.pass_on()
+            for part in gate_parts:
+                part.start()
+
         values = -jnp.exp(rows_ref[j, alog_row : alog_row + states, :]) * log2e
         rates = [jnp.broadcast_to(values[n : n + 1, :], (subs, lanes)) for n in range(states)]
 
         def forward(s, held):
-            step = step_ref[j, pl.ds(s, subs, stride=steps), :]
-            drive = step * mixed_ref[j, pl.ds(s, subs, stride=steps), :]
-            step = step + reset_ref[pl.ds(s, subs, stride=steps), :]
+            step = step_ref[j, step_rows(s), :]
+            drive = drive_ref[j, step_rows(s), :]
             now_all = []
             for n in range(states):
                 now = jnp.exp2(step * rates[n]) * held[n] + in_ref[s, n] * drive
@@ -1635,11 +1653,10 @@
         def backward(turn, carry):
             s = steps - 1 - turn
             later, sums = carry
-            delta = step_ref[j, pl.ds(s, subs, stride=steps), :]
-            drive = delta * mixed_ref[j, pl.ds(s, subs, stride=steps), :]
-            step = delta + reset_ref[pl.ds(s, subs, stride=steps), :]
+            step = step_ref[j, step_rows(s), :]
+            drive = drive_ref[j, step_rows(s), :]
             dy = dy_ref[j, pl.ds(s, subs, stride=steps), :]
-            rows = pl.ds(pl.multiple_of(s * subs, subs), subs)
+            rows = step_rows(s)
             q = jnp.zeros((subs, lanes), jnp.float32)
             r = jnp.zeros((subs, lanes), jnp.float32)
             later_next, sums_next = [], []
@@ -1648,7 +1665,7 @@
                 d_state = out_ref[s, n] * dy + later[n]
                 back = jnp.exp2(step * rates[n]) * d_state
                 scaled = back * hist_ref[s, n]
-                sums_next.append(sums[n] + scaled * delta)
+                sums_next.append(sums[n] + scaled * step)
                 q = q + scaled * rates[n]
                 r = r + d_state * in_ref[s, n]
                 acc_in_ref[rows, cols] += d_state * drive
@@ -1668,7 +1685,7 @@
 
     lax.fori_loop(0, tiles, back_of, 0)
 
-    for copy in loads[7:]:
+    for copy in loads[8:]:
         copy.wait()
 
     source = lax.broadcasted_iota(jnp.int32, select_ref.shape, 0) // lanes
@@ -1693,14 +1710,21 @@
     fold(acc_out_ref, dt_rank + states, False)
     dt_full = first_ref[:, :, model_width + lanes : model_width + 2 * lanes].reshape(width, lanes)
 
+    def mixed_of(j, rows):
+        conv = conv_ref[j, rows, :]
+        return low_bits(conv * sigmoid_of(conv)).astype(jnp.float32)
+
     def step_grads(at):
         rows = pl.ds(at, 128)
         pre = matmul_nt(low_bits(coef_ref[rows, :]), dt_full)
         for j in range(tiles):
             cols = slice(j * lanes, (j + 1) * lanes)
-            mixed = mixed_ref[j, rows, :]
-            d_step = q_ref[j, rows, :] + r_ref[j, rows, :] * mixed
-            d_dt = d_step * sigmoid_of(pre[:, cols] + rows_ref[j, bias_row : bias_row + 1, :])
+            mixed = mixed_of(j, rows)
+            in_sum = r_ref[j, rows, :]
+            d_step = q_ref[j, rows, :] + in_sum * mixed
+            biased = pre[:, cols] + rows_ref[j, bias_row : bias_row + 1, :]
+            r_ref[j, rows, :] = in_sum * softplus_of(biased)
+            d_dt = d_step * sigmoid_of(biased)
             gdt_ref[rows, cols] = low_bits(d_dt)
             misc_ref[j, bias_row : bias_row + 1, :] += jnp.sum(d_dt, 0, keepdims=True)
             misc_ref[j, skip_row : skip_row + 1, :] += jnp.sum(
@@ -1711,7 +1735,6 @@
         coef_send_ref[rows, :] = low_bits(part)
 
     row_loop(row_count, 128, step_grads)
-    gate.pass_on()
     coef_copies = plane_copies(lambda to, k: coef_send_ref, coef_arrive_ref, coef_sems, False)
     for copy in coef_copies:
         copy.start()
@@ -1735,7 +1758,7 @@
         for j in range(tiles):
             cols = slice(j * lanes, (j + 1) * lanes)
             d_mixed = rows_ref[j, skip_row : skip_row + 1, :] * dy_ref[j, rows, :]
-            d_mixed = d_mixed + r_ref[j, rows, :] * step_ref[j, rows, :] + from_coef[:, cols]
+            d_mixed = d_mixed + r_ref[j, rows, :] + from_coef[:, cols]
             conv = conv_ref[j, rows, :]
             sig = sigmoid_of(conv)
             q_ref[j, rows, :] = d_mixed * (sig * (1.0 + conv * (1.0 - sig)))
@@ -1747,6 +1770,9 @@
             q_ref.at[:, pl.ds(0, subs)], halo_ref, halo_sems.at[0], halo_sems.at[1],
             core, lax.rem(high + split - 1, split), low,
         )
+
+    for part in gate_parts:
+        part.pass_on()
 
     @pl.when(high > 0)
     def _():
@@ -1799,7 +1825,7 @@
     for j in range(tiles):
         rows = slice(j * lanes, (j + 1) * lanes)
         payload_ref[rows, model_width : model_width + lanes] = low_bits(
-            matmul_tn(low_bits(mixed_ref[j]), gcoef_ref[...])
+            matmul_tn(low_bits(mixed_of(j, slice(0, row_count))), gcoef_ref[...])
         )
         payload_ref[rows, model_width + 2 * lanes :] = low_bits(misc_ref[j].T)
     half_width = width // 2
@@ -1861,7 +1887,8 @@
     for copy in plane:
         copy.start()
     first.pass_on()
-    gate.finish(gate_own_ref)
+    gate_parts[0].finish(second_own_ref)
+    gate_parts[1].finish(out_own_ref)
     d_normed = grad_tokens_ref[...]
     for k in range(1, split):
         sum_copies[k - 1].wait()
@@ -1883,7 +1910,8 @@
 
 def run_back(
     dy, gz, later, mine, gate_mine, first_full, gate_full, normed, input_all, coef, step, start, rows,
-    d_resid, tokens, gains, small, lengths, spread_in, spread_out, dt_rank, states, tap_count,
+    d_resid, tokens, gains, small, lengths, spread_in, spread_out, drive, dt_rank, states,
+    tap_count,
 ):
     _, own_rows, model_width = normed.shape
     row_count = own_rows * split
@@ -1893,21 +1921,21 @@
     channel_rows = width // (2 * split)
     others = split - 1
     late_rows = mine.shape[1]
-    gate_rows = gate_mine.shape[1]
     first_columns = first_full.shape[2]
     vmem = pl.BlockSpec(memory_space=pltpu.VMEM)
     specs = [pl.BlockSpec(memory_space=pl.ANY) if i in (0, 1, 2, 4, 5, 6, 7, 10, 11) else vmem for i in range(17)]
     loaded = [dy, gz, later, gate_mine, first_full, gate_full, normed, step, start]
-    loaded += [spread_in, spread_out]
+    loaded += [spread_in, spread_out, drive]
     specs.append(pl.BlockSpec(memory_space=pltpu.SMEM))
-    specs += [pl.BlockSpec(memory_space=pl.ANY)] * 2
+    specs += [pl.BlockSpec(memory_space=pl.ANY)] * 3
     f32, bf16 = jnp.float32, jnp.bfloat16
     dma = pltpu.SemaphoreType.DMA
     outs = [
         (own_rows, model_width),
         (8, model_width),
         (late_rows, model_width),
-        (gate_rows, model_width),
+        (channel_rows, model_width),
+        (channel_rows, model_width),
         (channel_rows, first_columns),
     ]
     tiled = pltpu.VMEM((tiles, row_count, lanes), f32)
@@ -1924,10 +1952,8 @@
             summed,
             summed,
             tiled,
-            tiled,
             pltpu.VMEM((tiles, row_count + subs, lanes), f32),
             tiled,
-            pltpu.VMEM((row_count, lanes), f32),
             pltpu.VMEM((row_count, width), bf16),
             pltpu.VMEM((row_count, width), bf16),
             pltpu.VMEM((tiles, subs, lanes), f32),
@@ -1943,13 +1969,14 @@
             pltpu.VMEM((width // 2, first_columns), bf16),
             pltpu.VMEM((width // 2, first_columns), bf16),
             pltpu.VMEM((split + 1, late_rows, model_width), bf16),
-            pltpu.VMEM((split + 1, gate_rows, model_width), bf16),
+            pltpu.VMEM((split + 1, channel_rows, model_width), bf16),
+            pltpu.VMEM((split + 1, channel_rows, model_width), bf16),
             pltpu.VMEM((split + 1, channel_rows, first_columns), bf16),
             pltpu.VMEM((2, 8, model_width), f32),
             pltpu.VMEM((split, 8, model_width), f32),
             pltpu.VMEM((split, 8, model_width), f32),
         ]
-        + [dma((2, split + 1))] * 3
+        + [dma((2, split + 1))] * 4
         + [dma((2,)), dma((2,)), dma((2, others)), dma((2, others)), dma((2,))]
         + [dma((2, others)), dma((2, others))],
         compiler_params=pltpu.CompilerParams(
@@ -1958,26 +1985,25 @@
         cost_estimate=pl.CostEstimate(flops=1000, bytes_accessed=1000, transcendentals=0),
     )(
         dy, gz, later, mine, gate_mine, first_full, gate_full, normed, input_all, coef, step, start,
-        rows, d_resid, tokens, gains, small, lengths, spread_in, spread_out,
+        rows, d_resid, tokens, gains, small, lengths, spread_in, spread_out, drive,
     )
 
 
 def results_kernel(
     tap_count, states, coef_count, dt_rank, expert_count,
-    mixed_ref, tokens_ref, total_ref, early_ref, late_ref, gate_ref, first_ref,
+    mixed_ref, tokens_ref, total_ref, early_ref, mid_ref, late_ref, second_ref, out_ref, first_ref,
     mixed_out, tokens_out, gains_out, router_out, in_out, conv_out, x_out, dt_out, bias_out, alog_out,
     skip_out, out_out, up_out, down_out,
 ):
     channels, model_width = out_out.shape
     hidden = up_out.shape[1]
-    channel_rows = first_ref.shape[0]
     mixed_out[...] = mixed_ref[...]
     tokens_out[...] = tokens_ref[...]
     gains_out[...] = total_ref[:2]
     router_out[...] = total_ref[2 : 2 + expert_count]
     in_out[0] = first_ref[:channels, :model_width]
-    in_out[1] = gate_ref[:channels]
-    out_out[...] = gate_ref[channel_rows : channel_rows + channels]
+    in_out[1] = second_ref[:channels]
+    out_out[...] = out_ref[:channels]
     at = model_width
     x_out[...] = first_ref[:channels, at : at + lanes][:, :coef_count]
     dt_out[...] = first_ref[:channels, at + lanes : at + 2 * lanes][:, :dt_rank]
@@ -1987,10 +2013,8 @@
     alog_out[...] = rows[alog_row : alog_row + states, :channels]
     bias_out[...] = rows[bias_row : bias_row + 1, :channels]
     skip_out[...] = rows[skip_row : skip_row + 1, :channels]
-    for e in range(expert_count):
-        source, first = (early_ref, 0) if e == 0 else (late_ref, 2 * (e - 1) * hidden)
-        up_out[e] = source[first : first + hidden]
-        down_out[e] = source[first + hidden : first + 2 * hidden]
+    up_out[0], down_out[0] = early_ref[:hidden], early_ref[hidden:]
+    up_out[1], down_out[1] = mid_ref[...], late_ref[...]
 
 
 def run_results(parts, channels, tap_count, states, coef_count, dt_rank, expert_count, hidden):
@@ -2476,25 +2500,25 @@
     coef_count = dt_rank + 2 * states
     (
         first_full, gate_full, hidden_full, normed, routed, input_all, coef, step, z, y, gated, start,
-        resid, second, rows, spread_in, spread_out,
+        resid, second, rows, spread_in, spread_out, drive,
     ) = run_mixer(
         tokens, norm_gains, lengths, in_weight, conv_weight.T, x_weight, dt_weight, dt_bias[None], a_log.T,
         skip_gain[None], out_weight, expert_in, expert_out, grad_out, routes[None],
     )
-    mixed_out, d_resid, small_sums, dy, gz, later, mine, early, gate_mine = run_turn(
-        second, routed, hidden_full, expert_out, router.T, resid, grad_out, norm_gains, lengths,
+    mixed_out, d_resid, small_sums, dy, gz, later, mine, early, gate_mine, mid = run_turn(
+        second, routed, hidden_full, expert_out, router.T, resid, grad_out, norm_gains,
         gate_full, normed, spread_out, step, z, y, gated, rows, states, expert_count,
     )
-    grad_tokens, sums, late, gate_own, first_own = run_back(
+    grad_tokens, sums, late, second_own, out_own, first_own = run_back(
         dy, gz, later, mine, gate_mine, first_full, gate_full, normed, input_all, coef, step, start,
-        rows, d_resid, tokens, norm_gains, small_sums, lengths, spread_in, spread_out, dt_rank, states,
-        tap_count,
+        rows, d_resid, tokens, norm_gains, small_sums, lengths, spread_in, spread_out, drive, dt_rank,
+        states, tap_count,
     )
     (
         mixed_out, grad_tokens, grad_gains, grad_router, grad_in, grad_conv, grad_x, grad_dt, grad_bias,
         grad_alog, grad_skip, grad_out_w, grad_up, grad_down,
     ) = run_results(
-        (mixed_out, grad_tokens, sums, early, late, gate_own, first_own),
+        (mixed_out, grad_tokens, sums, early, mid, late, second_own, out_own, first_own),
         channels, tap_count, states, coef_count, dt_rank, expert_count, hidden,
     )
     return (

time: 286 us -> 283 us (0.990)
  Pallas kernels: 286 us -> 281 us
    pallas_call x1, Pallas kernels: 86.9 us -> 77.9 us  [run_back(): pl.pallas_call(functools.partial(back_kernel, dt_rank, states, tap_count)...]
    pallas_call x1, Pallas kernels: 78.5 us -> 82.8 us  [run_turn(): pl.pallas_call(functools.partial(turn_kernel, states, expert_count), in_s...]
where the time goes in v5:
time: 283 us; the launch traced here: 281 us
  Pallas kernels  281 us (99%)
    pallas_call x1, Pallas kernels, run_mixer(): pl.pallas_call(functools.partial(mixer_kernel, dt_rank, states, tap_count...  116 us
    pallas_call x1, Pallas kernels, run_turn(): pl.pallas_call(functools.partial(turn_kernel, states, expert_count), in_s...  82.8 us
    pallas_call x1, Pallas kernels, run_back(): pl.pallas_call(functools.partial(back_kernel, dt_rank, states, tap_count)...  77.9 us

profile of v5, /device:TPU:0, one launch (start us, length us, event | category | flops | bytes accessed | tf_op | source)
XLA Modules:
  0.0 281.4 jit_solution(947448757249434659)
XLA Ops:
  0.6 116.0 %shard_map.263 = (bf16[8,80,1536]{2,1,0:T(8,128)(2,1)}, bf16[8,160,1152]{2,1,0:T(8,128)(2,1)}, bf16[8,288,1152]{2,1,0:T(8,128)(2,1)}, bf16[4,128,1152]{2,1,0:T(8...) custom-call(bf16[128,1152]{1,0:T(8,128)(2,1)} %tokens_ref.3, ...), custom_call_target="tpu_custom_call" | custom-call | flops 1000 | bytes 1000 | tf_op jit(solution)/shard_map/pallas_call | solution.py:960
  116.6 82.8 %shard_map.264 = (bf16[128,1152]{1,0:T(8,128)(2,1)}, f32[128,1152]{1,0:T(8,128)}, f32[8,1152]{1,0:T(8,128)}, f32[5,512,128]{2,1,0:T(8,128)}, bf16[512,640]{1,0:T...) custom-call(bf16[4,128,1152]{2,1,0:T(8,128)(2,1)} %get-tuple-element, ...), custom_call_target="tpu_custom_call" | custom-call | flops 1000 | bytes 1000 | tf_op jit(solution)/shard_map/pallas_call | solution.py:1497
  199.4 77.9 %shard_map.265 = (f32[128,1152]{1,0:T(8,128)}, f32[8,1152]{1,0:T(8,128)}, f32[96,1152]{1,0:T(8,128)}, f32[80,1152]{1,0:T(8,128)}, f32[80,1152]{1,0:T(8,128)}, /*index=5*/f32[80,1536]{1,0:T(8,128)}) custom-call(f32[5,512,128]{2,1,0:T(8,128)} %get-tuple-element.75.dy_hbm, bf16[512,640]{1,0:T(8,128)(2,1)} %get-tuple-element.76.gz_hbm, ...), custom_call_target="tpu_custom_call" | custom-call | flops 1000 | bytes 1000 | tf_op jit(solution)/shard_map/pallas_call | solution.py:1943
  277.4 4.0 %shard_map.266 = (bf16[128,1152]{1,0:T(8,128)(2,1)}, f32[128,1152]{1,0:T(8,128)}, f32[2,1152]{1,0:T(2,128)}, f32[2,1152]{1,0:T(2,128)}, f32[2,72,1152]{2,1,0:T(8...) custom-call(bf16[128,1152]{1,0:T(8,128)(2,1)} %get-tuple-element.74., ...), custom_call_target="tpu_custom_call" | custom-call | flops 1000 | bytes 1000 | tf_op jit(solution)/shard_map/pallas_call | solution.py:2039

commit v6 on v5

--- a/solution.py
+++ b/solution.py
@@ -538,9 +538,10 @@
     return copies
 
 
-alog_row = 8
-bias_row = 4
-skip_row = 5
+tap_row = lanes - 24
+bias_row = lanes - 20
+skip_row = lanes - 19
+alog_row = lanes - 16
 early_hidden = 64
 
 
@@ -612,16 +613,15 @@
         return matmul(value, jnp.where(at == to, 1.0, 0.0).astype(jnp.bfloat16))
 
     first_ref[high, :, :model_width] = filled(in_weight_ref[0])
-    first_ref[high, :, model_width : model_width + lanes] = filled(widened(x_weight_ref[...], 0))
-    first_ref[high, :, model_width + lanes : model_width + 2 * lanes] = filled(
-        widened(dt_weight_ref[...], 0)
-    )
+    first_ref[high, :, model_width + lanes :] = filled(widened(dt_weight_ref[...], 0))
     rows_ref[0] = jnp.zeros((lanes, lanes), jnp.float32)
     for row, ref in (
-        (0, conv_weight_ref), (bias_row, dt_bias_ref), (skip_row, skip_ref), (alog_row, a_log_ref)
+        (tap_row, conv_weight_ref), (bias_row, dt_bias_ref), (skip_row, skip_ref), (alog_row, a_log_ref)
     ):
         rows_ref[0, row : row + ref.shape[0], :channels] = ref[...].astype(jnp.float32)
-    first_ref[high, :, model_width + 2 * lanes :] = filled(rows_ref[0].T[:channels])
+    first_ref[high, :, model_width : model_width + lanes] = filled(
+        widened(x_weight_ref[...], 0) + rows_ref[0].T[:channels]
+    )
     pl.semaphore_wait(barrier, greeted)
 
     @pl.when((low == split - 1) & (high < split - 1))
@@ -736,7 +736,8 @@
     store(first_ref, first_out)
     store(normed_ref, normed_out)
     store(input_ref, input_out)
-    small = first_ref[:, :, model_width + 2 * lanes :].reshape(width, lanes).astype(jnp.float32)
+    small = first_ref[:, :, model_width : model_width + lanes].reshape(width, lanes)
+    small = small.astype(jnp.float32)
     for j in range(tiles):
         rows_ref[j] = small[j * lanes : (j + 1) * lanes].T
 
@@ -749,7 +750,7 @@
             conv_sum = jnp.zeros((32, lanes), jnp.float32)
             for k in range(tap_count):
                 shift = edge - (tap_count - 1) + k
-                term = rows_ref[j, k : k + 1, :] * span[shift : shift + 32]
+                term = rows_ref[j, tap_row + k : tap_row + k + 1, :] * span[shift : shift + 32]
                 conv_sum = conv_sum + jnp.where(offset >= tap_count - 1 - k, term, 0.0)
             mixed_ref[pl.ds(at, 32), j * lanes : (j + 1) * lanes] = low_bits(
                 conv_sum * sigmoid_of(conv_sum)
@@ -938,7 +939,7 @@
     f32, bf16 = jnp.float32, jnp.bfloat16
     tiled = (tiles, row_count, lanes)
     hidden_part = ((2 * expert_count - 1) * hidden, model_width)
-    first = ((blocks, channel_rows, model_width + 3 * lanes), bf16)
+    first = ((blocks, channel_rows, model_width + 2 * lanes), bf16)
     gate = ((blocks, 2 * channel_rows, model_width), bf16)
     normed = ((split, own_rows, model_width), bf16)
     edge = ((16, model_width), bf16)
@@ -1611,7 +1612,7 @@
             conv_sum = jnp.zeros((32, lanes), jnp.float32)
             for k in range(tap_count):
                 shift = edge - (tap_count - 1) + k
-                term = rows_ref[j, k : k + 1, :] * span[shift : shift + 32]
+                term = rows_ref[j, tap_row + k : tap_row + k + 1, :] * span[shift : shift + 32]
                 conv_sum = conv_sum + jnp.where(offset >= tap_count - 1 - k, term, 0.0)
             conv_ref[j, pl.ds(at, 32), :] = conv_sum
 
@@ -1787,7 +1788,7 @@
             for k in range(tap_count):
                 shift = edge - (tap_count - 1) + k
                 term = jnp.where(offset >= tap_count - 1 - k, d_conv * span[shift : shift + 32], 0.0)
-                misc_ref[j, k : k + 1, :] += jnp.sum(term, 0, keepdims=True)
+                misc_ref[j, tap_row + k : tap_row + k + 1, :] += jnp.sum(term, 0, keepdims=True)
 
     row_loop(row_count, 32, tap_grads)
 
@@ -1808,7 +1809,7 @@
             d_input = jnp.zeros((32, lanes), jnp.float32)
             for m in range(tap_count):
                 k = tap_count - 1 - m
-                term = rows_ref[j, k : k + 1, :] * span[m : m + 32]
+                term = rows_ref[j, tap_row + k : tap_row + k + 1, :] * span[m : m + 32]
                 d_input = d_input + jnp.where(masks[m], term, 0.0)
             gin_ref[pl.ds(at, 32), cols] = low_bits(d_input)
 
@@ -1824,10 +1825,8 @@
     normed = normed_ref[...].reshape(row_count, model_width)
     for j in range(tiles):
         rows = slice(j * lanes, (j + 1) * lanes)
-        payload_ref[rows, model_width : model_width + lanes] = low_bits(
-            matmul_tn(low_bits(mixed_of(j, slice(0, row_count))), gcoef_ref[...])
-        )
-        payload_ref[rows, model_width + 2 * lanes :] = low_bits(misc_ref[j].T)
+        grad_x = matmul_tn(low_bits(mixed_of(j, slice(0, row_count))), gcoef_ref[...])
+        payload_ref[rows, model_width : model_width + lanes] = low_bits(grad_x + misc_ref[j].T)
     half_width = width // 2
     half = remote(
         payload_ref.at[pl.ds(half_width, half_width)], half_ref, half_sems.at[0], half_sems.at[1],
@@ -2007,9 +2006,9 @@
     at = model_width
     x_out[...] = first_ref[:channels, at : at + lanes][:, :coef_count]
     dt_out[...] = first_ref[:channels, at + lanes : at + 2 * lanes][:, :dt_rank]
-    misc = first_ref[:, at + 2 * lanes :]
+    misc = first_ref[:, at : at + lanes]
     rows = misc.T
-    conv_out[...] = rows[:tap_count, :channels]
+    conv_out[...] = rows[tap_row : tap_row + tap_count, :channels]
     alog_out[...] = rows[alog_row : alog_row + states, :channels]
     bias_out[...] = rows[bias_row : bias_row + 1, :channels]
     skip_out[...] = rows[skip_row : skip_row + 1, :channels]

time: 283 us -> 280 us (0.989)
  Pallas kernels: 281 us -> 278 us
where the time goes in v6:
time: 280 us; the launch traced here: 279 us
  Pallas kernels  278 us (99%)
    pallas_call x1, Pallas kernels, run_mixer(): pl.pallas_call(functools.partial(mixer_kernel, dt_rank, states, tap_count...  115 us
    pallas_call x1, Pallas kernels, run_turn(): pl.pallas_call(functools.partial(turn_kernel, states, expert_count), in_s...  82.7 us
    pallas_call x1, Pallas kernels, run_back(): pl.pallas_call(functools.partial(back_kernel, dt_rank, states, tap_count)...  76.6 us

profile of v6, /device:TPU:0, one launch (start us, length us, event | category | flops | bytes accessed | tf_op | source)
XLA Modules:
  0.0 278.6 jit_solution(3610238554717499866)
XLA Ops:
  0.6 114.7 %shard_map.263 = (bf16[8,80,1408]{2,1,0:T(8,128)(2,1)}, bf16[8,160,1152]{2,1,0:T(8,128)(2,1)}, bf16[8,288,1152]{2,1,0:T(8,128)(2,1)}, bf16[4,128,1152]{2,1,0:T(8...) custom-call(bf16[128,1152]{1,0:T(8,128)(2,1)} %tokens_ref.3, ...), custom_call_target="tpu_custom_call" | custom-call | flops 1000 | bytes 1000 | tf_op jit(solution)/shard_map/pallas_call | solution.py:961
  115.3 82.7 %shard_map.264 = (bf16[128,1152]{1,0:T(8,128)(2,1)}, f32[128,1152]{1,0:T(8,128)}, f32[8,1152]{1,0:T(8,128)}, f32[5,512,128]{2,1,0:T(8,128)}, bf16[512,640]{1,0:T...) custom-call(bf16[4,128,1152]{2,1,0:T(8,128)(2,1)} %get-tuple-element, ...), custom_call_target="tpu_custom_call" | custom-call | flops 1000 | bytes 1000 | tf_op jit(solution)/shard_map/pallas_call | solution.py:1498
  198.0 76.6 %shard_map.265 = (f32[128,1152]{1,0:T(8,128)}, f32[8,1152]{1,0:T(8,128)}, f32[96,1152]{1,0:T(8,128)}, f32[80,1152]{1,0:T(8,128)}, f32[80,1152]{1,0:T(8,128)}, /*index=5*/f32[80,1408]{1,0:T(8,128)}) custom-call(f32[5,512,128]{2,1,0:T(8,128)} %get-tuple-element.75.dy_hbm, bf16[512,640]{1,0:T(8,128)(2,1)} %get-tuple-element.76.gz_hbm, ...), custom_call_target="tpu_custom_call" | custom-call | flops 1000 | bytes 1000 | tf_op jit(solution)/shard_map/pallas_call | solution.py:1942
  274.6 4.0 %shard_map.266 = (bf16[128,1152]{1,0:T(8,128)(2,1)}, f32[128,1152]{1,0:T(8,128)}, f32[2,1152]{1,0:T(2,128)}, f32[2,1152]{1,0:T(2,128)}, f32[2,72,1152]{2,1,0:T(8...) custom-call(bf16[128,1152]{1,0:T(8,128)(2,1)} %get-tuple-element.74., ...), custom_call_target="tpu_custom_call" | custom-call | flops 1000 | bytes 1000 | tf_op jit(solution)/shard_map/pallas_call | solution.py:2038
